TPU v7x, 128 devices: a whole 4x4x4 slice. The times are simulated.
128 devices in a mesh: grp: 4 (over y_hi, core), blk: 32 (over y_lo, z, x).
Axes of the slice: x: 4, y: 4 (y_hi: 2, y_lo: 2; y = y_hi * 2 + y_lo), z: 4, core: 2. Of those that a mesh axis runs over, the one named last changes fastest.
Arguments:
- embeddings: bfloat16 [49152, 1024], P(('grp', 'blk')), may hold values from -6 to 6
- cluster_id: int32 [49152], P(('grp', 'blk')), may hold values from 0 to 7, as said below
- source_id: int32 [49152], P(('grp', 'blk')), may hold values from 0 to 65535
Outputs:
- max_similarity: float32 [49152], P(('grp', 'blk'))
Inputs may be any that keep to these rules, and one draw needn't show every extreme that they name: `cluster_id`: within each group's 12288 rows the ids start at 0 at the group's first row, rise by 0 or 1 from one row to the next, and end at 7.
All inputs are finite; a program needn't handle non-finite values.
Results may differ from a plain program's by a relative error of at most 0.0013.
Values may be sent and summed in bfloat16 or wider, within the bound.
No kernel may reach another device: no remote copies, remote signals or barrier semaphores. Data moves between devices by JAX's collectives and lax.ppermute only.
A program may use at most 64 MiB of HBM per device.

v0:
```python
import functools

import jax
import jax.numpy as jnp
from jax import lax
from jax.experimental import pallas as pl
from jax.experimental.pallas import tpu as pltpu
from jax.sharding import PartitionSpec as P

TORUS = (2, 4, 4)
OFFSETS = (
    (0, 0, 0),
    (0, 0, 1),
    (0, 1, 3),
    (0, 3, 0),
    (1, 0, 0),
    (0, 2, 3),
    (1, 1, 2),
    (0, 0, 2),
    (0, 2, 0),
)
FIRST = ((3, (0, 3, 0)), (1, (0, 0, 1)), (2, (0, 1, 3)), (4, (1, 0, 0)))
SECOND = ((8, 3, (0, 3, 0)), (7, 1, (0, 0, 1)), (6, 2, (1, 0, 3)), (5, 2, (0, 1, 0)))
ROWS = 384
TAIL = 16
BLOCK = ROWS + TAIL
WIDTH = 1024
STEPS = {
    "early": (
        (0, 1, 2, 3, 4),
        (
            (0, 0, 4, (0, 1, 2, 3, 4)),
            (1, 2, 4, (1, 2, 3, 4)),
            (2, 3, 4, (2, 3, 4)),
            (3, 4, 4, (3, 4)),
        ),
        (0, 1, 2, 3, 4),
    ),
    "middle": (
        (1, 4, 6, 5, 3, 0),
        ((5, 0, 2, (5, 4, 6)), (6, 4, 5, (6, 0))),
        (0, 4, 5, 6),
    ),
    "late": (
        (7, 8, 0, 4),
        ((0, 0, 1, (0,)), (4, 0, 1, (4,))),
        (0, 4),
    ),
}


def difference(a, b):
    return tuple((p - q) % n for p, q, n in zip(a, b, TORUS))


def check():
    met = []
    for order, strips, _ in STEPS.values():
        for a, first, last, sides in strips:
            for b in order[first : last + 1]:
                met += [difference(OFFSETS[b], OFFSETS[a])] * (a in sides)
                met += [difference(OFFSETS[a], OFFSETS[b])] * (b in sides and b != a)
    assert len(set(met)) == 32
    for block, by in FIRST:
        assert OFFSETS[block] == by
    for block, parent, by in SECOND:
        assert difference(OFFSETS[block], OFFSETS[parent]) == by


check()


def flat(y, z, x):
    return ((y % TORUS[0]) * TORUS[1] + z % TORUS[1]) * TORUS[2] + x % TORUS[2]


def receive(array, by, back=False):
    links = []
    for y in range(TORUS[0]):
        for z in range(TORUS[1]):
            for x in range(TORUS[2]):
                far, near = flat(y + by[0], z + by[1], x + by[2]), flat(y, z, x)
                links.append((near, far) if back else (far, near))
    return lax.ppermute(array, "blk", links)


def prepare_kernel(embeddings, cluster, source, out):
    @pl.loop(0, ROWS // 64)
    def _(step):
        rows = pl.ds(pl.multiple_of(step * 64, 64), 64)
        widened = embeddings[rows, :].astype(jnp.float32)
        factor = lax.rsqrt(jnp.mean(widened * widened, axis=1, keepdims=True) + 1e-06) / 32.0
        out[rows, :] = (widened * factor).astype(jnp.bfloat16)

    line = lax.broadcasted_iota(jnp.int32, (TAIL, ROWS), 0)
    ids = source[...].reshape(1, ROWS)
    clusters = cluster[...].reshape(1, ROWS)
    tail = jnp.where(line == 0, clusters, jnp.where(line == 1, ids // 256, jnp.where(line == 2, ids % 256, 0)))
    out[ROWS:, :ROWS] = tail.astype(jnp.float32).astype(jnp.bfloat16)
    out[ROWS:, ROWS:] = jnp.zeros((TAIL, WIDTH - ROWS), jnp.bfloat16)


def prepare(embeddings, cluster_id, source_id):
    return pl.pallas_call(
        prepare_kernel,
        out_shape=jax.ShapeDtypeStruct((BLOCK, WIDTH), jnp.bfloat16),
        in_specs=[pl.BlockSpec(memory_space=pltpu.VMEM)] * 3,
        out_specs=pl.BlockSpec(memory_space=pltpu.VMEM),
        compiler_params=pltpu.CompilerParams(vmem_limit_bytes=8 << 20),
        name="prepare",
    )(embeddings, cluster_id, source_id)


def score_kernel(step, given, *refs):
    order, strips, results = STEPS[step]
    n = len(order)
    place = {b: i for i, b in enumerate(order)}
    blocks, refs = refs[:n], refs[n:]
    earlier, refs = dict(zip(given, refs)), refs[len(given) :]
    outs, refs = dict(zip(results, refs)), refs[len(results) :]
    held, ids, sems = refs
    copies = []
    for i, block in enumerate(blocks):
        copies.append(pltpu.make_async_copy(block.at[:ROWS], held.at[pl.ds(i * ROWS, ROWS)], sems.at[0, i]))
        copies.append(pltpu.make_async_copy(block.at[ROWS:], ids.at[i], sems.at[1, i]))
    for copy in copies:
        copy.start()
    for copy in copies:
        copy.wait()

    def word(b):
        parts = ids[place[b], :, :ROWS].astype(jnp.float32)
        return parts[0:1] * 65536.0 + parts[1:2] * 256.0 + parts[2:3]

    def words(b):
        return word(b).astype(jnp.int32)

    def word_columns(b):
        return jnp.broadcast_to(word(b), (128, ROWS)).T.astype(jnp.int32)

    over_lanes, over_rows = {}, {}

    def update(table, b, value):
        table[b] = jnp.maximum(table[b], value) if b in table else value

    for a, first, last, sides in strips:
        scores = lax.dot_general(
            held[place[a] * ROWS : (place[a] + 1) * ROWS, :],
            held[first * ROWS : (last + 1) * ROWS, :],
            (((1,), (1,)), ((), ())),
            preferred_element_type=jnp.float32,
        )
        near = word_columns(a)
        for i in range(first, last + 1):
            b = order[i]
            far = words(b)
            down = []
            for k in range(ROWS // 128):
                at = (i - first) * ROWS + k * 128
                mixed = near ^ far[:, k * 128 : (k + 1) * 128]
                partner = (mixed > 0) & (mixed < 65536)
                kept = jnp.where(partner, scores[:, at : at + 128], -1.0)
                if a in sides:
                    update(over_lanes, a, kept)
                down.append(jnp.max(kept.reshape(ROWS // 8, 8, 128), axis=0))
            if b in sides and b != a:
                update(over_rows, b, jnp.concatenate(down, axis=1))

    for b in results:
        value = jnp.full((1, ROWS), -1.0, jnp.float32)
        if b in over_lanes:
            value = jnp.maximum(value, jnp.max(over_lanes[b].T, axis=0, keepdims=True))
        if b in over_rows:
            value = jnp.maximum(value, jnp.max(over_rows[b], axis=0, keepdims=True))
        if b in earlier:
            value = jnp.maximum(value, earlier[b][...])
        outs[b][...] = value


def score(step, blocks, earlier):
    order, strips, results = STEPS[step]
    n = len(order)
    given = tuple(b for b in results if b in earlier)
    pairs = sum(last + 1 - first for _, first, last, _ in strips)
    vmem = pl.BlockSpec(memory_space=pltpu.VMEM)
    values = pl.pallas_call(
        functools.partial(score_kernel, step, given),
        out_shape=[jax.ShapeDtypeStruct((1, ROWS), jnp.float32)] * len(results),
        in_specs=[pl.BlockSpec(memory_space=pl.ANY)] * n + [vmem] * len(given),
        out_specs=[vmem] * len(results),
        scratch_shapes=[
            pltpu.VMEM((n * ROWS, WIDTH), jnp.bfloat16),
            pltpu.VMEM((n, TAIL, WIDTH), jnp.bfloat16),
            pltpu.SemaphoreType.DMA((2, n)),
        ],
        compiler_params=pltpu.CompilerParams(vmem_limit_bytes=24 << 20),
        cost_estimate=pl.CostEstimate(
            flops=2 * pairs * ROWS * ROWS * WIDTH, bytes_accessed=n * BLOCK * WIDTH * 2, transcendentals=0
        ),
        name="score_" + step,
    )(*[blocks[b] for b in order], *[earlier[b] for b in given])
    return dict(zip(results, values))


def local(embeddings, cluster_id, source_id):
    blocks = {0: prepare(embeddings, cluster_id, source_id)}
    for block, by in FIRST:
        blocks[block] = receive(blocks[0], by)
    for block, parent, by in SECOND:
        blocks[block] = receive(blocks[parent], by)
    early = score("early", blocks, {})
    middle = score("middle", blocks, {b: early[b] for b in (0, 4)})
    late = score("late", blocks, {b: middle[b] for b in (0, 4)})
    own = late[0]
    for b, values in ((1, early), (2, early), (3, early), (5, middle), (6, middle), (4, late)):
        own = jnp.maximum(own, receive(values[b], OFFSETS[b], back=True))
    return own.reshape(ROWS)


def solution(mesh):
    return jax.shard_map(
        local,
        mesh=mesh,
        in_specs=(P(("grp", "blk"), None), P(("grp", "blk")), P(("grp", "blk"))),
        out_specs=P(("grp", "blk")),
        check_vma=False,
    )
```

profile of v0, /device:TPU:0, one launch (start us, length us, event | category | flops | bytes accessed | tf_op | source)
XLA Modules:
  0.0 70.5 jit_solution(6766041970530718054)
XLA Ops:
  0.0 1.1 %copy-done = bf16[384,1024]{1,0:T(8,128)(2,1)S(1)} copy-done((bf16[384,1024]{1,0:T(8,128)(2,1)S(1)}, bf16[384,1024]{1,0:T(8,128)(2,1)}, u32[]{:S(2)}) %copy-start) | copy-done | bytes 786456
  1.1 0.7 copy-done.1
  1.8 0.7 copy-done.2
  2.5 0.7 %prepare.1.refs_0_.refs_5_.refs_2_ = bf16[400,1024]{1,0:T(8,128)(2,1)S(1)} custom-call(bf16[384,1024]{1,0:T(8,128)(2,1)S(1)} %copy-done, s32[384]{0:T(512)S(1)} %copy-done.1, s32[384]{0:T(512)S(1)} %copy-done.2), custom_call_target="tpu_custom_call" | custom-call | tf_op jit(solution)/shard_map/prepare/pallas_call | solution.py:104
  3.2 5.1 %collective-permute-start.5 = (bf16[400,1024]{1,0:T(8,128)(2,1)S(1)}, bf16[400,1024]{1,0:T(8,128)(2,1)S(1)}, u32[]{:S(2)}, u32[]{:S(2)}) collective-permute-start(bf16[400,1024]{1,0:T(8,128)(2,1)S(1)} %prepare.1.refs_0_.refs_5_.refs_2_), channel_id=1, source_target_pairs={{7,0},{4,1},{5,2},{6,3},{11,4},{8,5},{9,6},{10,7},{15,8},{12,9},{1... | collective-permute-start | bytes 2457608 | tf_op jit(solution)/shard_map/ppermute | solution.py:84
  8.3 1.7 %collective-permute-start = (bf16[400,1024]{1,0:T(8,128)(2,1)S(1)}, bf16[400,1024]{1,0:T(8,128)(2,1)S(1)}, u32[]{:S(2)}, u32[]{:S(2)}) collective-permute-start(bf16[400,1024]{1,0:T(8,128)(2,1)S(1)} %prepare.1.refs_0_.refs_5_.refs_2_), channel_id=1, source_target_pairs={{1,0},{2,1},{3,2},{0,3},{5,4},{6,5},{7,6},{4,7},{9,8},{10,9},{11,1... | collective-permute-start | bytes 2457608 | tf_op jit(solution)/shard_map/ppermute | solution.py:84
  10.1 0.0 collective-permute-start.2
  10.1 1.6 %collective-permute-start.4 = (bf16[400,1024]{1,0:T(8,128)(2,1)S(1)}, bf16[400,1024]{1,0:T(8,128)(2,1)S(1)}, u32[]{:S(2)}, u32[]{:S(2)}) collective-permute-start(bf16[400,1024]{1,0:T(8,128)(2,1)S(1)} %prepare.1.refs_0_.refs_5_.refs_2_), channel_id=1, source_target_pairs={{16,0},{17,1},{18,2},{19,3},{20,4},{21,5},{22,6},{23,7},{24,8},{25... | collective-permute-start | bytes 2457608 | tf_op jit(solution)/shard_map/ppermute | solution.py:84
  11.7 14.2 %collective-permute-done.5.refs_2_ = bf16[400,1024]{1,0:T(8,128)(2,1)S(1)} collective-permute-done((bf16[400,1024]{1,0:T(8,128)(2,1)S(1)}, bf16[400,1024]{1,0:T(8,128)(2,1)S(1)}, u32[]{:S(2)}, u32[]{:S(2)}) %collective-permute-start.5) | collective-permute-done | bytes 819232 | tf_op jit(solution)/shard_map/ppermute | solution.py:84
  25.8 2.5 %collective-permute-start.6 = (bf16[400,1024]{1,0:T(8,128)(2,1)S(1)}, bf16[400,1024]{1,0:T(8,128)(2,1)S(1)}, u32[]{:S(2)}, u32[]{:S(2)}) collective-permute-start(bf16[400,1024]{1,0:T(8,128)(2,1)S(1)} %collective-permute-done.5.refs_2_), channel_id=1, source_target_pairs={{19,0},{16,1},{17,2},{18,3},{23,4},{20,5},{21,6},{22,7},{27,8},{24... | collective-permute-start | bytes 2457608 | tf_op jit(solution)/shard_map/ppermute | solution.py:84
  28.3 3.7 %collective-permute-start.7 = (bf16[400,1024]{1,0:T(8,128)(2,1)S(1)}, bf16[400,1024]{1,0:T(8,128)(2,1)S(1)}, u32[]{:S(2)}, u32[]{:S(2)}) collective-permute-start(bf16[400,1024]{1,0:T(8,128)(2,1)S(1)} %collective-permute-done.5.refs_2_), channel_id=1, source_target_pairs={{4,0},{5,1},{6,2},{7,3},{8,4},{9,5},{10,6},{11,7},{12,8},{13,9},{1... | collective-permute-start | bytes 2457608 | tf_op jit(solution)/shard_map/ppermute | solution.py:84
  32.0 0.0 collective-permute-done.refs_1_.refs_0_
  32.0 3.0 %collective-permute-start.1 = (bf16[400,1024]{1,0:T(8,128)(2,1)S(1)}, bf16[400,1024]{1,0:T(8,128)(2,1)S(1)}, u32[]{:S(2)}, u32[]{:S(2)}) collective-permute-start(bf16[400,1024]{1,0:T(8,128)(2,1)S(1)} %collective-permute-done.refs_1_.refs_0_), channel_id=1, source_target_pairs={{1,0},{2,1},{3,2},{0,3},{5,4},{6,5},{7,6},{4,7},{9,8},{10,9},{11,1... | collective-permute-start | bytes 2457608 | tf_op jit(solution)/shard_map/ppermute | solution.py:84
  35.0 0.0 collective-permute-done.2.refs_3_.refs_4_
  35.0 0.0 collective-permute-start.3
  35.0 0.0 collective-permute-done.4.refs_4_.refs_1_.refs_3_
  35.0 5.0 %score_early.1 = (f32[1,384]{1,0:T(1,128)S(1)}, f32[1,384]{1,0:T(1,128)S(1)}, f32[1,384]{1,0:T(1,128)S(1)}, f32[1,384]{1,0:T(1,128)S(1)}, f32[1,384]{1,0:T(1,128)S(1)}) custom-call(bf16[400,1024]{1,0:T(8,128)(2,1)S(1)} %prepare.1.refs_0_.refs_5_.refs_2_, bf16[400,1024]{1,0:T(8,128)(2,1)S(1)} %collective-permute-done.refs_1_.refs_0_, ...), custom_call_target="tpu_custom_call" | custom-call | flops 3321888768 | bytes 4096000 | tf_op jit(solution)/shard_map/score_early/pallas_call | solution.py:186
  40.0 3.3 %collective-permute-start.10 = (f32[1,384]{1,0:T(1,128)S(1)}, f32[1,384]{1,0:T(1,128)S(1)}, u32[]{:S(2)}, u32[]{:S(2)}) collective-permute-start(f32[1,384]{1,0:T(1,128)S(1)} %get-tuple-element.23), channel_id=1, source_target_pairs={{0,12},{1,13},{2,14},{3,15},{4,0},{5,1},{6,2},{7,3},{8,4},{9,5},{1... | collective-permute-start | bytes 4616 | tf_op jit(solution)/shard_map/ppermute | solution.py:84
  43.3 4.0 %collective-permute-done.6.refs_2_ = bf16[400,1024]{1,0:T(8,128)(2,1)S(1)} collective-permute-done((bf16[400,1024]{1,0:T(8,128)(2,1)S(1)}, bf16[400,1024]{1,0:T(8,128)(2,1)S(1)}, u32[]{:S(2)}, u32[]{:S(2)}) %collective-permute-start.6) | collective-permute-done | bytes 819232 | tf_op jit(solution)/shard_map/ppermute | solution.py:84
  47.3 0.1 collective-permute-start.8
  47.3 1.0 %collective-permute-done.7.refs_3_ = bf16[400,1024]{1,0:T(8,128)(2,1)S(1)} collective-permute-done((bf16[400,1024]{1,0:T(8,128)(2,1)S(1)}, bf16[400,1024]{1,0:T(8,128)(2,1)S(1)}, u32[]{:S(2)}, u32[]{:S(2)}) %collective-permute-start.7) | collective-permute-done | bytes 819232 | tf_op jit(solution)/shard_map/ppermute | solution.py:84
  48.4 6.8 %collective-permute-start.9 = (f32[1,384]{1,0:T(1,128)S(1)}, f32[1,384]{1,0:T(1,128)S(1)}, u32[]{:S(2)}, u32[]{:S(2)}) collective-permute-start(f32[1,384]{1,0:T(1,128)S(1)} %get-tuple-element.22), channel_id=1, source_target_pairs={{0,7},{1,4},{2,5},{3,6},{4,11},{5,8},{6,9},{7,10},{8,15},{9,12},{1... | collective-permute-start | bytes 4616 | tf_op jit(solution)/shard_map/ppermute | solution.py:84
  55.2 2.8 %score_middle.1 = (f32[1,384]{1,0:T(1,128)S(1)}, f32[1,384]{1,0:T(1,128)S(1)}, f32[1,384]{1,0:T(1,128)S(1)}, f32[1,384]{1,0:T(1,128)S(1)}) custom-call(bf16[400,1024]{1,0:T(8,128)(2,1)S(1)} %collective-permute-done.refs_1_.refs_0_, bf16[400,1024]{1,0:T(8,128)(2,1)S(1)} %collective-permute-done.4.refs_4_.refs_1_.refs_3_, ...), custom_call_target="tpu_custom_call" | custom-call | flops 1509949440 | bytes 4915200 | tf_op jit(solution)/shard_map/score_middle/pallas_call | solution.py:186
  58.0 0.0 collective-permute-done.1.refs_0_
  58.0 0.0 collective-permute-done.3.refs_1_
  58.0 2.1 %score_late.1 = (f32[1,384]{1,0:T(1,128)S(1)}, f32[1,384]{1,0:T(1,128)S(1)}) custom-call(bf16[400,1024]{1,0:T(8,128)(2,1)S(1)} %collective-permute-done.1.refs_0_, bf16[400,1024]{1,0:T(8,128)(2,1)S(1)} %collective-permute-done.3.refs_1_, bf16[400,1024]{1,0:T(8,128)(2,1)S(1)} %prepare.1.refs_0_.refs_5_.refs_2_, ...), custom_call_target="tpu_custom_call" | custom-call | flops 1207959552 | bytes 3276800 | tf_op jit(solution)/shard_map/score_late/pallas_call | solution.py:186
  60.2 1.7 %collective-permute-start.13 = (f32[1,384]{1,0:T(1,128)S(1)}, f32[1,384]{1,0:T(1,128)S(1)}, u32[]{:S(2)}, u32[]{:S(2)}) collective-permute-start(f32[1,384]{1,0:T(1,128)S(1)} %get-tuple-element.26), channel_id=1, source_target_pairs={{0,16},{1,17},{2,18},{3,19},{4,20},{5,21},{6,22},{7,23},{8,24},{9,... | collective-permute-start | bytes 4616 | tf_op jit(solution)/shard_map/ppermute | solution.py:84
  61.9 1.3 %collective-permute-start.12 = (f32[1,384]{1,0:T(1,128)S(1)}, f32[1,384]{1,0:T(1,128)S(1)}, u32[]{:S(2)}, u32[]{:S(2)}) collective-permute-start(f32[1,384]{1,0:T(1,128)S(1)} %get-tuple-element.25), channel_id=1, source_target_pairs={{0,22},{1,23},{2,20},{3,21},{4,26},{5,27},{6,24},{7,25},{8,30},{9,... | collective-permute-start | bytes 4616 | tf_op jit(solution)/shard_map/ppermute | solution.py:84
  63.1 0.7 %collective-permute-done.13 = f32[1,384]{1,0:T(1,128)S(1)} collective-permute-done((f32[1,384]{1,0:T(1,128)S(1)}, f32[1,384]{1,0:T(1,128)S(1)}, u32[]{:S(2)}, u32[]{:S(2)}) %collective-permute-start.13) | collective-permute-done | bytes 1568 | tf_op jit(solution)/shard_map/ppermute | solution.py:84
  63.8 4.0 %collective-permute-done.11 = f32[1,384]{1,0:T(1,128)S(1)} collective-permute-done((f32[1,384]{1,0:T(1,128)S(1)}, f32[1,384]{1,0:T(1,128)S(1)}, u32[]{:S(2)}, u32[]{:S(2)}) %collective-permute-start.11) | collective-permute-done | bytes 1568 | tf_op jit(solution)/shard_map/ppermute | solution.py:84
  67.8 2.1 %collective-permute-done.12 = f32[1,384]{1,0:T(1,128)S(1)} collective-permute-done((f32[1,384]{1,0:T(1,128)S(1)}, f32[1,384]{1,0:T(1,128)S(1)}, u32[]{:S(2)}, u32[]{:S(2)}) %collective-permute-start.12) | collective-permute-done | bytes 1568 | tf_op jit(solution)/shard_map/ppermute | solution.py:84
  69.9 0.6 maximum_reduce_fusion
  (7 shorter events, 0.0 us)
Async XLA Ops:
  0.0 1.1 %copy-start = (bf16[384,1024]{1,0:T(8,128)(2,1)S(1)}, bf16[384,1024]{1,0:T(8,128)(2,1)}, u32[]{:S(2)}) copy-start(bf16[384,1024]{1,0:T(8,128)(2,1)} %embeddings.1) | copy-start | bytes 2359300
  1.1 0.7 copy-start.1
  1.8 0.7 copy-start.2
  3.2 22.6 %collective-permute-start.5 = (bf16[400,1024]{1,0:T(8,128)(2,1)S(1)}, bf16[400,1024]{1,0:T(8,128)(2,1)S(1)}, u32[]{:S(2)}, u32[]{:S(2)}) collective-permute-start(bf16[400,1024]{1,0:T(8,128)(2,1)S(1)} %prepare.1.refs_0_.refs_5_.refs_2_), channel_id=1, source_target_pairs={{7,0},{4,1},{5,2},{6,3},{11,4},{8,5},{9,6},{10,7},{15,8},{12,9},{1... | collective-permute-start | bytes 2457608 | tf_op jit(solution)/shard_map/ppermute | solution.py:84
  8.3 23.7 %collective-permute-start = (bf16[400,1024]{1,0:T(8,128)(2,1)S(1)}, bf16[400,1024]{1,0:T(8,128)(2,1)S(1)}, u32[]{:S(2)}, u32[]{:S(2)}) collective-permute-start(bf16[400,1024]{1,0:T(8,128)(2,1)S(1)} %prepare.1.refs_0_.refs_5_.refs_2_), channel_id=1, source_target_pairs={{1,0},{2,1},{3,2},{0,3},{5,4},{6,5},{7,6},{4,7},{9,8},{10,9},{11,1... | collective-permute-start | bytes 2457608 | tf_op jit(solution)/shard_map/ppermute | solution.py:84
  10.1 24.9 %collective-permute-start.2 = (bf16[400,1024]{1,0:T(8,128)(2,1)S(1)}, bf16[400,1024]{1,0:T(8,128)(2,1)S(1)}, u32[]{:S(2)}, u32[]{:S(2)}) collective-permute-start(bf16[400,1024]{1,0:T(8,128)(2,1)S(1)} %prepare.1.refs_0_.refs_5_.refs_2_), channel_id=1, source_target_pairs={{12,0},{13,1},{14,2},{15,3},{0,4},{1,5},{2,6},{3,7},{4,8},{5,9},{6... | collective-permute-start | bytes 2457608 | tf_op jit(solution)/shard_map/ppermute | solution.py:84
  10.1 24.9 %collective-permute-start.4 = (bf16[400,1024]{1,0:T(8,128)(2,1)S(1)}, bf16[400,1024]{1,0:T(8,128)(2,1)S(1)}, u32[]{:S(2)}, u32[]{:S(2)}) collective-permute-start(bf16[400,1024]{1,0:T(8,128)(2,1)S(1)} %prepare.1.refs_0_.refs_5_.refs_2_), channel_id=1, source_target_pairs={{16,0},{17,1},{18,2},{19,3},{20,4},{21,5},{22,6},{23,7},{24,8},{25... | collective-permute-start | bytes 2457608 | tf_op jit(solution)/shard_map/ppermute | solution.py:84
  25.8 21.4 %collective-permute-start.6 = (bf16[400,1024]{1,0:T(8,128)(2,1)S(1)}, bf16[400,1024]{1,0:T(8,128)(2,1)S(1)}, u32[]{:S(2)}, u32[]{:S(2)}) collective-permute-start(bf16[400,1024]{1,0:T(8,128)(2,1)S(1)} %collective-permute-done.5.refs_2_), channel_id=1, source_target_pairs={{19,0},{16,1},{17,2},{18,3},{23,4},{20,5},{21,6},{22,7},{27,8},{24... | collective-permute-start | bytes 2457608 | tf_op jit(solution)/shard_map/ppermute | solution.py:84
  28.3 20.0 %collective-permute-start.7 = (bf16[400,1024]{1,0:T(8,128)(2,1)S(1)}, bf16[400,1024]{1,0:T(8,128)(2,1)S(1)}, u32[]{:S(2)}, u32[]{:S(2)}) collective-permute-start(bf16[400,1024]{1,0:T(8,128)(2,1)S(1)} %collective-permute-done.5.refs_2_), channel_id=1, source_target_pairs={{4,0},{5,1},{6,2},{7,3},{8,4},{9,5},{10,6},{11,7},{12,8},{13,9},{1... | collective-permute-start | bytes 2457608 | tf_op jit(solution)/shard_map/ppermute | solution.py:84
  32.0 26.0 %collective-permute-start.1 = (bf16[400,1024]{1,0:T(8,128)(2,1)S(1)}, bf16[400,1024]{1,0:T(8,128)(2,1)S(1)}, u32[]{:S(2)}, u32[]{:S(2)}) collective-permute-start(bf16[400,1024]{1,0:T(8,128)(2,1)S(1)} %collective-permute-done.refs_1_.refs_0_), channel_id=1, source_target_pairs={{1,0},{2,1},{3,2},{0,3},{5,4},{6,5},{7,6},{4,7},{9,8},{10,9},{11,1... | collective-permute-start | bytes 2457608 | tf_op jit(solution)/shard_map/ppermute | solution.py:84
  35.0 23.1 %collective-permute-start.3 = (bf16[400,1024]{1,0:T(8,128)(2,1)S(1)}, bf16[400,1024]{1,0:T(8,128)(2,1)S(1)}, u32[]{:S(2)}, u32[]{:S(2)}) collective-permute-start(bf16[400,1024]{1,0:T(8,128)(2,1)S(1)} %collective-permute-done.2.refs_3_.refs_4_), channel_id=1, source_target_pairs={{12,0},{13,1},{14,2},{15,3},{0,4},{1,5},{2,6},{3,7},{4,8},{5,9},{6... | collective-permute-start | bytes 2457608 | tf_op jit(solution)/shard_map/ppermute | solution.py:84
  40.0 21.9 %collective-permute-start.10 = (f32[1,384]{1,0:T(1,128)S(1)}, f32[1,384]{1,0:T(1,128)S(1)}, u32[]{:S(2)}, u32[]{:S(2)}) collective-permute-start(f32[1,384]{1,0:T(1,128)S(1)} %get-tuple-element.23), channel_id=1, source_target_pairs={{0,12},{1,13},{2,14},{3,15},{4,0},{5,1},{6,2},{7,3},{8,4},{9,5},{1... | collective-permute-start | bytes 4616 | tf_op jit(solution)/shard_map/ppermute | solution.py:84
  47.3 15.9 %collective-permute-start.8 = (f32[1,384]{1,0:T(1,128)S(1)}, f32[1,384]{1,0:T(1,128)S(1)}, u32[]{:S(2)}, u32[]{:S(2)}) collective-permute-start(f32[1,384]{1,0:T(1,128)S(1)} %get-tuple-element.21), channel_id=1, source_target_pairs={{0,1},{1,2},{2,3},{3,0},{4,5},{5,6},{6,7},{7,4},{8,9},{9,10},{10,1... | collective-permute-start | bytes 4616 | tf_op jit(solution)/shard_map/ppermute | solution.py:84
  48.4 14.8 %collective-permute-start.9 = (f32[1,384]{1,0:T(1,128)S(1)}, f32[1,384]{1,0:T(1,128)S(1)}, u32[]{:S(2)}, u32[]{:S(2)}) collective-permute-start(f32[1,384]{1,0:T(1,128)S(1)} %get-tuple-element.22), channel_id=1, source_target_pairs={{0,7},{1,4},{2,5},{3,6},{4,11},{5,8},{6,9},{7,10},{8,15},{9,12},{1... | collective-permute-start | bytes 4616 | tf_op jit(solution)/shard_map/ppermute | solution.py:84
  60.2 3.7 %collective-permute-start.13 = (f32[1,384]{1,0:T(1,128)S(1)}, f32[1,384]{1,0:T(1,128)S(1)}, u32[]{:S(2)}, u32[]{:S(2)}) collective-permute-start(f32[1,384]{1,0:T(1,128)S(1)} %get-tuple-element.26), channel_id=1, source_target_pairs={{0,16},{1,17},{2,18},{3,19},{4,20},{5,21},{6,22},{7,23},{8,24},{9,... | collective-permute-start | bytes 4616 | tf_op jit(solution)/shard_map/ppermute | solution.py:84
  61.8 6.0 %collective-permute-start.11 = (f32[1,384]{1,0:T(1,128)S(1)}, f32[1,384]{1,0:T(1,128)S(1)}, u32[]{:S(2)}, u32[]{:S(2)}) collective-permute-start(f32[1,384]{1,0:T(1,128)S(1)} %get-tuple-element.24), channel_id=1, source_target_pairs={{0,11},{1,8},{2,9},{3,10},{4,15},{5,12},{6,13},{7,14},{8,3},{9,0},... | collective-permute-start | bytes 4616 | tf_op jit(solution)/shard_map/ppermute | solution.py:84
  61.9 8.1 %collective-permute-start.12 = (f32[1,384]{1,0:T(1,128)S(1)}, f32[1,384]{1,0:T(1,128)S(1)}, u32[]{:S(2)}, u32[]{:S(2)}) collective-permute-start(f32[1,384]{1,0:T(1,128)S(1)} %get-tuple-element.25), channel_id=1, source_target_pairs={{0,22},{1,23},{2,20},{3,21},{4,26},{5,27},{6,24},{7,25},{8,30},{9,... | collective-permute-start | bytes 4616 | tf_op jit(solution)/shard_map/ppermute | solution.py:84
where the time goes:
time: 71.5 us; the launch traced here: 70.5 us
  starting transfers between devices  30.7 us (43%)
  waiting for transfers between devices  26 us (36%)
  Pallas kernels  10.6 us (15%)
  local copies, waits for them, and re-layouts  2.49 us (3%)
    ppermute x14, starting transfers between devices, receive(): return lax.ppermute(array, 'blk', links)  30.7 us
    ppermute x14, waiting for transfers between devices, receive(): return lax.ppermute(array, 'blk', links)  26 us
    pallas_call x3, Pallas kernels, score(): pl.pallas_call(functools.partial(score_kernel, step, given), out_shape=[j...  9.93 us
    unnamed x6, local copies, waits for them, and re-layouts  2.49 us
  transfers between devices with their start and end apart: 14, of which 6 were waited for; matrix products, arithmetic and copies ran while one was open for 0% of the time, Pallas kernels for 14%

commit v1 on v0

v1 whole, which is shorter than its diff:
```python
import functools

import jax
import jax.numpy as jnp
from jax import lax
from jax.experimental import pallas as pl
from jax.experimental.pallas import tpu as pltpu
from jax.sharding import PartitionSpec as P

TORUS = (2, 4, 4)
OFFSETS = (
    (0, 0, 0),
    (0, 0, 3),
    (0, 1, 0),
    (0, 3, 1),
    (1, 0, 0),
    (0, 0, 2),
    (0, 2, 0),
    (0, 2, 2),
    (1, 0, 3),
)
FIRST = ((1, (0, 0, 3)), (2, (0, 1, 0)), (3, (0, 3, 1)), (4, (1, 0, 0)))
SECOND = ((8, 1, (1, 0, 0)), (5, 1, (0, 0, 3)), (6, 2, (0, 1, 0)), (7, 3, (0, 3, 1)))
ROWS = 384
TAIL = 16
BLOCK = ROWS + TAIL
WIDTH = 1024
STRIPE = 64
STRIPES = ROWS // STRIPE
STEPS = {
    "early": (
        (0, 1, 2, 3, 4),
        ((0, 0, 0, 4, (0, 2, 3)), (1, 1, 2, 4, (2, 3, 4)), (2, 2, 3, 4, (2, 3, 4)), (3, 3, 4, 4, (3, 4))),
    ),
    "middle": ((0, 2, 3, 4, 8, 5), ((4, 4, 0, 3, (2, 3, 8)), (5, 5, 0, 3, (0, 2, 3, 4)))),
    "late": ((8, 4, 6, 7), ((0, 1, 2, 3, (4, 8)),)),
    "last": ((0, 6, 7), ((0, 0, 1, 2, (0,)),)),
}


def difference(a, b):
    return tuple((p - q) % n for p, q, n in zip(a, b, TORUS))


def products(step):
    order, strips = STEPS[step]
    for first, last, left, right, sides in strips:
        yield order[first : last + 1], order[left : right + 1], sides


def targets(step):
    return tuple(sorted({b for rows, columns, sides in products(step) for b in sides if b in rows + columns}))


def check():
    met = set()
    for step in STEPS:
        for rows, columns, sides in products(step):
            for a in rows:
                for b in columns:
                    met |= {difference(OFFSETS[b], OFFSETS[a])} if a in sides else set()
                    met |= {difference(OFFSETS[a], OFFSETS[b])} if b in sides else set()
    assert len(met) == 32
    assert all(OFFSETS[block] == by for block, by in FIRST)
    assert all(difference(OFFSETS[block], OFFSETS[parent]) == by for block, parent, by in SECOND)


check()


def flat(y, z, x):
    return ((y % TORUS[0]) * TORUS[1] + z % TORUS[1]) * TORUS[2] + x % TORUS[2]


def receive(array, by, back=False):
    links = []
    for y in range(TORUS[0]):
        for z in range(TORUS[1]):
            for x in range(TORUS[2]):
                far, near = flat(y + by[0], z + by[1], x + by[2]), flat(y, z, x)
                links.append((near, far) if back else (far, near))
    return lax.ppermute(array, "blk", links)


def prepare_kernel(embeddings, cluster, source, out, raw, clusters, sources, unit, sems):
    def copy(source_rows, target_rows, sem):
        return pltpu.make_async_copy(source_rows, target_rows, sems.at[sem])

    stripes = [slice(i * STRIPE, (i + 1) * STRIPE) for i in range(STRIPES)]
    ids = [copy(cluster, clusters, 2 * STRIPES), copy(source, sources, 2 * STRIPES + 1)]
    arriving = [copy(embeddings.at[rows], raw.at[rows], i) for i, rows in enumerate(stripes)]
    leaving = [copy(unit.at[rows], out.at[rows], STRIPES + i) for i, rows in enumerate(stripes)]
    leaving.append(copy(unit.at[ROWS:], out.at[ROWS:], 2 * STRIPES + 2))
    for move in ids + arriving:
        move.start()
    for move in ids:
        move.wait()
    line = lax.broadcasted_iota(jnp.int32, (TAIL, ROWS), 0)
    number = sources[...].reshape(1, ROWS)
    rank = clusters[...].reshape(1, ROWS)
    tail = jnp.where(line == 0, rank, jnp.where(line == 1, number // 256, jnp.where(line == 2, number % 256, 0)))
    unit[ROWS:, :ROWS] = tail.astype(jnp.float32).astype(jnp.bfloat16)
    unit[ROWS:, ROWS:] = jnp.zeros((TAIL, WIDTH - ROWS), jnp.bfloat16)
    leaving[STRIPES].start()
    for i, rows in enumerate(stripes):
        arriving[i].wait()
        widened = raw[rows, :].astype(jnp.float32)
        factor = lax.rsqrt(jnp.mean(widened * widened, axis=1, keepdims=True) + 1e-06) / 32.0
        unit[rows, :] = (widened * factor).astype(jnp.bfloat16)
        leaving[i].start()
    for move in leaving:
        move.wait()


def prepare(embeddings, cluster_id, source_id):
    far = pl.BlockSpec(memory_space=pltpu.HBM)
    return pl.pallas_call(
        prepare_kernel,
        out_shape=jax.ShapeDtypeStruct((BLOCK, WIDTH), jnp.bfloat16),
        in_specs=[far] * 3,
        out_specs=far,
        scratch_shapes=[
            pltpu.VMEM((ROWS, WIDTH), jnp.bfloat16),
            pltpu.VMEM((ROWS,), jnp.int32),
            pltpu.VMEM((ROWS,), jnp.int32),
            pltpu.VMEM((BLOCK, WIDTH), jnp.bfloat16),
            pltpu.SemaphoreType.DMA((2 * STRIPES + 3,)),
        ],
        compiler_params=pltpu.CompilerParams(vmem_limit_bytes=60 << 20),
        name="prepare",
    )(embeddings, cluster_id, source_id)


def score_kernel(step, given, *refs):
    order = STEPS[step][0]
    n = len(order)
    results = targets(step)
    place = {b: i for i, b in enumerate(order)}
    blocks, refs = refs[:n], refs[n:]
    earlier, refs = dict(zip(given, refs)), refs[len(given) :]
    outs, refs = dict(zip(results, refs)), refs[len(results) :]
    held, ids, sems = refs
    copies = []
    for i, block in enumerate(blocks):
        copies.append(pltpu.make_async_copy(block.at[ROWS:], ids.at[i], sems.at[0, i]))
        copies.append(pltpu.make_async_copy(block.at[:ROWS], held.at[pl.ds(i * ROWS, ROWS)], sems.at[1, i]))
    for copy in copies:
        copy.start()
    for copy in copies:
        copy.wait()

    def word(b):
        parts = ids[place[b], :, :ROWS].astype(jnp.float32)
        return parts[0:1] * 65536.0 + parts[1:2] * 256.0 + parts[2:3]

    over_lanes, over_rows = {}, {}

    def update(table, b, value):
        table[b] = jnp.maximum(table[b], value) if b in table else value

    for rows, columns, sides in products(step):
        scores = lax.dot_general(
            held[place[rows[0]] * ROWS : (place[rows[-1]] + 1) * ROWS, :],
            held[place[columns[0]] * ROWS : (place[columns[-1]] + 1) * ROWS, :],
            (((1,), (1,)), ((), ())),
            preferred_element_type=jnp.float32,
        )
        for j, a in enumerate(rows):
            near = jnp.broadcast_to(word(a), (128, ROWS)).T.astype(jnp.int32)
            for i, b in enumerate(columns):
                far = word(b).astype(jnp.int32)
                down = []
                for k in range(ROWS // 128):
                    at = i * ROWS + k * 128
                    mixed = near ^ far[:, k * 128 : (k + 1) * 128]
                    partner = (mixed > 0) & (mixed < 65536)
                    kept = jnp.where(partner, scores[j * ROWS : (j + 1) * ROWS, at : at + 128], -1.0)
                    if a in sides:
                        update(over_lanes, a, kept)
                    down.append(jnp.max(kept.reshape(ROWS // 8, 8, 128), axis=0))
                if b in sides and b != a:
                    update(over_rows, b, jnp.concatenate(down, axis=1))

    for b in results:
        value = jnp.full((1, ROWS), -1.0, jnp.float32)
        if b in over_lanes:
            value = jnp.maximum(value, jnp.max(over_lanes[b].T, axis=0, keepdims=True))
        if b in over_rows:
            value = jnp.maximum(value, jnp.max(over_rows[b], axis=0, keepdims=True))
        if b in earlier:
            value = jnp.maximum(value, earlier[b][...])
        outs[b][...] = value


def score(step, blocks, earlier):
    order = STEPS[step][0]
    n = len(order)
    results = targets(step)
    given = tuple(b for b in results if b in earlier)
    pairs = sum(len(rows) * len(columns) for rows, columns, _ in products(step))
    vmem = pl.BlockSpec(memory_space=pltpu.VMEM)
    values = pl.pallas_call(
        functools.partial(score_kernel, step, given),
        out_shape=[jax.ShapeDtypeStruct((1, ROWS), jnp.float32)] * len(results),
        in_specs=[pl.BlockSpec(memory_space=pl.ANY)] * n + [vmem] * len(given),
        out_specs=[vmem] * len(results),
        scratch_shapes=[
            pltpu.VMEM((n * ROWS, WIDTH), jnp.bfloat16),
            pltpu.VMEM((n, TAIL, WIDTH), jnp.bfloat16),
            pltpu.SemaphoreType.DMA((2, n)),
        ],
        compiler_params=pltpu.CompilerParams(vmem_limit_bytes=28 << 20),
        cost_estimate=pl.CostEstimate(
            flops=2 * pairs * ROWS * ROWS * WIDTH, bytes_accessed=n * BLOCK * WIDTH * 2, transcendentals=0
        ),
        name="score_" + step,
    )(*[blocks[b] for b in order], *[earlier[b] for b in given])
    return {**earlier, **dict(zip(results, values))}


def local(embeddings, cluster_id, source_id):
    blocks = {0: prepare(embeddings, cluster_id, source_id)}
    for block, by in FIRST:
        blocks[block] = receive(blocks[0], by)
    for block, parent, by in SECOND:
        blocks[block] = receive(blocks[parent], by)
    best = score("early", blocks, {})
    best = score("middle", blocks, best)
    got = [receive(best[b], OFFSETS[b], back=True) for b in (3, 2)]
    best = score("late", blocks, best)
    got += [receive(best[b], OFFSETS[b], back=True) for b in (8, 4)]
    best = score("last", blocks, best)
    own = best[0]
    for value in got:
        own = jnp.maximum(own, value)
    return own.reshape(ROWS)


def solution(mesh):
    return jax.shard_map(
        local,
        mesh=mesh,
        in_specs=(P(("grp", "blk"), None), P(("grp", "blk")), P(("grp", "blk"))),
        out_specs=P(("grp", "blk")),
        check_vma=False,
    )
```

time: 71.5 us -> 64.7 us (0.905); the launches traced: 70.5 us -> 64.6 us
  starting transfers between devices: 30.7 us -> 19.6 us
  Pallas kernels: 10.6 us -> 14.3 us
  waiting for transfers between devices: 26 us -> 28.8 us
  local copies, waits for them, and re-layouts: 2.49 us -> 1.15 us
    ppermute x14 -> x12, starting transfers between devices: 30.7 us -> 19.6 us  [receive(): return lax.ppermute(array, 'blk', links)]
    ppermute x14 -> x12, waiting for transfers between devices: 26 us -> 28.8 us  [receive(): return lax.ppermute(array, 'blk', links)]
    pallas_call x3 -> x4, Pallas kernels: 9.93 us -> 11.9 us  [score(): pl.pallas_call(functools.partial(score_kernel, step, given), out_shape=[j...]
    pallas_call x1, Pallas kernels: 0.71 us -> 2.43 us  [prepare(): pl.pallas_call(prepare_kernel, out_shape=jax.ShapeDtypeStruct((BLOCK, WID...]
    unnamed x6 -> x4, local copies, waits for them, and re-layouts: 2.49 us -> 1.15 us
  transfers between devices with their start and end apart: 14 -> 12, of which waited for: 6 -> 6; matrix products, arithmetic and copies ran while one was open for 0% -> 0% of each run, Pallas kernels for 14% -> 15%
where the time goes in v1:
time: 64.7 us; the launch traced here: 64.6 us
  waiting for transfers between devices  28.8 us (45%)
  starting transfers between devices  19.6 us (30%)
  Pallas kernels  14.3 us (22%)
  local copies, waits for them, and re-layouts  1.15 us (2%)
    ppermute x12, waiting for transfers between devices, receive(): return lax.ppermute(array, 'blk', links)  28.8 us
    ppermute x12, starting transfers between devices, receive(): return lax.ppermute(array, 'blk', links)  19.6 us
    pallas_call x4, Pallas kernels, score(): pl.pallas_call(functools.partial(score_kernel, step, given), out_shape=[j...  11.9 us
    pallas_call x1, Pallas kernels, prepare(): pl.pallas_call(prepare_kernel, out_shape=jax.ShapeDtypeStruct((BLOCK, WID...  2.43 us
  transfers between devices with their start and end apart: 12, of which 6 were waited for; matrix products, arithmetic and copies ran while one was open for 0% of the time, Pallas kernels for 15%

profile of v1, /device:TPU:0, one launch (start us, length us, event | category | flops | bytes accessed | tf_op | source)
XLA Modules:
  0.0 64.6 jit_solution(18152057922672813017)
XLA Ops:
  0.0 2.4 %prepare.1.refs_0_ = bf16[400,1024]{1,0:T(8,128)(2,1)} custom-call(bf16[384,1024]{1,0:T(8,128)(2,1)} %embeddings.1, s32[384]{0:T(512)} %cluster.1, s32[384]{0:T(512)} %source.1), custom_call_target="tpu_custom_call" | custom-call | tf_op jit(solution)/shard_map/prepare/pallas_call | solution.py:117
  2.4 1.6 %collective-permute-start.5 = (bf16[400,1024]{1,0:T(8,128)(2,1)}, bf16[400,1024]{1,0:T(8,128)(2,1)S(1)}, u32[]{:S(2)}, u32[]{:S(2)}) collective-permute-start(bf16[400,1024]{1,0:T(8,128)(2,1)} %prepare.1.refs_0_), channel_id=1, source_target_pairs={{3,0},{0,1},{1,2},{2,3},{7,4},{4,5},{5,6},{6,7},{11,8},{8,9},{9,10... | collective-permute-start | bytes 2457608 | tf_op jit(solution)/shard_map/ppermute | solution.py:82
  4.1 4.0 %collective-permute-start = (bf16[400,1024]{1,0:T(8,128)(2,1)}, bf16[400,1024]{1,0:T(8,128)(2,1)S(1)}, u32[]{:S(2)}, u32[]{:S(2)}) collective-permute-start(bf16[400,1024]{1,0:T(8,128)(2,1)} %prepare.1.refs_0_), channel_id=1, source_target_pairs={{4,0},{5,1},{6,2},{7,3},{8,4},{9,5},{10,6},{11,7},{12,8},{13,9},{1... | collective-permute-start | bytes 2457608 | tf_op jit(solution)/shard_map/ppermute | solution.py:82
  8.1 0.0 collective-permute-start.2
  8.1 1.6 %collective-permute-start.4 = (bf16[400,1024]{1,0:T(8,128)(2,1)}, bf16[400,1024]{1,0:T(8,128)(2,1)S(1)}, u32[]{:S(2)}, u32[]{:S(2)}) collective-permute-start(bf16[400,1024]{1,0:T(8,128)(2,1)} %prepare.1.refs_0_), channel_id=1, source_target_pairs={{16,0},{17,1},{18,2},{19,3},{20,4},{21,5},{22,6},{23,7},{24,8},{25... | collective-permute-start | bytes 2457608 | tf_op jit(solution)/shard_map/ppermute | solution.py:82
  9.7 14.1 %collective-permute-done.5.refs_1_ = bf16[400,1024]{1,0:T(8,128)(2,1)S(1)} collective-permute-done((bf16[400,1024]{1,0:T(8,128)(2,1)}, bf16[400,1024]{1,0:T(8,128)(2,1)S(1)}, u32[]{:S(2)}, u32[]{:S(2)}) %collective-permute-start.5) | collective-permute-done | bytes 819232 | tf_op jit(solution)/shard_map/ppermute | solution.py:82
  23.8 1.8 %collective-permute-start.6 = (bf16[400,1024]{1,0:T(8,128)(2,1)S(1)}, bf16[400,1024]{1,0:T(8,128)(2,1)S(1)}, u32[]{:S(2)}, u32[]{:S(2)}) collective-permute-start(bf16[400,1024]{1,0:T(8,128)(2,1)S(1)} %collective-permute-done.5.refs_1_), channel_id=1, source_target_pairs={{16,0},{17,1},{18,2},{19,3},{20,4},{21,5},{22,6},{23,7},{24,8},{25... | collective-permute-start | bytes 2457608 | tf_op jit(solution)/shard_map/ppermute | solution.py:82
  25.6 0.3 collective-permute-start.7
  25.9 0.0 collective-permute-done.refs_2_.refs_1_
  25.9 4.0 %collective-permute-start.1 = (bf16[400,1024]{1,0:T(8,128)(2,1)S(1)}, bf16[400,1024]{1,0:T(8,128)(2,1)S(1)}, u32[]{:S(2)}, u32[]{:S(2)}) collective-permute-start(bf16[400,1024]{1,0:T(8,128)(2,1)S(1)} %collective-permute-done.refs_2_.refs_1_), channel_id=1, source_target_pairs={{4,0},{5,1},{6,2},{7,3},{8,4},{9,5},{10,6},{11,7},{12,8},{13,9},{1... | collective-permute-start | bytes 2457608 | tf_op jit(solution)/shard_map/ppermute | solution.py:82
  29.9 0.0 collective-permute-done.2.refs_3_.refs_2_
  29.9 0.4 collective-permute-start.3
  30.3 0.0 collective-permute-done.4.refs_4_.refs_3_.refs_1_
  30.3 1.1 %copy-done = bf16[400,1024]{1,0:T(8,128)(2,1)S(1)} copy-done((bf16[400,1024]{1,0:T(8,128)(2,1)S(1)}, bf16[400,1024]{1,0:T(8,128)(2,1)}, u32[]{:S(2)}) %copy-start) | copy-done | bytes 819224
  31.4 4.9 %score_early.1 = (f32[1,384]{1,0:T(1,128)S(1)}, f32[1,384]{1,0:T(1,128)S(1)}, f32[1,384]{1,0:T(1,128)S(1)}, f32[1,384]{1,0:T(1,128)S(1)}) custom-call(bf16[400,1024]{1,0:T(8,128)(2,1)S(1)} %copy-done, bf16[400,1024]{1,0:T(8,128)(2,1)S(1)} %collective-permute-done.5.refs_1_, bf16[400,1024]{1,0:T(8,128)(2,1)S(1)} %collective-permute-done.refs_2_.refs_1_, ...), custom_call_target="tpu_custom_call" | custom-call | flops 3321888768 | bytes 4096000 | tf_op jit(solution)/shard_map/score_early/pallas_call | solution.py:202
  36.4 9.0 %collective-permute-done.6.refs_4_.refs_0_ = bf16[400,1024]{1,0:T(8,128)(2,1)S(1)} collective-permute-done((bf16[400,1024]{1,0:T(8,128)(2,1)S(1)}, bf16[400,1024]{1,0:T(8,128)(2,1)S(1)}, u32[]{:S(2)}, u32[]{:S(2)}) %collective-permute-start.6) | collective-permute-done | bytes 819232 | tf_op jit(solution)/shard_map/ppermute | solution.py:82
  45.3 0.3 collective-permute-done.7.refs_5_
  45.6 0.0 copy-done.1
  45.6 3.6 %score_middle.1 = (f32[1,384]{1,0:T(1,128)S(1)}, f32[1,384]{1,0:T(1,128)S(1)}, f32[1,384]{1,0:T(1,128)S(1)}, f32[1,384]{1,0:T(1,128)S(1)}, f32[1,384]{1,0:T(1,128)S(1)}) custom-call(bf16[400,1024]{1,0:T(8,128)(2,1)S(1)} %copy-done.1, bf16[400,1024]{1,0:T(8,128)(2,1)S(1)} %collective-permute-done.refs_2_.refs_1_, ...), custom_call_target="tpu_custom_call" | custom-call | flops 2415919104 | bytes 4915200 | tf_op jit(solution)/shard_map/score_middle/pallas_call | solution.py:202
  49.2 0.0 collective-permute-done.1.refs_1_.refs_2_
  49.3 1.2 %collective-permute-done.3.refs_2_.refs_3_ = bf16[400,1024]{1,0:T(8,128)(2,1)S(1)} collective-permute-done((bf16[400,1024]{1,0:T(8,128)(2,1)S(1)}, bf16[400,1024]{1,0:T(8,128)(2,1)S(1)}, u32[]{:S(2)}, u32[]{:S(2)}) %collective-permute-start.3) | collective-permute-done | bytes 819232 | tf_op jit(solution)/shard_map/ppermute | solution.py:82
  50.5 2.1 %score_late.1 = (f32[1,384]{1,0:T(1,128)S(1)}, f32[1,384]{1,0:T(1,128)S(1)}) custom-call(bf16[400,1024]{1,0:T(8,128)(2,1)S(1)} %collective-permute-done.6.refs_4_.refs_0_, bf16[400,1024]{1,0:T(8,128)(2,1)S(1)} %collective-permute-done.4.refs_4_.refs_3_.refs_1_, bf16[400,1024]{1,0:T(8,128)(2,1)S(1)} %collective-permute-done.1.refs_1_.refs_2_, ...), custom_call_target="tpu_custom_call" | custom-call | flops 1207959552 | bytes 3276800 | tf_op jit(solution)/shard_map/score_late/pallas_call | solution.py:202
  52.6 5.2 %collective-permute-start.10 = (f32[1,384]{1,0:T(1,128)S(1)}, f32[1,384]{1,0:T(1,128)S(1)}, u32[]{:S(2)}, u32[]{:S(2)}) collective-permute-start(f32[1,384]{1,0:T(1,128)S(1)} %get-tuple-element.25), channel_id=1, source_target_pairs={{0,19},{1,16},{2,17},{3,18},{4,23},{5,20},{6,21},{7,22},{8,27},{9,... | collective-permute-start | bytes 4616 | tf_op jit(solution)/shard_map/ppermute | solution.py:82
  57.8 0.5 collective-permute-start.11
  58.3 0.2 collective-permute-start.8
  58.4 0.0 collective-permute-start.9
  58.4 1.3 %score_last.1 = f32[1,384]{1,0:T(1,128)S(1)} custom-call(bf16[400,1024]{1,0:T(8,128)(2,1)S(1)} %copy-done.1, bf16[400,1024]{1,0:T(8,128)(2,1)S(1)} %collective-permute-done.1.refs_1_.refs_2_, bf16[400,1024]{1,0:T(8,128)(2,1)S(1)} %collective-permute-done.3.refs_2_.refs_3_, f32[1,384]{1,0:T(1,128)S(1)} %get-tuple-element.20.refs_3_), custom_call_target="tpu_custom_call" | custom-call | flops 603979776 | bytes 2457600 | tf_op jit(solution)/shard_map/score_last/pallas_call | solution.py:202
  59.7 0.0 collective-permute-done.10
  59.7 1.6 %collective-permute-done.11 = f32[1,384]{1,0:T(1,128)S(1)} collective-permute-done((f32[1,384]{1,0:T(1,128)S(1)}, f32[1,384]{1,0:T(1,128)S(1)}, u32[]{:S(2)}, u32[]{:S(2)}) %collective-permute-start.11) | collective-permute-done | bytes 1568 | tf_op jit(solution)/shard_map/ppermute | solution.py:82
  61.4 2.6 %collective-permute-done.8 = f32[1,384]{1,0:T(1,128)S(1)} collective-permute-done((f32[1,384]{1,0:T(1,128)S(1)}, f32[1,384]{1,0:T(1,128)S(1)}, u32[]{:S(2)}, u32[]{:S(2)}) %collective-permute-start.8) | collective-permute-done | bytes 1568 | tf_op jit(solution)/shard_map/ppermute | solution.py:82
  64.0 0.0 collective-permute-done.9
  64.0 0.6 maximum_reduce_fusion
  (2 shorter events, 0.0 us)
Async XLA Ops:
  2.4 21.4 %collective-permute-start.5 = (bf16[400,1024]{1,0:T(8,128)(2,1)}, bf16[400,1024]{1,0:T(8,128)(2,1)S(1)}, u32[]{:S(2)}, u32[]{:S(2)}) collective-permute-start(bf16[400,1024]{1,0:T(8,128)(2,1)} %prepare.1.refs_0_), channel_id=1, source_target_pairs={{3,0},{0,1},{1,2},{2,3},{7,4},{4,5},{5,6},{6,7},{11,8},{8,9},{9,10... | collective-permute-start | bytes 2457608 | tf_op jit(solution)/shard_map/ppermute | solution.py:82
  4.1 21.8 %collective-permute-start = (bf16[400,1024]{1,0:T(8,128)(2,1)}, bf16[400,1024]{1,0:T(8,128)(2,1)S(1)}, u32[]{:S(2)}, u32[]{:S(2)}) collective-permute-start(bf16[400,1024]{1,0:T(8,128)(2,1)} %prepare.1.refs_0_), channel_id=1, source_target_pairs={{4,0},{5,1},{6,2},{7,3},{8,4},{9,5},{10,6},{11,7},{12,8},{13,9},{1... | collective-permute-start | bytes 2457608 | tf_op jit(solution)/shard_map/ppermute | solution.py:82
  8.1 21.8 %collective-permute-start.2 = (bf16[400,1024]{1,0:T(8,128)(2,1)}, bf16[400,1024]{1,0:T(8,128)(2,1)S(1)}, u32[]{:S(2)}, u32[]{:S(2)}) collective-permute-start(bf16[400,1024]{1,0:T(8,128)(2,1)} %prepare.1.refs_0_), channel_id=1, source_target_pairs={{13,0},{14,1},{15,2},{12,3},{1,4},{2,5},{3,6},{0,7},{5,8},{6,9},{7... | collective-permute-start | bytes 2457608 | tf_op jit(solution)/shard_map/ppermute | solution.py:82
  8.1 22.2 %collective-permute-start.4 = (bf16[400,1024]{1,0:T(8,128)(2,1)}, bf16[400,1024]{1,0:T(8,128)(2,1)S(1)}, u32[]{:S(2)}, u32[]{:S(2)}) collective-permute-start(bf16[400,1024]{1,0:T(8,128)(2,1)} %prepare.1.refs_0_), channel_id=1, source_target_pairs={{16,0},{17,1},{18,2},{19,3},{20,4},{21,5},{22,6},{23,7},{24,8},{25... | collective-permute-start | bytes 2457608 | tf_op jit(solution)/shard_map/ppermute | solution.py:82
  23.8 21.5 %collective-permute-start.6 = (bf16[400,1024]{1,0:T(8,128)(2,1)S(1)}, bf16[400,1024]{1,0:T(8,128)(2,1)S(1)}, u32[]{:S(2)}, u32[]{:S(2)}) collective-permute-start(bf16[400,1024]{1,0:T(8,128)(2,1)S(1)} %collective-permute-done.5.refs_1_), channel_id=1, source_target_pairs={{16,0},{17,1},{18,2},{19,3},{20,4},{21,5},{22,6},{23,7},{24,8},{25... | collective-permute-start | bytes 2457608 | tf_op jit(solution)/shard_map/ppermute | solution.py:82
  25.6 20.0 %collective-permute-start.7 = (bf16[400,1024]{1,0:T(8,128)(2,1)S(1)}, bf16[400,1024]{1,0:T(8,128)(2,1)S(1)}, u32[]{:S(2)}, u32[]{:S(2)}) collective-permute-start(bf16[400,1024]{1,0:T(8,128)(2,1)S(1)} %collective-permute-done.5.refs_1_), channel_id=1, source_target_pairs={{3,0},{0,1},{1,2},{2,3},{7,4},{4,5},{5,6},{6,7},{11,8},{8,9},{9,10... | collective-permute-start | bytes 2457608 | tf_op jit(solution)/shard_map/ppermute | solution.py:82
  25.9 23.4 %collective-permute-start.1 = (bf16[400,1024]{1,0:T(8,128)(2,1)S(1)}, bf16[400,1024]{1,0:T(8,128)(2,1)S(1)}, u32[]{:S(2)}, u32[]{:S(2)}) collective-permute-start(bf16[400,1024]{1,0:T(8,128)(2,1)S(1)} %collective-permute-done.refs_2_.refs_1_), channel_id=1, source_target_pairs={{4,0},{5,1},{6,2},{7,3},{8,4},{9,5},{10,6},{11,7},{12,8},{13,9},{1... | collective-permute-start | bytes 2457608 | tf_op jit(solution)/shard_map/ppermute | solution.py:82
  29.9 20.6 %collective-permute-start.3 = (bf16[400,1024]{1,0:T(8,128)(2,1)S(1)}, bf16[400,1024]{1,0:T(8,128)(2,1)S(1)}, u32[]{:S(2)}, u32[]{:S(2)}) collective-permute-start(bf16[400,1024]{1,0:T(8,128)(2,1)S(1)} %collective-permute-done.2.refs_3_.refs_2_), channel_id=1, source_target_pairs={{13,0},{14,1},{15,2},{12,3},{1,4},{2,5},{3,6},{0,7},{5,8},{6,9},{7... | collective-permute-start | bytes 2457608 | tf_op jit(solution)/shard_map/ppermute | solution.py:82
  30.3 1.1 %copy-start = (bf16[400,1024]{1,0:T(8,128)(2,1)S(1)}, bf16[400,1024]{1,0:T(8,128)(2,1)}, u32[]{:S(2)}) copy-start(bf16[400,1024]{1,0:T(8,128)(2,1)} %prepare.1.refs_0_) | copy-start | bytes 2457604
  31.4 14.2 %copy-start.1 = (bf16[400,1024]{1,0:T(8,128)(2,1)S(1)}, bf16[400,1024]{1,0:T(8,128)(2,1)}, u32[]{:S(2)}) copy-start(bf16[400,1024]{1,0:T(8,128)(2,1)} %prepare.1.refs_0_) | copy-start | bytes 2457604
  52.6 7.2 %collective-permute-start.10 = (f32[1,384]{1,0:T(1,128)S(1)}, f32[1,384]{1,0:T(1,128)S(1)}, u32[]{:S(2)}, u32[]{:S(2)}) collective-permute-start(f32[1,384]{1,0:T(1,128)S(1)} %get-tuple-element.25), channel_id=1, source_target_pairs={{0,19},{1,16},{2,17},{3,18},{4,23},{5,20},{6,21},{7,22},{8,27},{9,... | collective-permute-start | bytes 4616 | tf_op jit(solution)/shard_map/ppermute | solution.py:82
  57.8 3.6 %collective-permute-start.11 = (f32[1,384]{1,0:T(1,128)S(1)}, f32[1,384]{1,0:T(1,128)S(1)}, u32[]{:S(2)}, u32[]{:S(2)}) collective-permute-start(f32[1,384]{1,0:T(1,128)S(1)} %get-tuple-element.26), channel_id=1, source_target_pairs={{0,16},{1,17},{2,18},{3,19},{4,20},{5,21},{6,22},{7,23},{8,24},{9,... | collective-permute-start | bytes 4616 | tf_op jit(solution)/shard_map/ppermute | solution.py:82
  58.3 5.7 %collective-permute-start.8 = (f32[1,384]{1,0:T(1,128)S(1)}, f32[1,384]{1,0:T(1,128)S(1)}, u32[]{:S(2)}, u32[]{:S(2)}) collective-permute-start(f32[1,384]{1,0:T(1,128)S(1)} %get-tuple-element.21), channel_id=1, source_target_pairs={{0,13},{1,14},{2,15},{3,12},{4,1},{5,2},{6,3},{7,0},{8,5},{9,6},{1... | collective-permute-start | bytes 4616 | tf_op jit(solution)/shard_map/ppermute | solution.py:82
  58.4 5.5 %collective-permute-start.9 = (f32[1,384]{1,0:T(1,128)S(1)}, f32[1,384]{1,0:T(1,128)S(1)}, u32[]{:S(2)}, u32[]{:S(2)}) collective-permute-start(f32[1,384]{1,0:T(1,128)S(1)} %get-tuple-element.22), channel_id=1, source_target_pairs={{0,4},{1,5},{2,6},{3,7},{4,8},{5,9},{6,10},{7,11},{8,12},{9,13},{1... | collective-permute-start | bytes 4616 | tf_op jit(solution)/shard_map/ppermute | solution.py:82

commit v2 on v1

--- a/solution.py
+++ b/solution.py
@@ -32,7 +32,8 @@
         (0, 1, 2, 3, 4),
         ((0, 0, 0, 4, (0, 2, 3)), (1, 1, 2, 4, (2, 3, 4)), (2, 2, 3, 4, (2, 3, 4)), (3, 3, 4, 4, (3, 4))),
     ),
-    "middle": ((0, 2, 3, 4, 8, 5), ((4, 4, 0, 3, (2, 3, 8)), (5, 5, 0, 3, (0, 2, 3, 4)))),
+    "middle": ((5, 0, 2, 3, 4), ((0, 0, 1, 4, (0, 2, 3, 4)),)),
+    "second": ((8, 0, 2, 3, 4), ((0, 0, 1, 4, (2, 3, 8)),)),
     "late": ((8, 4, 6, 7), ((0, 1, 2, 3, (4, 8)),)),
     "last": ((0, 6, 7), ((0, 0, 1, 2, (0,)),)),
 }
@@ -82,7 +83,13 @@
     return lax.ppermute(array, "blk", links)
 
 
-def prepare_kernel(embeddings, cluster, source, out, raw, clusters, sources, unit, sems):
+def unit_rows(rows):
+    widened = rows.astype(jnp.float32)
+    factor = lax.rsqrt(jnp.mean(widened * widened, axis=1, keepdims=True) + 1e-06) / 32.0
+    return (widened * factor).astype(jnp.bfloat16)
+
+
+def prepare_kernel(embeddings, cluster, source, out, out_tail, raw, clusters, sources, unit, sems):
     def copy(source_rows, target_rows, sem):
         return pltpu.make_async_copy(source_rows, target_rows, sems.at[sem])
 
@@ -91,6 +98,7 @@
     arriving = [copy(embeddings.at[rows], raw.at[rows], i) for i, rows in enumerate(stripes)]
     leaving = [copy(unit.at[rows], out.at[rows], STRIPES + i) for i, rows in enumerate(stripes)]
     leaving.append(copy(unit.at[ROWS:], out.at[ROWS:], 2 * STRIPES + 2))
+    leaving.append(copy(unit.at[ROWS:], out_tail, 2 * STRIPES + 3))
     for move in ids + arriving:
         move.start()
     for move in ids:
@@ -102,11 +110,10 @@
     unit[ROWS:, :ROWS] = tail.astype(jnp.float32).astype(jnp.bfloat16)
     unit[ROWS:, ROWS:] = jnp.zeros((TAIL, WIDTH - ROWS), jnp.bfloat16)
     leaving[STRIPES].start()
+    leaving[STRIPES + 1].start()
     for i, rows in enumerate(stripes):
         arriving[i].wait()
-        widened = raw[rows, :].astype(jnp.float32)
-        factor = lax.rsqrt(jnp.mean(widened * widened, axis=1, keepdims=True) + 1e-06) / 32.0
-        unit[rows, :] = (widened * factor).astype(jnp.bfloat16)
+        unit[rows, :] = unit_rows(raw[rows, :])
         leaving[i].start()
     for move in leaving:
         move.wait()
@@ -116,19 +123,38 @@
     far = pl.BlockSpec(memory_space=pltpu.HBM)
     return pl.pallas_call(
         prepare_kernel,
-        out_shape=jax.ShapeDtypeStruct((BLOCK, WIDTH), jnp.bfloat16),
+        out_shape=[jax.ShapeDtypeStruct((rows, WIDTH), jnp.bfloat16) for rows in (BLOCK, TAIL)],
         in_specs=[far] * 3,
-        out_specs=far,
+        out_specs=[far] * 2,
         scratch_shapes=[
             pltpu.VMEM((ROWS, WIDTH), jnp.bfloat16),
             pltpu.VMEM((ROWS,), jnp.int32),
             pltpu.VMEM((ROWS,), jnp.int32),
             pltpu.VMEM((BLOCK, WIDTH), jnp.bfloat16),
-            pltpu.SemaphoreType.DMA((2 * STRIPES + 3,)),
+            pltpu.SemaphoreType.DMA((2 * STRIPES + 4,)),
         ],
         compiler_params=pltpu.CompilerParams(vmem_limit_bytes=60 << 20),
         name="prepare",
     )(embeddings, cluster_id, source_id)
+
+
+def join_kernel(raw, tail, out):
+    for i in range(STRIPES):
+        rows = slice(i * STRIPE, (i + 1) * STRIPE)
+        out[rows, :] = unit_rows(raw[rows, :])
+    out[ROWS:, :] = tail[...]
+
+
+def join(raw, tail):
+    vmem = pl.BlockSpec(memory_space=pltpu.VMEM)
+    return pl.pallas_call(
+        join_kernel,
+        out_shape=jax.ShapeDtypeStruct((BLOCK, WIDTH), jnp.bfloat16),
+        in_specs=[vmem] * 2,
+        out_specs=vmem,
+        compiler_params=pltpu.CompilerParams(vmem_limit_bytes=16 << 20),
+        name="join",
+    )(raw, tail)
 
 
 def score_kernel(step, given, *refs):
@@ -219,13 +245,18 @@
 
 
 def local(embeddings, cluster_id, source_id):
-    blocks = {0: prepare(embeddings, cluster_id, source_id)}
+    whole, tail = prepare(embeddings, cluster_id, source_id)
+    blocks = {0: whole}
     for block, by in FIRST:
-        blocks[block] = receive(blocks[0], by)
+        if block == 1:
+            blocks[block] = join(receive(embeddings, by), receive(tail, by))
+        else:
+            blocks[block] = receive(whole, by)
     for block, parent, by in SECOND:
         blocks[block] = receive(blocks[parent], by)
     best = score("early", blocks, {})
     best = score("middle", blocks, best)
+    best = score("second", blocks, best)
     got = [receive(best[b], OFFSETS[b], back=True) for b in (3, 2)]
     best = score("late", blocks, best)
     got += [receive(best[b], OFFSETS[b], back=True) for b in (8, 4)]

time: 64.7 us -> 60.9 us (0.941)
  waiting for transfers between devices: 28.8 us -> 22 us
  starting transfers between devices: 19.6 us -> 22.6 us
  local copies, waits for them, and re-layouts: 1.15 us -> 0.01 us
  Pallas kernels: 14.3 us -> 15.4 us
    ppermute x12 -> x13, waiting for transfers between devices: 28.8 us -> 22 us  [receive(): return lax.ppermute(array, 'blk', links)]
    ppermute x12 -> x13, starting transfers between devices: 19.6 us -> 22.6 us  [receive(): return lax.ppermute(array, 'blk', links)]
    unnamed x4 -> x2, local copies, waits for them, and re-layouts: 1.15 us -> 0.01 us
    pallas_call x4 -> x5, Pallas kernels: 11.9 us -> 12.7 us  [score(): pl.pallas_call(functools.partial(score_kernel, step, given), out_shape=[j...]
    pallas_call x1 -> x2, Pallas kernels: 2.43 us -> 2.7 us  [the longest x1 2.45 us: prepare(): pl.pallas_call(prepare_kernel, out_shape=[jax.ShapeDtypeStruct((rows, WID...]
  transfers between devices with their start and end apart: 12 -> 13, of which waited for: 6 -> 5; matrix products, arithmetic and copies ran while one was open for 0% -> 0% of each run, Pallas kernels for 15% -> 25%
where the time goes in v2:
time: 60.9 us; the launch traced here: 60.8 us
  starting transfers between devices  22.6 us (37%)
  waiting for transfers between devices  22 us (36%)
  Pallas kernels  15.4 us (25%)
    ppermute x13, starting transfers between devices, receive(): return lax.ppermute(array, 'blk', links)  22.6 us
    ppermute x13, waiting for transfers between devices, receive(): return lax.ppermute(array, 'blk', links)  22 us
    pallas_call x5, Pallas kernels, score(): pl.pallas_call(functools.partial(score_kernel, step, given), out_shape=[j...  12.7 us
    pallas_call x1, Pallas kernels, prepare(): pl.pallas_call(prepare_kernel, out_shape=[jax.ShapeDtypeStruct((rows, WID...  2.45 us
  transfers between devices with their start and end apart: 13, of which 5 were waited for; matrix products, arithmetic and copies ran while one was open for 0% of the time, Pallas kernels for 25%

profile of v2, /device:TPU:0, one launch (start us, length us, event | category | flops | bytes accessed | tf_op | source)
XLA Modules:
  0.0 60.8 jit_solution(9899972846254765993)
XLA Ops:
  0.0 1.6 %collective-permute-start.4 = (bf16[384,1024]{1,0:T(8,128)(2,1)}, bf16[384,1024]{1,0:T(8,128)(2,1)S(1)}, u32[]{:S(2)}, u32[]{:S(2)}) collective-permute-start(bf16[384,1024]{1,0:T(8,128)(2,1)} %embeddings.1), channel_id=1, source_target_pairs={{3,0},{0,1},{1,2},{2,3},{7,4},{4,5},{5,6},{6,7},{11,8},{8,9},{9,10... | collective-permute-start | bytes 2359304 | tf_op jit(solution)/shard_map/ppermute | solution.py:83
  1.6 2.4 %prepare.1 = (bf16[400,1024]{1,0:T(8,128)(2,1)}, bf16[16,1024]{1,0:T(8,128)(2,1)}) custom-call(bf16[384,1024]{1,0:T(8,128)(2,1)} %embeddings.1, s32[384]{0:T(512)} %cluster.1, s32[384]{0:T(512)} %source.1), custom_call_target="tpu_custom_call" | custom-call | tf_op jit(solution)/shard_map/prepare/pallas_call | solution.py:124
  4.0 3.2 %collective-permute-start.2 = (bf16[400,1024]{1,0:T(8,128)(2,1)}, bf16[400,1024]{1,0:T(8,128)(2,1)S(1)}, u32[]{:S(2)}, u32[]{:S(2)}) collective-permute-start(bf16[400,1024]{1,0:T(8,128)(2,1)} %get-tuple-element.20.refs_0_.refs_1_), channel_id=1, source_target_pairs={{13,0},{14,1},{15,2},{12,3},{1,4},{2,5},{3,6},{0,7},{5,8},{6,9},{7... | collective-permute-start | bytes 2457608 | tf_op jit(solution)/shard_map/ppermute | solution.py:83
  7.2 1.2 %collective-permute-start = (bf16[400,1024]{1,0:T(8,128)(2,1)}, bf16[400,1024]{1,0:T(8,128)(2,1)S(1)}, u32[]{:S(2)}, u32[]{:S(2)}) collective-permute-start(bf16[400,1024]{1,0:T(8,128)(2,1)} %get-tuple-element.20.refs_0_.refs_1_), channel_id=1, source_target_pairs={{4,0},{5,1},{6,2},{7,3},{8,4},{9,5},{10,6},{11,7},{12,8},{13,9},{1... | collective-permute-start | bytes 2457608 | tf_op jit(solution)/shard_map/ppermute | solution.py:83
  8.4 1.7 %collective-permute-start.7 = (bf16[400,1024]{1,0:T(8,128)(2,1)}, bf16[400,1024]{1,0:T(8,128)(2,1)S(1)}, u32[]{:S(2)}, u32[]{:S(2)}) collective-permute-start(bf16[400,1024]{1,0:T(8,128)(2,1)} %get-tuple-element.20.refs_0_.refs_1_), channel_id=1, source_target_pairs={{16,0},{17,1},{18,2},{19,3},{20,4},{21,5},{22,6},{23,7},{24,8},{25... | collective-permute-start | bytes 2457608 | tf_op jit(solution)/shard_map/ppermute | solution.py:83
  10.1 1.2 %collective-permute-start.5 = (bf16[16,1024]{1,0:T(8,128)(2,1)}, bf16[16,1024]{1,0:T(8,128)(2,1)S(1)}, u32[]{:S(2)}, u32[]{:S(2)}) collective-permute-start(bf16[16,1024]{1,0:T(8,128)(2,1)} %get-tuple-element.21), channel_id=1, source_target_pairs={{3,0},{0,1},{1,2},{2,3},{7,4},{4,5},{5,6},{6,7},{11,8},{8,9},{9,10... | collective-permute-start | bytes 98312 | tf_op jit(solution)/shard_map/ppermute | solution.py:83
  11.3 10.0 %collective-permute-done.5.tail = bf16[16,1024]{1,0:T(8,128)(2,1)S(1)} collective-permute-done((bf16[16,1024]{1,0:T(8,128)(2,1)}, bf16[16,1024]{1,0:T(8,128)(2,1)S(1)}, u32[]{:S(2)}, u32[]{:S(2)}) %collective-permute-start.5) | collective-permute-done | bytes 32800 | tf_op jit(solution)/shard_map/ppermute | solution.py:83
  21.3 0.0 collective-permute-done.4.raw
  21.3 0.2 join.1.refs_1_
  21.6 0.5 collective-permute-start.6
  22.1 1.6 %collective-permute-start.8 = (bf16[400,1024]{1,0:T(8,128)(2,1)S(1)}, bf16[400,1024]{1,0:T(8,128)(2,1)S(1)}, u32[]{:S(2)}, u32[]{:S(2)}) collective-permute-start(bf16[400,1024]{1,0:T(8,128)(2,1)S(1)} %join.1.refs_1_), channel_id=1, source_target_pairs={{16,0},{17,1},{18,2},{19,3},{20,4},{21,5},{22,6},{23,7},{24,8},{25... | collective-permute-start | bytes 2457608 | tf_op jit(solution)/shard_map/ppermute | solution.py:83
  23.7 3.6 %collective-permute-done.2.refs_3_ = bf16[400,1024]{1,0:T(8,128)(2,1)S(1)} collective-permute-done((bf16[400,1024]{1,0:T(8,128)(2,1)}, bf16[400,1024]{1,0:T(8,128)(2,1)S(1)}, u32[]{:S(2)}, u32[]{:S(2)}) %collective-permute-start.2) | collective-permute-done | bytes 819232 | tf_op jit(solution)/shard_map/ppermute | solution.py:83
  27.2 2.0 %collective-permute-start.3 = (bf16[400,1024]{1,0:T(8,128)(2,1)S(1)}, bf16[400,1024]{1,0:T(8,128)(2,1)S(1)}, u32[]{:S(2)}, u32[]{:S(2)}) collective-permute-start(bf16[400,1024]{1,0:T(8,128)(2,1)S(1)} %collective-permute-done.2.refs_3_), channel_id=1, source_target_pairs={{13,0},{14,1},{15,2},{12,3},{1,4},{2,5},{3,6},{0,7},{5,8},{6,9},{7... | collective-permute-start | bytes 2457608 | tf_op jit(solution)/shard_map/ppermute | solution.py:83
  29.2 0.0 collective-permute-done.refs_2_
  29.2 2.4 %collective-permute-start.1 = (bf16[400,1024]{1,0:T(8,128)(2,1)S(1)}, bf16[400,1024]{1,0:T(8,128)(2,1)S(1)}, u32[]{:S(2)}, u32[]{:S(2)}) collective-permute-start(bf16[400,1024]{1,0:T(8,128)(2,1)S(1)} %collective-permute-done.refs_2_), channel_id=1, source_target_pairs={{4,0},{5,1},{6,2},{7,3},{8,4},{9,5},{10,6},{11,7},{12,8},{13,9},{1... | collective-permute-start | bytes 2457608 | tf_op jit(solution)/shard_map/ppermute | solution.py:83
  31.7 0.0 collective-permute-done.7.refs_4_.refs_1_
  31.7 4.9 %score_early.1 = (f32[1,384]{1,0:T(1,128)S(1)}, f32[1,384]{1,0:T(1,128)S(1)}, f32[1,384]{1,0:T(1,128)S(1)}, f32[1,384]{1,0:T(1,128)S(1)}) custom-call(bf16[400,1024]{1,0:T(8,128)(2,1)S(1)} %copy-done, bf16[400,1024]{1,0:T(8,128)(2,1)S(1)} %join.1.refs_1_, bf16[400,1024]{1,0:T(8,128)(2,1)S(1)} %collective-permute-done.refs_2_, ...), custom_call_target="tpu_custom_call" | custom-call | flops 3321888768 | bytes 4096000 | tf_op jit(solution)/shard_map/score_early/pallas_call | solution.py:228
  36.6 5.2 %collective-permute-done.6.refs_0_ = bf16[400,1024]{1,0:T(8,128)(2,1)S(1)} collective-permute-done((bf16[400,1024]{1,0:T(8,128)(2,1)S(1)}, bf16[400,1024]{1,0:T(8,128)(2,1)S(1)}, u32[]{:S(2)}, u32[]{:S(2)}) %collective-permute-start.6) | collective-permute-done | bytes 819232 | tf_op jit(solution)/shard_map/ppermute | solution.py:83
  41.8 2.1 %score_middle.1 = (f32[1,384]{1,0:T(1,128)S(1)}, f32[1,384]{1,0:T(1,128)S(1)}, f32[1,384]{1,0:T(1,128)S(1)}, f32[1,384]{1,0:T(1,128)S(1)}) custom-call(bf16[400,1024]{1,0:T(8,128)(2,1)S(1)} %collective-permute-done.6.refs_0_, bf16[400,1024]{1,0:T(8,128)(2,1)S(1)} %copy-done, bf16[400,1024]{1,0:T(8,128)(2,1)S(1)} %collective-permute-done.refs_2_, ...), custom_call_target="tpu_custom_call" | custom-call | flops 1207959552 | bytes 4096000 | tf_op jit(solution)/shard_map/score_middle/pallas_call | solution.py:228
  44.0 1.4 %collective-permute-done.8.refs_0_ = bf16[400,1024]{1,0:T(8,128)(2,1)S(1)} collective-permute-done((bf16[400,1024]{1,0:T(8,128)(2,1)S(1)}, bf16[400,1024]{1,0:T(8,128)(2,1)S(1)}, u32[]{:S(2)}, u32[]{:S(2)}) %collective-permute-start.8) | collective-permute-done | bytes 819232 | tf_op jit(solution)/shard_map/ppermute | solution.py:83
  45.4 2.2 %score_second.1 = (f32[1,384]{1,0:T(1,128)S(1)}, f32[1,384]{1,0:T(1,128)S(1)}, f32[1,384]{1,0:T(1,128)S(1)}) custom-call(bf16[400,1024]{1,0:T(8,128)(2,1)S(1)} %collective-permute-done.8.refs_0_, bf16[400,1024]{1,0:T(8,128)(2,1)S(1)} %copy-done, bf16[400,1024]{1,0:T(8,128)(2,1)S(1)} %collective-permute-done.refs_2_, ...), custom_call_target="tpu_custom_call" | custom-call | flops 1207959552 | bytes 4096000 | tf_op jit(solution)/shard_map/score_second/pallas_call | solution.py:228
  47.7 2.6 %collective-permute-start.9 = (f32[1,384]{1,0:T(1,128)S(1)}, f32[1,384]{1,0:T(1,128)S(1)}, u32[]{:S(2)}, u32[]{:S(2)}) collective-permute-start(f32[1,384]{1,0:T(1,128)S(1)} %get-tuple-element.29), channel_id=1, source_target_pairs={{0,13},{1,14},{2,15},{3,12},{4,1},{5,2},{6,3},{7,0},{8,5},{9,6},{1... | collective-permute-start | bytes 4616 | tf_op jit(solution)/shard_map/ppermute | solution.py:83
  50.3 0.4 collective-permute-start.10
  50.7 0.0 collective-permute-done.3.refs_2_.refs_3_
  50.7 2.1 %score_late.1 = (f32[1,384]{1,0:T(1,128)S(1)}, f32[1,384]{1,0:T(1,128)S(1)}) custom-call(bf16[400,1024]{1,0:T(8,128)(2,1)S(1)} %collective-permute-done.8.refs_0_, bf16[400,1024]{1,0:T(8,128)(2,1)S(1)} %collective-permute-done.7.refs_4_.refs_1_, bf16[400,1024]{1,0:T(8,128)(2,1)S(1)} %collective-permute-done.1.refs_1_.refs_2_, ...), custom_call_target="tpu_custom_call" | custom-call | flops 1207959552 | bytes 3276800 | tf_op jit(solution)/shard_map/score_late/pallas_call | solution.py:228
  52.8 3.8 %collective-permute-start.11 = (f32[1,384]{1,0:T(1,128)S(1)}, f32[1,384]{1,0:T(1,128)S(1)}, u32[]{:S(2)}, u32[]{:S(2)}) collective-permute-start(f32[1,384]{1,0:T(1,128)S(1)} %get-tuple-element.33), channel_id=1, source_target_pairs={{0,19},{1,16},{2,17},{3,18},{4,23},{5,20},{6,21},{7,22},{8,27},{9,... | collective-permute-start | bytes 4616 | tf_op jit(solution)/shard_map/ppermute | solution.py:83
  56.6 0.5 collective-permute-start.12
  57.0 1.3 %score_last.1 = f32[1,384]{1,0:T(1,128)S(1)} custom-call(bf16[400,1024]{1,0:T(8,128)(2,1)S(1)} %copy-done, bf16[400,1024]{1,0:T(8,128)(2,1)S(1)} %collective-permute-done.1.refs_1_.refs_2_, bf16[400,1024]{1,0:T(8,128)(2,1)S(1)} %collective-permute-done.3.refs_2_.refs_3_, f32[1,384]{1,0:T(1,128)S(1)} %get-tuple-element.26.refs_3_), custom_call_target="tpu_custom_call" | custom-call | flops 603979776 | bytes 2457600 | tf_op jit(solution)/shard_map/score_last/pallas_call | solution.py:228
  58.3 0.0 collective-permute-done.10
  58.4 0.0 collective-permute-done.11
  58.4 1.8 %collective-permute-done.12 = f32[1,384]{1,0:T(1,128)S(1)} collective-permute-done((f32[1,384]{1,0:T(1,128)S(1)}, f32[1,384]{1,0:T(1,128)S(1)}, u32[]{:S(2)}, u32[]{:S(2)}) %collective-permute-start.12) | collective-permute-done | bytes 1568 | tf_op jit(solution)/shard_map/ppermute | solution.py:83
  60.2 0.6 maximum_reduce_fusion
  (4 shorter events, 0.0 us)
Async XLA Ops:
  0.0 21.3 %collective-permute-start.4 = (bf16[384,1024]{1,0:T(8,128)(2,1)}, bf16[384,1024]{1,0:T(8,128)(2,1)S(1)}, u32[]{:S(2)}, u32[]{:S(2)}) collective-permute-start(bf16[384,1024]{1,0:T(8,128)(2,1)} %embeddings.1), channel_id=1, source_target_pairs={{3,0},{0,1},{1,2},{2,3},{7,4},{4,5},{5,6},{6,7},{11,8},{8,9},{9,10... | collective-permute-start | bytes 2359304 | tf_op jit(solution)/shard_map/ppermute | solution.py:83
  4.0 23.2 %collective-permute-start.2 = (bf16[400,1024]{1,0:T(8,128)(2,1)}, bf16[400,1024]{1,0:T(8,128)(2,1)S(1)}, u32[]{:S(2)}, u32[]{:S(2)}) collective-permute-start(bf16[400,1024]{1,0:T(8,128)(2,1)} %get-tuple-element.20.refs_0_.refs_1_), channel_id=1, source_target_pairs={{13,0},{14,1},{15,2},{12,3},{1,4},{2,5},{3,6},{0,7},{5,8},{6,9},{7... | collective-permute-start | bytes 2457608 | tf_op jit(solution)/shard_map/ppermute | solution.py:83
  7.2 22.0 %collective-permute-start = (bf16[400,1024]{1,0:T(8,128)(2,1)}, bf16[400,1024]{1,0:T(8,128)(2,1)S(1)}, u32[]{:S(2)}, u32[]{:S(2)}) collective-permute-start(bf16[400,1024]{1,0:T(8,128)(2,1)} %get-tuple-element.20.refs_0_.refs_1_), channel_id=1, source_target_pairs={{4,0},{5,1},{6,2},{7,3},{8,4},{9,5},{10,6},{11,7},{12,8},{13,9},{1... | collective-permute-start | bytes 2457608 | tf_op jit(solution)/shard_map/ppermute | solution.py:83
  8.4 23.2 %collective-permute-start.7 = (bf16[400,1024]{1,0:T(8,128)(2,1)}, bf16[400,1024]{1,0:T(8,128)(2,1)S(1)}, u32[]{:S(2)}, u32[]{:S(2)}) collective-permute-start(bf16[400,1024]{1,0:T(8,128)(2,1)} %get-tuple-element.20.refs_0_.refs_1_), channel_id=1, source_target_pairs={{16,0},{17,1},{18,2},{19,3},{20,4},{21,5},{22,6},{23,7},{24,8},{25... | collective-permute-start | bytes 2457608 | tf_op jit(solution)/shard_map/ppermute | solution.py:83
  10.1 21.6 %copy-start = (bf16[400,1024]{1,0:T(8,128)(2,1)S(1)}, bf16[400,1024]{1,0:T(8,128)(2,1)}, u32[]{:S(2)}) copy-start(bf16[400,1024]{1,0:T(8,128)(2,1)} %get-tuple-element.20.refs_0_.refs_1_) | copy-start | bytes 2457604
  10.1 11.2 %collective-permute-start.5 = (bf16[16,1024]{1,0:T(8,128)(2,1)}, bf16[16,1024]{1,0:T(8,128)(2,1)S(1)}, u32[]{:S(2)}, u32[]{:S(2)}) collective-permute-start(bf16[16,1024]{1,0:T(8,128)(2,1)} %get-tuple-element.21), channel_id=1, source_target_pairs={{3,0},{0,1},{1,2},{2,3},{7,4},{4,5},{5,6},{6,7},{11,8},{8,9},{9,10... | collective-permute-start | bytes 98312 | tf_op jit(solution)/shard_map/ppermute | solution.py:83
  21.6 20.3 %collective-permute-start.6 = (bf16[400,1024]{1,0:T(8,128)(2,1)S(1)}, bf16[400,1024]{1,0:T(8,128)(2,1)S(1)}, u32[]{:S(2)}, u32[]{:S(2)}) collective-permute-start(bf16[400,1024]{1,0:T(8,128)(2,1)S(1)} %join.1.refs_1_), channel_id=1, source_target_pairs={{3,0},{0,1},{1,2},{2,3},{7,4},{4,5},{5,6},{6,7},{11,8},{8,9},{9,10... | collective-permute-start | bytes 2457608 | tf_op jit(solution)/shard_map/ppermute | solution.py:83
  22.1 23.3 %collective-permute-start.8 = (bf16[400,1024]{1,0:T(8,128)(2,1)S(1)}, bf16[400,1024]{1,0:T(8,128)(2,1)S(1)}, u32[]{:S(2)}, u32[]{:S(2)}) collective-permute-start(bf16[400,1024]{1,0:T(8,128)(2,1)S(1)} %join.1.refs_1_), channel_id=1, source_target_pairs={{16,0},{17,1},{18,2},{19,3},{20,4},{21,5},{22,6},{23,7},{24,8},{25... | collective-permute-start | bytes 2457608 | tf_op jit(solution)/shard_map/ppermute | solution.py:83
  27.2 23.4 %collective-permute-start.3 = (bf16[400,1024]{1,0:T(8,128)(2,1)S(1)}, bf16[400,1024]{1,0:T(8,128)(2,1)S(1)}, u32[]{:S(2)}, u32[]{:S(2)}) collective-permute-start(bf16[400,1024]{1,0:T(8,128)(2,1)S(1)} %collective-permute-done.2.refs_3_), channel_id=1, source_target_pairs={{13,0},{14,1},{15,2},{12,3},{1,4},{2,5},{3,6},{0,7},{5,8},{6,9},{7... | collective-permute-start | bytes 2457608 | tf_op jit(solution)/shard_map/ppermute | solution.py:83
  29.2 21.5 %collective-permute-start.1 = (bf16[400,1024]{1,0:T(8,128)(2,1)S(1)}, bf16[400,1024]{1,0:T(8,128)(2,1)S(1)}, u32[]{:S(2)}, u32[]{:S(2)}) collective-permute-start(bf16[400,1024]{1,0:T(8,128)(2,1)S(1)} %collective-permute-done.refs_2_), channel_id=1, source_target_pairs={{4,0},{5,1},{6,2},{7,3},{8,4},{9,5},{10,6},{11,7},{12,8},{13,9},{1... | collective-permute-start | bytes 2457608 | tf_op jit(solution)/shard_map/ppermute | solution.py:83
  47.7 10.7 %collective-permute-start.9 = (f32[1,384]{1,0:T(1,128)S(1)}, f32[1,384]{1,0:T(1,128)S(1)}, u32[]{:S(2)}, u32[]{:S(2)}) collective-permute-start(f32[1,384]{1,0:T(1,128)S(1)} %get-tuple-element.29), channel_id=1, source_target_pairs={{0,13},{1,14},{2,15},{3,12},{4,1},{5,2},{6,3},{7,0},{8,5},{9,6},{1... | collective-permute-start | bytes 4616 | tf_op jit(solution)/shard_map/ppermute | solution.py:83
  50.3 8.1 %collective-permute-start.10 = (f32[1,384]{1,0:T(1,128)S(1)}, f32[1,384]{1,0:T(1,128)S(1)}, u32[]{:S(2)}, u32[]{:S(2)}) collective-permute-start(f32[1,384]{1,0:T(1,128)S(1)} %get-tuple-element.30), channel_id=1, source_target_pairs={{0,4},{1,5},{2,6},{3,7},{4,8},{5,9},{6,10},{7,11},{8,12},{9,13},{1... | collective-permute-start | bytes 4616 | tf_op jit(solution)/shard_map/ppermute | solution.py:83
  52.8 5.6 %collective-permute-start.11 = (f32[1,384]{1,0:T(1,128)S(1)}, f32[1,384]{1,0:T(1,128)S(1)}, u32[]{:S(2)}, u32[]{:S(2)}) collective-permute-start(f32[1,384]{1,0:T(1,128)S(1)} %get-tuple-element.33), channel_id=1, source_target_pairs={{0,19},{1,16},{2,17},{3,18},{4,23},{5,20},{6,21},{7,22},{8,27},{9,... | collective-permute-start | bytes 4616 | tf_op jit(solution)/shard_map/ppermute | solution.py:83
  56.6 3.6 %collective-permute-start.12 = (f32[1,384]{1,0:T(1,128)S(1)}, f32[1,384]{1,0:T(1,128)S(1)}, u32[]{:S(2)}, u32[]{:S(2)}) collective-permute-start(f32[1,384]{1,0:T(1,128)S(1)} %get-tuple-element.34), channel_id=1, source_target_pairs={{0,16},{1,17},{2,18},{3,19},{4,20},{5,21},{6,22},{7,23},{8,24},{9,... | collective-permute-start | bytes 4616 | tf_op jit(solution)/shard_map/ppermute | solution.py:83

commit v3 on v2

--- a/solution.py
+++ b/solution.py
@@ -25,17 +25,19 @@
 TAIL = 16
 BLOCK = ROWS + TAIL
 WIDTH = 1024
-STRIPE = 64
+STRIPE = 128
 STRIPES = ROWS // STRIPE
+PACKED = (1, 0, 2, 3, 4)
 STEPS = {
     "early": (
-        (0, 1, 2, 3, 4),
-        ((0, 0, 0, 4, (0, 2, 3)), (1, 1, 2, 4, (2, 3, 4)), (2, 2, 3, 4, (2, 3, 4)), (3, 3, 4, 4, (3, 4))),
+        (),
+        PACKED,
+        ((0, PACKED, (0, 2, 3)), (1, (2, 3, 4), (2, 3, 4)), (2, (3, 4), (2, 3, 4)), (3, (4,), (3, 4))),
     ),
-    "middle": ((5, 0, 2, 3, 4), ((0, 0, 1, 4, (0, 2, 3, 4)),)),
-    "second": ((8, 0, 2, 3, 4), ((0, 0, 1, 4, (2, 3, 8)),)),
-    "late": ((8, 4, 6, 7), ((0, 1, 2, 3, (4, 8)),)),
-    "last": ((0, 6, 7), ((0, 0, 1, 2, (0,)),)),
+    "middle": ((5,), (), ((5, (2, 3, 4), (2, 3, 4)),)),
+    "second": ((8,), (), ((8, (0, 2, 3, 4), (2, 3, 8)),)),
+    "late": ((8,), (7, 6), ((8, (7, 6), (8,)), (4, (7, 6), (4,)))),
+    "last": ((), (5, 7, 6), ((0, (5, 7, 6), (0,)),)),
 }
 
 
@@ -43,24 +45,17 @@
     return tuple((p - q) % n for p, q, n in zip(a, b, TORUS))
 
 
-def products(step):
-    order, strips = STEPS[step]
-    for first, last, left, right, sides in strips:
-        yield order[first : last + 1], order[left : right + 1], sides
-
-
 def targets(step):
-    return tuple(sorted({b for rows, columns, sides in products(step) for b in sides if b in rows + columns}))
+    return tuple(sorted({b for a, others, sides in STEPS[step][2] for b in sides if b in (a, *others)}))
 
 
 def check():
     met = set()
-    for step in STEPS:
-        for rows, columns, sides in products(step):
-            for a in rows:
-                for b in columns:
-                    met |= {difference(OFFSETS[b], OFFSETS[a])} if a in sides else set()
-                    met |= {difference(OFFSETS[a], OFFSETS[b])} if b in sides else set()
+    for _, _, strips in STEPS.values():
+        for a, others, sides in strips:
+            for b in others:
+                met |= {difference(OFFSETS[b], OFFSETS[a])} if a in sides else set()
+                met |= {difference(OFFSETS[a], OFFSETS[b])} if b in sides else set()
     assert len(met) == 32
     assert all(OFFSETS[block] == by for block, by in FIRST)
     assert all(difference(OFFSETS[block], OFFSETS[parent]) == by for block, parent, by in SECOND)
@@ -158,25 +153,49 @@
 
 
 def score_kernel(step, given, *refs):
-    order = STEPS[step][0]
-    n = len(order)
+    direct, joined, strips = STEPS[step]
     results = targets(step)
-    place = {b: i for i, b in enumerate(order)}
-    blocks, refs = refs[:n], refs[n:]
-    earlier, refs = dict(zip(given, refs)), refs[len(given) :]
-    outs, refs = dict(zip(results, refs)), refs[len(results) :]
-    held, ids, sems = refs
-    copies = []
-    for i, block in enumerate(blocks):
-        copies.append(pltpu.make_async_copy(block.at[ROWS:], ids.at[i], sems.at[0, i]))
-        copies.append(pltpu.make_async_copy(block.at[:ROWS], held.at[pl.ds(i * ROWS, ROWS)], sems.at[1, i]))
-    for copy in copies:
-        copy.start()
-    for copy in copies:
-        copy.wait()
+    first = step == "early"
+    refs = list(refs)
+
+    def take(count):
+        taken, refs[:count] = refs[:count], []
+        return taken
+
+    in_place = dict(zip(direct, take(len(direct))))
+    sources = take(len(joined))
+    packed, packed_ids = (None, None) if first else take(2)
+    earlier = dict(zip(given, take(len(given))))
+    outs = dict(zip(results, take(len(results))))
+    if joined:
+        held, ids = take(2)
+        (sems,) = take(1)
+        copies = []
+        for i, block in enumerate(sources):
+            copies.append(pltpu.make_async_copy(block.at[ROWS:], ids.at[i], sems.at[0, i]))
+            copies.append(pltpu.make_async_copy(block.at[:ROWS], held.at[pl.ds(i * ROWS, ROWS)], sems.at[1, i]))
+        for copy in copies:
+            copy.start()
+        for copy in copies:
+            copy.wait()
+
+    def rows_of(blocks):
+        b, n = blocks[0], len(blocks)
+        if b in in_place:
+            return in_place[b][:ROWS, :]
+        order, ref = (joined, held) if b in joined else (PACKED, packed)
+        at = order.index(b)
+        assert order[at : at + n] == tuple(blocks)
+        return ref[at * ROWS : (at + n) * ROWS, :]
 
     def word(b):
-        parts = ids[place[b], :, :ROWS].astype(jnp.float32)
+        if b in in_place:
+            parts = in_place[b][ROWS:, :ROWS]
+        elif b in joined:
+            parts = ids[joined.index(b), :, :ROWS]
+        else:
+            parts = packed_ids[PACKED.index(b), :, :ROWS]
+        parts = parts.astype(jnp.float32)
         return parts[0:1] * 65536.0 + parts[1:2] * 256.0 + parts[2:3]
 
     over_lanes, over_rows = {}, {}
@@ -184,28 +203,24 @@
     def update(table, b, value):
         table[b] = jnp.maximum(table[b], value) if b in table else value
 
-    for rows, columns, sides in products(step):
+    for a, others, sides in strips:
         scores = lax.dot_general(
-            held[place[rows[0]] * ROWS : (place[rows[-1]] + 1) * ROWS, :],
-            held[place[columns[0]] * ROWS : (place[columns[-1]] + 1) * ROWS, :],
-            (((1,), (1,)), ((), ())),
-            preferred_element_type=jnp.float32,
+            rows_of((a,)), rows_of(others), (((1,), (1,)), ((), ())), preferred_element_type=jnp.float32
         )
-        for j, a in enumerate(rows):
-            near = jnp.broadcast_to(word(a), (128, ROWS)).T.astype(jnp.int32)
-            for i, b in enumerate(columns):
-                far = word(b).astype(jnp.int32)
-                down = []
-                for k in range(ROWS // 128):
-                    at = i * ROWS + k * 128
-                    mixed = near ^ far[:, k * 128 : (k + 1) * 128]
-                    partner = (mixed > 0) & (mixed < 65536)
-                    kept = jnp.where(partner, scores[j * ROWS : (j + 1) * ROWS, at : at + 128], -1.0)
-                    if a in sides:
-                        update(over_lanes, a, kept)
-                    down.append(jnp.max(kept.reshape(ROWS // 8, 8, 128), axis=0))
-                if b in sides and b != a:
-                    update(over_rows, b, jnp.concatenate(down, axis=1))
+        near = jnp.broadcast_to(word(a), (128, ROWS)).T.astype(jnp.int32)
+        for i, b in enumerate(others):
+            far = word(b).astype(jnp.int32)
+            down = []
+            for k in range(ROWS // 128):
+                at = i * ROWS + k * 128
+                mixed = near ^ far[:, k * 128 : (k + 1) * 128]
+                partner = (mixed > 0) & (mixed < 65536)
+                kept = jnp.where(partner, scores[:, at : at + 128], -1.0)
+                if a in sides:
+                    update(over_lanes, a, kept)
+                down.append(jnp.max(kept.reshape(ROWS // 8, 8, 128), axis=0))
+            if b in sides and b != a:
+                update(over_rows, b, jnp.concatenate(down, axis=1))
 
     for b in results:
         value = jnp.full((1, ROWS), -1.0, jnp.float32)
@@ -218,30 +233,30 @@
         outs[b][...] = value
 
 
-def score(step, blocks, earlier):
-    order = STEPS[step][0]
-    n = len(order)
+def score(step, blocks, earlier, packed=()):
+    direct, joined, strips = STEPS[step]
     results = targets(step)
     given = tuple(b for b in results if b in earlier)
-    pairs = sum(len(rows) * len(columns) for rows, columns, _ in products(step))
-    vmem = pl.BlockSpec(memory_space=pltpu.VMEM)
+    n = len(joined)
+    first = step == "early"
+    pairs = sum(len(others) for _, others, _ in strips)
+    vmem, free = pl.BlockSpec(memory_space=pltpu.VMEM), pl.BlockSpec(memory_space=pl.ANY)
+    shapes = [((n * ROWS, WIDTH), jnp.bfloat16), ((n, TAIL, WIDTH), jnp.bfloat16)] if n else []
     values = pl.pallas_call(
         functools.partial(score_kernel, step, given),
-        out_shape=[jax.ShapeDtypeStruct((1, ROWS), jnp.float32)] * len(results),
-        in_specs=[pl.BlockSpec(memory_space=pl.ANY)] * n + [vmem] * len(given),
-        out_specs=[vmem] * len(results),
-        scratch_shapes=[
-            pltpu.VMEM((n * ROWS, WIDTH), jnp.bfloat16),
-            pltpu.VMEM((n, TAIL, WIDTH), jnp.bfloat16),
-            pltpu.SemaphoreType.DMA((2, n)),
-        ],
+        out_shape=[jax.ShapeDtypeStruct((1, ROWS), jnp.float32)] * len(results)
+        + [jax.ShapeDtypeStruct(*shape) for shape in shapes if first],
+        in_specs=[vmem] * len(direct) + [free] * n + [vmem] * (len(packed) + len(given)),
+        out_specs=[vmem] * (len(results) + (len(shapes) if first else 0)),
+        scratch_shapes=[pltpu.VMEM(*shape) for shape in shapes if not first]
+        + ([pltpu.SemaphoreType.DMA((2, n))] if n else []),
         compiler_params=pltpu.CompilerParams(vmem_limit_bytes=28 << 20),
         cost_estimate=pl.CostEstimate(
-            flops=2 * pairs * ROWS * ROWS * WIDTH, bytes_accessed=n * BLOCK * WIDTH * 2, transcendentals=0
+            flops=2 * pairs * ROWS * ROWS * WIDTH, bytes_accessed=2 * pairs * ROWS * WIDTH, transcendentals=0
         ),
         name="score_" + step,
-    )(*[blocks[b] for b in order], *[earlier[b] for b in given])
-    return {**earlier, **dict(zip(results, values))}
+    )(*[blocks[b] for b in direct + joined], *packed, *[earlier[b] for b in given])
+    return {**earlier, **dict(zip(results, values))}, values[len(results) :]
 
 
 def local(embeddings, cluster_id, source_id):
@@ -253,14 +268,17 @@
         else:
             blocks[block] = receive(whole, by)
     for block, parent, by in SECOND:
-        blocks[block] = receive(blocks[parent], by)
-    best = score("early", blocks, {})
-    best = score("middle", blocks, best)
-    best = score("second", blocks, best)
-    got = [receive(best[b], OFFSETS[b], back=True) for b in (3, 2)]
-    best = score("late", blocks, best)
+        whole = blocks[parent]
+        if block == 7:
+            whole, blocks[4] = lax.optimization_barrier((whole, blocks[4]))
+        blocks[block] = receive(whole, by)
+    best, packed = score("early", blocks, {})
+    best, _ = score("middle", blocks, best, packed)
+    best, _ = score("second", blocks, best, packed)
+    got = [receive(best[b], OFFSETS[b], back=True) for b in (2, 3)]
+    best, _ = score("late", blocks, best, packed)
     got += [receive(best[b], OFFSETS[b], back=True) for b in (8, 4)]
-    best = score("last", blocks, best)
+    best, _ = score("last", blocks, best, packed)
     own = best[0]
     for value in got:
         own = jnp.maximum(own, value)

time: 60.9 us -> 59.3 us (0.974)
  Pallas kernels: 15.4 us -> 13.9 us
  waiting for transfers between devices: 22 us -> 20.6 us
  local copies, waits for them, and re-layouts: 0.01 us -> 1.14 us
    ppermute x13, waiting for transfers between devices: 22 us -> 20.6 us  [receive(): return lax.ppermute(array, 'blk', links)]
    pallas_call x5, Pallas kernels: 12.7 us -> 11.5 us  [score(): pl.pallas_call(functools.partial(score_kernel, step, given), out_shape=[j...]
    unnamed x2, local copies, waits for them, and re-layouts: 0.01 us -> 1.14 us
  transfers between devices with their start and end apart: 13 -> 13, of which waited for: 5 -> 7; matrix products, arithmetic and copies ran while one was open for 0% -> 0% of each run, Pallas kernels for 25% -> 24%
where the time goes in v3:
time: 59.3 us; the launch traced here: 59.1 us
  starting transfers between devices  22.7 us (38%)
  waiting for transfers between devices  20.6 us (35%)
  Pallas kernels  13.9 us (23%)
  local copies, waits for them, and re-layouts  1.14 us (2%)
  other arithmetic  0.6 us (1%)
    ppermute x13, starting transfers between devices, receive(): return lax.ppermute(array, 'blk', links)  22.7 us
    ppermute x13, waiting for transfers between devices, receive(): return lax.ppermute(array, 'blk', links)  20.6 us
    pallas_call x5, Pallas kernels, score(): pl.pallas_call(functools.partial(score_kernel, step, given), out_shape=[j...  11.5 us
    pallas_call x1, Pallas kernels, prepare(): pl.pallas_call(prepare_kernel, out_shape=[jax.ShapeDtypeStruct((rows, WID...  2.21 us
  transfers between devices with their start and end apart: 13, of which 7 were waited for; matrix products, arithmetic and copies ran while one was open for 0% of the time, Pallas kernels for 24%

profile of v3, /device:TPU:0, one launch (start us, length us, event | category | flops | bytes accessed | tf_op | source)
XLA Modules:
  0.0 59.1 jit_solution(7367446463154991974)
XLA Ops:
  0.0 1.6 %collective-permute-start = (bf16[384,1024]{1,0:T(8,128)(2,1)}, bf16[384,1024]{1,0:T(8,128)(2,1)S(1)}, u32[]{:S(2)}, u32[]{:S(2)}) collective-permute-start(bf16[384,1024]{1,0:T(8,128)(2,1)} %embeddings.1), channel_id=1, source_target_pairs={{3,0},{0,1},{1,2},{2,3},{7,4},{4,5},{5,6},{6,7},{11,8},{8,9},{9,10... | collective-permute-start | bytes 2359304 | tf_op jit(solution)/shard_map/ppermute | solution.py:78
  1.6 2.2 %prepare.1 = (bf16[400,1024]{1,0:T(8,128)(2,1)}, bf16[16,1024]{1,0:T(8,128)(2,1)}) custom-call(bf16[384,1024]{1,0:T(8,128)(2,1)} %embeddings.1, s32[384]{0:T(512)} %cluster.1, s32[384]{0:T(512)} %source.1), custom_call_target="tpu_custom_call" | custom-call | tf_op jit(solution)/shard_map/prepare/pallas_call | solution.py:119
  3.8 3.2 %collective-permute-start.3 = (bf16[400,1024]{1,0:T(8,128)(2,1)}, bf16[400,1024]{1,0:T(8,128)(2,1)S(1)}, u32[]{:S(2)}, u32[]{:S(2)}) collective-permute-start(bf16[400,1024]{1,0:T(8,128)(2,1)} %get-tuple-element.24.refs_1_), channel_id=1, source_target_pairs={{13,0},{14,1},{15,2},{12,3},{1,4},{2,5},{3,6},{0,7},{5,8},{6,9},{7... | collective-permute-start | bytes 2457608 | tf_op jit(solution)/shard_map/ppermute | solution.py:78
  7.0 1.6 %collective-permute-start.4 = (bf16[400,1024]{1,0:T(8,128)(2,1)}, bf16[400,1024]{1,0:T(8,128)(2,1)S(1)}, u32[]{:S(2)}, u32[]{:S(2)}) collective-permute-start(bf16[400,1024]{1,0:T(8,128)(2,1)} %get-tuple-element.24.refs_1_), channel_id=1, source_target_pairs={{16,0},{17,1},{18,2},{19,3},{20,4},{21,5},{22,6},{23,7},{24,8},{25... | collective-permute-start | bytes 2457608 | tf_op jit(solution)/shard_map/ppermute | solution.py:78
  8.5 1.3 %collective-permute-start.6 = (bf16[400,1024]{1,0:T(8,128)(2,1)}, bf16[400,1024]{1,0:T(8,128)(2,1)S(1)}, u32[]{:S(2)}, u32[]{:S(2)}) collective-permute-start(bf16[400,1024]{1,0:T(8,128)(2,1)} %get-tuple-element.24.refs_1_), channel_id=1, source_target_pairs={{4,0},{5,1},{6,2},{7,3},{8,4},{9,5},{10,6},{11,7},{12,8},{13,9},{1... | collective-permute-start | bytes 2457608 | tf_op jit(solution)/shard_map/ppermute | solution.py:78
  9.9 1.2 %collective-permute-start.1 = (bf16[16,1024]{1,0:T(8,128)(2,1)}, bf16[16,1024]{1,0:T(8,128)(2,1)S(1)}, u32[]{:S(2)}, u32[]{:S(2)}) collective-permute-start(bf16[16,1024]{1,0:T(8,128)(2,1)} %get-tuple-element.23), channel_id=1, source_target_pairs={{3,0},{0,1},{1,2},{2,3},{7,4},{4,5},{5,6},{6,7},{11,8},{8,9},{9,10... | collective-permute-start | bytes 98312 | tf_op jit(solution)/shard_map/ppermute | solution.py:78
  11.1 10.2 %collective-permute-done.1.tail = bf16[16,1024]{1,0:T(8,128)(2,1)S(1)} collective-permute-done((bf16[16,1024]{1,0:T(8,128)(2,1)}, bf16[16,1024]{1,0:T(8,128)(2,1)S(1)}, u32[]{:S(2)}, u32[]{:S(2)}) %collective-permute-start.1) | collective-permute-done | bytes 32800 | tf_op jit(solution)/shard_map/ppermute | solution.py:78
  21.3 0.0 collective-permute-done.raw
  21.3 0.2 join.1.refs_0_
  21.6 0.5 collective-permute-start.2
  22.1 1.6 %collective-permute-start.8 = (bf16[400,1024]{1,0:T(8,128)(2,1)S(1)}, bf16[400,1024]{1,0:T(8,128)(2,1)S(1)}, u32[]{:S(2)}, u32[]{:S(2)}) collective-permute-start(bf16[400,1024]{1,0:T(8,128)(2,1)S(1)} %join.1.refs_0_), channel_id=1, source_target_pairs={{16,0},{17,1},{18,2},{19,3},{20,4},{21,5},{22,6},{23,7},{24,8},{25... | collective-permute-start | bytes 2457608 | tf_op jit(solution)/shard_map/ppermute | solution.py:78
  23.7 3.3 %collective-permute-done.3.refs_3_ = bf16[400,1024]{1,0:T(8,128)(2,1)S(1)} collective-permute-done((bf16[400,1024]{1,0:T(8,128)(2,1)}, bf16[400,1024]{1,0:T(8,128)(2,1)S(1)}, u32[]{:S(2)}, u32[]{:S(2)}) %collective-permute-start.3) | collective-permute-done | bytes 819232 | tf_op jit(solution)/shard_map/ppermute | solution.py:78
  27.0 1.4 %collective-permute-done.4.refs_4_ = bf16[400,1024]{1,0:T(8,128)(2,1)S(1)} collective-permute-done((bf16[400,1024]{1,0:T(8,128)(2,1)}, bf16[400,1024]{1,0:T(8,128)(2,1)S(1)}, u32[]{:S(2)}, u32[]{:S(2)}) %collective-permute-start.4) | collective-permute-done | bytes 819232 | tf_op jit(solution)/shard_map/ppermute | solution.py:78
  28.4 2.9 %collective-permute-start.5 = (bf16[400,1024]{1,0:T(8,128)(2,1)S(1)}, bf16[400,1024]{1,0:T(8,128)(2,1)S(1)}, u32[]{:S(2)}, u32[]{:S(2)}) collective-permute-start(bf16[400,1024]{1,0:T(8,128)(2,1)S(1)} %collective-permute-done.3.refs_3_), channel_id=1, source_target_pairs={{13,0},{14,1},{15,2},{12,3},{1,4},{2,5},{3,6},{0,7},{5,8},{6,9},{7... | collective-permute-start | bytes 2457608 | tf_op jit(solution)/shard_map/ppermute | solution.py:78
  31.3 1.3 %collective-permute-start.7 = (bf16[400,1024]{1,0:T(8,128)(2,1)S(1)}, bf16[400,1024]{1,0:T(8,128)(2,1)S(1)}, u32[]{:S(2)}, u32[]{:S(2)}) collective-permute-start(bf16[400,1024]{1,0:T(8,128)(2,1)S(1)} %collective-permute-done.6.refs_2_), channel_id=1, source_target_pairs={{4,0},{5,1},{6,2},{7,3},{8,4},{9,5},{10,6},{11,7},{12,8},{13,9},{1... | collective-permute-start | bytes 2457608 | tf_op jit(solution)/shard_map/ppermute | solution.py:78
  32.6 1.1 %copy-done = bf16[400,1024]{1,0:T(8,128)(2,1)S(1)} copy-done((bf16[400,1024]{1,0:T(8,128)(2,1)S(1)}, bf16[400,1024]{1,0:T(8,128)(2,1)}, u32[]{:S(2)}) %copy-start) | copy-done | bytes 819224
  33.7 4.9 %score_early.1 = (f32[1,384]{1,0:T(1,128)S(1)}, f32[1,384]{1,0:T(1,128)S(1)}, f32[1,384]{1,0:T(1,128)S(1)}, f32[1,384]{1,0:T(1,128)S(1)}, bf16[1920,1024]{1,0:T(...) custom-call(bf16[400,1024]{1,0:T(8,128)(2,1)S(1)} %join.1.refs_0_, bf16[400,1024]{1,0:T(8,128)(2,1)S(1)} %copy-done, ...), custom_call_target="tpu_custom_call" | custom-call | flops 3321888768 | bytes 8650752 | tf_op jit(solution)/shard_map/score_early/pallas_call | solution.py:245
  38.6 3.2 %collective-permute-done.2.refs_0_ = bf16[400,1024]{1,0:T(8,128)(2,1)S(1)} collective-permute-done((bf16[400,1024]{1,0:T(8,128)(2,1)S(1)}, bf16[400,1024]{1,0:T(8,128)(2,1)S(1)}, u32[]{:S(2)}, u32[]{:S(2)}) %collective-permute-start.2) | collective-permute-done | bytes 819232 | tf_op jit(solution)/shard_map/ppermute | solution.py:78
  41.8 1.3 %score_middle.1 = (f32[1,384]{1,0:T(1,128)S(1)}, f32[1,384]{1,0:T(1,128)S(1)}, f32[1,384]{1,0:T(1,128)S(1)}) custom-call(bf16[400,1024]{1,0:T(8,128)(2,1)S(1)} %collective-permute-done.2.refs_0_, bf16[1920,1024]{1,0:T(8,128)(2,1)S(1)} %get-tuple-element.27.refs_3_.refs_1_, bf16[5,16,1024]{2,1,0:T(8,128)(2,1)S(1)} %get-tuple-element.28.refs_4_.refs_2_, ...), custom_call_target="tpu_custom_call" | custom-call | flops 905969664 | bytes 2359296 | tf_op jit(solution)/shard_map/score_middle/pallas_call | solution.py:245
  43.1 1.0 %collective-permute-done.8.refs_0_ = bf16[400,1024]{1,0:T(8,128)(2,1)S(1)} collective-permute-done((bf16[400,1024]{1,0:T(8,128)(2,1)S(1)}, bf16[400,1024]{1,0:T(8,128)(2,1)S(1)}, u32[]{:S(2)}, u32[]{:S(2)}) %collective-permute-start.8) | collective-permute-done | bytes 819232 | tf_op jit(solution)/shard_map/ppermute | solution.py:78
  44.1 1.7 %score_second.1 = (f32[1,384]{1,0:T(1,128)S(1)}, f32[1,384]{1,0:T(1,128)S(1)}, f32[1,384]{1,0:T(1,128)S(1)}) custom-call(bf16[400,1024]{1,0:T(8,128)(2,1)S(1)} %collective-permute-done.8.refs_0_, bf16[1920,1024]{1,0:T(8,128)(2,1)S(1)} %get-tuple-element.27.refs_3_.refs_1_, bf16[5,16,1024]{2,1,0:T(8,128)(2,1)S(1)} %get-tuple-element.28.refs_4_.refs_2_, ...), custom_call_target="tpu_custom_call" | custom-call | flops 1207959552 | bytes 3145728 | tf_op jit(solution)/shard_map/score_second/pallas_call | solution.py:245
  45.8 2.3 %collective-permute-start.10 = (f32[1,384]{1,0:T(1,128)S(1)}, f32[1,384]{1,0:T(1,128)S(1)}, u32[]{:S(2)}, u32[]{:S(2)}) collective-permute-start(f32[1,384]{1,0:T(1,128)S(1)} %get-tuple-element.36), channel_id=1, source_target_pairs={{0,13},{1,14},{2,15},{3,12},{4,1},{5,2},{6,3},{7,0},{8,5},{9,6},{1... | collective-permute-start | bytes 4616 | tf_op jit(solution)/shard_map/ppermute | solution.py:78
  48.1 0.0 collective-permute-start.9
  48.1 0.1 collective-permute-done.5.refs_1_
  48.2 1.9 %score_late.1 = (f32[1,384]{1,0:T(1,128)S(1)}, f32[1,384]{1,0:T(1,128)S(1)}) custom-call(bf16[400,1024]{1,0:T(8,128)(2,1)S(1)} %collective-permute-done.8.refs_0_, bf16[400,1024]{1,0:T(8,128)(2,1)S(1)} %collective-permute-done.5.refs_1_, bf16[400,1024]{1,0:T(8,128)(2,1)S(1)} %collective-permute-done.7.refs_2_, ...), custom_call_target="tpu_custom_call" | custom-call | flops 1207959552 | bytes 3145728 | tf_op jit(solution)/shard_map/score_late/pallas_call | solution.py:245
  50.2 4.8 %collective-permute-start.11 = (f32[1,384]{1,0:T(1,128)S(1)}, f32[1,384]{1,0:T(1,128)S(1)}, u32[]{:S(2)}, u32[]{:S(2)}) collective-permute-start(f32[1,384]{1,0:T(1,128)S(1)} %get-tuple-element.39), channel_id=1, source_target_pairs={{0,19},{1,16},{2,17},{3,18},{4,23},{5,20},{6,21},{7,22},{8,27},{9,... | collective-permute-start | bytes 4616 | tf_op jit(solution)/shard_map/ppermute | solution.py:78
  55.0 0.4 collective-permute-start.12
  55.4 1.7 %score_last.1 = f32[1,384]{1,0:T(1,128)S(1)} custom-call(bf16[400,1024]{1,0:T(8,128)(2,1)S(1)} %collective-permute-done.2.refs_0_, bf16[400,1024]{1,0:T(8,128)(2,1)S(1)} %collective-permute-done.5.refs_1_, bf16[400,1024]{1,0:T(8,128)(2,1)S(1)} %collective-permute-done.7.refs_2_, bf16[1920,1024]{1,0:T(8,128)(2,1)S(1)} %get-tuple-element.27.refs_3_.refs_1_, ...), custom_call_target="tpu_custom_call" | custom-call | flops 905969664 | bytes 2359296 | tf_op jit(solution)/shard_map/score_last/pallas_call | solution.py:245
  57.1 0.0 collective-permute-done.9
  57.1 0.0 collective-permute-done.11
  57.2 1.4 %collective-permute-done.12 = f32[1,384]{1,0:T(1,128)S(1)} collective-permute-done((f32[1,384]{1,0:T(1,128)S(1)}, f32[1,384]{1,0:T(1,128)S(1)}, u32[]{:S(2)}, u32[]{:S(2)}) %collective-permute-start.12) | collective-permute-done | bytes 1568 | tf_op jit(solution)/shard_map/ppermute | solution.py:78
  58.5 0.6 %maximum_reduce_fusion = f32[384]{0:T(512)} fusion(f32[1,384]{1,0:T(1,128)S(1)} %collective-permute-done.12, f32[1,384]{1,0:T(1,128)S(1)} %collective-permute-done.11, f32[1,384]{1,0:T(1,128)S(1)} %collective-permute-done.10, f32[1,384]{1,0:T(1,128)S(1)} %score_last.1, f32[1,384]{1,0:T(1,128)S(1)} %collective-permute-done.9), kind=kLoop, calls=%fused_computation | loop fusion | flops 1536 | bytes 9216 | tf_op jit(solution)/shard_map/max | solution.py:284
  (4 shorter events, 0.0 us)
Async XLA Ops:
  0.0 21.3 %collective-permute-start = (bf16[384,1024]{1,0:T(8,128)(2,1)}, bf16[384,1024]{1,0:T(8,128)(2,1)S(1)}, u32[]{:S(2)}, u32[]{:S(2)}) collective-permute-start(bf16[384,1024]{1,0:T(8,128)(2,1)} %embeddings.1), channel_id=1, source_target_pairs={{3,0},{0,1},{1,2},{2,3},{7,4},{4,5},{5,6},{6,7},{11,8},{8,9},{9,10... | collective-permute-start | bytes 2359304 | tf_op jit(solution)/shard_map/ppermute | solution.py:78
  3.8 23.2 %collective-permute-start.3 = (bf16[400,1024]{1,0:T(8,128)(2,1)}, bf16[400,1024]{1,0:T(8,128)(2,1)S(1)}, u32[]{:S(2)}, u32[]{:S(2)}) collective-permute-start(bf16[400,1024]{1,0:T(8,128)(2,1)} %get-tuple-element.24.refs_1_), channel_id=1, source_target_pairs={{13,0},{14,1},{15,2},{12,3},{1,4},{2,5},{3,6},{0,7},{5,8},{6,9},{7... | collective-permute-start | bytes 2457608 | tf_op jit(solution)/shard_map/ppermute | solution.py:78
  7.0 21.4 %collective-permute-start.4 = (bf16[400,1024]{1,0:T(8,128)(2,1)}, bf16[400,1024]{1,0:T(8,128)(2,1)S(1)}, u32[]{:S(2)}, u32[]{:S(2)}) collective-permute-start(bf16[400,1024]{1,0:T(8,128)(2,1)} %get-tuple-element.24.refs_1_), channel_id=1, source_target_pairs={{16,0},{17,1},{18,2},{19,3},{20,4},{21,5},{22,6},{23,7},{24,8},{25... | collective-permute-start | bytes 2457608 | tf_op jit(solution)/shard_map/ppermute | solution.py:78
  8.5 22.7 %collective-permute-start.6 = (bf16[400,1024]{1,0:T(8,128)(2,1)}, bf16[400,1024]{1,0:T(8,128)(2,1)S(1)}, u32[]{:S(2)}, u32[]{:S(2)}) collective-permute-start(bf16[400,1024]{1,0:T(8,128)(2,1)} %get-tuple-element.24.refs_1_), channel_id=1, source_target_pairs={{4,0},{5,1},{6,2},{7,3},{8,4},{9,5},{10,6},{11,7},{12,8},{13,9},{1... | collective-permute-start | bytes 2457608 | tf_op jit(solution)/shard_map/ppermute | solution.py:78
  9.9 11.4 %collective-permute-start.1 = (bf16[16,1024]{1,0:T(8,128)(2,1)}, bf16[16,1024]{1,0:T(8,128)(2,1)S(1)}, u32[]{:S(2)}, u32[]{:S(2)}) collective-permute-start(bf16[16,1024]{1,0:T(8,128)(2,1)} %get-tuple-element.23), channel_id=1, source_target_pairs={{3,0},{0,1},{1,2},{2,3},{7,4},{4,5},{5,6},{6,7},{11,8},{8,9},{9,10... | collective-permute-start | bytes 98312 | tf_op jit(solution)/shard_map/ppermute | solution.py:78
  21.6 20.3 %collective-permute-start.2 = (bf16[400,1024]{1,0:T(8,128)(2,1)S(1)}, bf16[400,1024]{1,0:T(8,128)(2,1)S(1)}, u32[]{:S(2)}, u32[]{:S(2)}) collective-permute-start(bf16[400,1024]{1,0:T(8,128)(2,1)S(1)} %join.1.refs_0_), channel_id=1, source_target_pairs={{3,0},{0,1},{1,2},{2,3},{7,4},{4,5},{5,6},{6,7},{11,8},{8,9},{9,10... | collective-permute-start | bytes 2457608 | tf_op jit(solution)/shard_map/ppermute | solution.py:78
  22.1 22.1 %collective-permute-start.8 = (bf16[400,1024]{1,0:T(8,128)(2,1)S(1)}, bf16[400,1024]{1,0:T(8,128)(2,1)S(1)}, u32[]{:S(2)}, u32[]{:S(2)}) collective-permute-start(bf16[400,1024]{1,0:T(8,128)(2,1)S(1)} %join.1.refs_0_), channel_id=1, source_target_pairs={{16,0},{17,1},{18,2},{19,3},{20,4},{21,5},{22,6},{23,7},{24,8},{25... | collective-permute-start | bytes 2457608 | tf_op jit(solution)/shard_map/ppermute | solution.py:78
  28.4 19.9 %collective-permute-start.5 = (bf16[400,1024]{1,0:T(8,128)(2,1)S(1)}, bf16[400,1024]{1,0:T(8,128)(2,1)S(1)}, u32[]{:S(2)}, u32[]{:S(2)}) collective-permute-start(bf16[400,1024]{1,0:T(8,128)(2,1)S(1)} %collective-permute-done.3.refs_3_), channel_id=1, source_target_pairs={{13,0},{14,1},{15,2},{12,3},{1,4},{2,5},{3,6},{0,7},{5,8},{6,9},{7... | collective-permute-start | bytes 2457608 | tf_op jit(solution)/shard_map/ppermute | solution.py:78
  31.3 17.0 %collective-permute-start.7 = (bf16[400,1024]{1,0:T(8,128)(2,1)S(1)}, bf16[400,1024]{1,0:T(8,128)(2,1)S(1)}, u32[]{:S(2)}, u32[]{:S(2)}) collective-permute-start(bf16[400,1024]{1,0:T(8,128)(2,1)S(1)} %collective-permute-done.6.refs_2_), channel_id=1, source_target_pairs={{4,0},{5,1},{6,2},{7,3},{8,4},{9,5},{10,6},{11,7},{12,8},{13,9},{1... | collective-permute-start | bytes 2457608 | tf_op jit(solution)/shard_map/ppermute | solution.py:78
  32.6 1.1 %copy-start = (bf16[400,1024]{1,0:T(8,128)(2,1)S(1)}, bf16[400,1024]{1,0:T(8,128)(2,1)}, u32[]{:S(2)}) copy-start(bf16[400,1024]{1,0:T(8,128)(2,1)} %get-tuple-element.24.refs_1_) | copy-start | bytes 2457604
  45.8 11.3 %collective-permute-start.10 = (f32[1,384]{1,0:T(1,128)S(1)}, f32[1,384]{1,0:T(1,128)S(1)}, u32[]{:S(2)}, u32[]{:S(2)}) collective-permute-start(f32[1,384]{1,0:T(1,128)S(1)} %get-tuple-element.36), channel_id=1, source_target_pairs={{0,13},{1,14},{2,15},{3,12},{4,1},{5,2},{6,3},{7,0},{8,5},{9,6},{1... | collective-permute-start | bytes 4616 | tf_op jit(solution)/shard_map/ppermute | solution.py:78
  48.1 9.0 %collective-permute-start.9 = (f32[1,384]{1,0:T(1,128)S(1)}, f32[1,384]{1,0:T(1,128)S(1)}, u32[]{:S(2)}, u32[]{:S(2)}) collective-permute-start(f32[1,384]{1,0:T(1,128)S(1)} %get-tuple-element.35), channel_id=1, source_target_pairs={{0,4},{1,5},{2,6},{3,7},{4,8},{5,9},{6,10},{7,11},{8,12},{9,13},{1... | collective-permute-start | bytes 4616 | tf_op jit(solution)/shard_map/ppermute | solution.py:78
  50.2 7.0 %collective-permute-start.11 = (f32[1,384]{1,0:T(1,128)S(1)}, f32[1,384]{1,0:T(1,128)S(1)}, u32[]{:S(2)}, u32[]{:S(2)}) collective-permute-start(f32[1,384]{1,0:T(1,128)S(1)} %get-tuple-element.39), channel_id=1, source_target_pairs={{0,19},{1,16},{2,17},{3,18},{4,23},{5,20},{6,21},{7,22},{8,27},{9,... | collective-permute-start | bytes 4616 | tf_op jit(solution)/shard_map/ppermute | solution.py:78
  55.0 3.6 %collective-permute-start.12 = (f32[1,384]{1,0:T(1,128)S(1)}, f32[1,384]{1,0:T(1,128)S(1)}, u32[]{:S(2)}, u32[]{:S(2)}) collective-permute-start(f32[1,384]{1,0:T(1,128)S(1)} %get-tuple-element.40), channel_id=1, source_target_pairs={{0,16},{1,17},{2,18},{3,19},{4,20},{5,21},{6,22},{7,23},{8,24},{9,... | collective-permute-start | bytes 4616 | tf_op jit(solution)/shard_map/ppermute | solution.py:78

commit v4 on v3

--- a/solution.py
+++ b/solution.py
@@ -84,7 +84,7 @@
     return (widened * factor).astype(jnp.bfloat16)
 
 
-def prepare_kernel(embeddings, cluster, source, out, out_tail, raw, clusters, sources, unit, sems):
+def prepare_kernel(embeddings, cluster, source, out, out_tail, raw, clusters, sources, unit, short, sems):
     def copy(source_rows, target_rows, sem):
         return pltpu.make_async_copy(source_rows, target_rows, sems.at[sem])
 
@@ -93,7 +93,7 @@
     arriving = [copy(embeddings.at[rows], raw.at[rows], i) for i, rows in enumerate(stripes)]
     leaving = [copy(unit.at[rows], out.at[rows], STRIPES + i) for i, rows in enumerate(stripes)]
     leaving.append(copy(unit.at[ROWS:], out.at[ROWS:], 2 * STRIPES + 2))
-    leaving.append(copy(unit.at[ROWS:], out_tail, 2 * STRIPES + 3))
+    leaving.append(copy(short, out_tail, 2 * STRIPES + 3))
     for move in ids + arriving:
         move.start()
     for move in ids:
@@ -102,7 +102,11 @@
     number = sources[...].reshape(1, ROWS)
     rank = clusters[...].reshape(1, ROWS)
     tail = jnp.where(line == 0, rank, jnp.where(line == 1, number // 256, jnp.where(line == 2, number % 256, 0)))
-    unit[ROWS:, :ROWS] = tail.astype(jnp.float32).astype(jnp.bfloat16)
+    tail = tail.astype(jnp.float32)
+    unit[ROWS:, :ROWS] = tail.astype(jnp.bfloat16)
+    pieces = [tail[i : i + 1, k * 128 : (k + 1) * 128] for i in range(3) for k in range(ROWS // 128)]
+    pieces.append(jnp.zeros((TAIL - len(pieces), 128), jnp.float32))
+    short[...] = jnp.concatenate(pieces, axis=0).astype(jnp.bfloat16)
     unit[ROWS:, ROWS:] = jnp.zeros((TAIL, WIDTH - ROWS), jnp.bfloat16)
     leaving[STRIPES].start()
     leaving[STRIPES + 1].start()
@@ -118,7 +122,7 @@
     far = pl.BlockSpec(memory_space=pltpu.HBM)
     return pl.pallas_call(
         prepare_kernel,
-        out_shape=[jax.ShapeDtypeStruct((rows, WIDTH), jnp.bfloat16) for rows in (BLOCK, TAIL)],
+        out_shape=[jax.ShapeDtypeStruct(shape, jnp.bfloat16) for shape in ((BLOCK, WIDTH), (TAIL, 128))],
         in_specs=[far] * 3,
         out_specs=[far] * 2,
         scratch_shapes=[
@@ -126,6 +130,7 @@
             pltpu.VMEM((ROWS,), jnp.int32),
             pltpu.VMEM((ROWS,), jnp.int32),
             pltpu.VMEM((BLOCK, WIDTH), jnp.bfloat16),
+            pltpu.VMEM((TAIL, 128), jnp.bfloat16),
             pltpu.SemaphoreType.DMA((2 * STRIPES + 4,)),
         ],
         compiler_params=pltpu.CompilerParams(vmem_limit_bytes=60 << 20),
@@ -137,7 +142,12 @@
     for i in range(STRIPES):
         rows = slice(i * STRIPE, (i + 1) * STRIPE)
         out[rows, :] = unit_rows(raw[rows, :])
-    out[ROWS:, :] = tail[...]
+    short = tail[...].astype(jnp.float32)
+    n = ROWS // 128
+    lines = [jnp.concatenate([short[i * n + k : i * n + k + 1] for k in range(n)], axis=1) for i in range(3)]
+    lines.append(jnp.zeros((TAIL - 3, ROWS), jnp.float32))
+    out[ROWS:, :ROWS] = jnp.concatenate(lines, axis=0).astype(jnp.bfloat16)
+    out[ROWS:, ROWS:] = jnp.zeros((TAIL, WIDTH - ROWS), jnp.bfloat16)
 
 
 def join(raw, tail):

time: 59.3 us -> 58.7 us (0.990)
  starting transfers between devices: 22.7 us -> 22.1 us
    ppermute x13, starting transfers between devices: 22.7 us -> 22.1 us  [receive(): return lax.ppermute(array, 'blk', links)]
where the time goes in v4:
time: 58.7 us; the launch traced here: 58.5 us
  starting transfers between devices  22.1 us (38%)
  waiting for transfers between devices  20.6 us (35%)
  Pallas kernels  14 us (24%)
  local copies, waits for them, and re-layouts  1.14 us (2%)
  other arithmetic  0.6 us (1%)
    ppermute x13, starting transfers between devices, receive(): return lax.ppermute(array, 'blk', links)  22.1 us
    ppermute x13, waiting for transfers between devices, receive(): return lax.ppermute(array, 'blk', links)  20.6 us
    pallas_call x5, Pallas kernels, score(): pl.pallas_call(functools.partial(score_kernel, step, given), out_shape=[j...  11.5 us
    pallas_call x1, Pallas kernels, prepare(): pl.pallas_call(prepare_kernel, out_shape=[jax.ShapeDtypeStruct(shape, jnp...  2.21 us
  transfers between devices with their start and end apart: 13, of which 7 were waited for; matrix products, arithmetic and copies ran while one was open for 0% of the time, Pallas kernels for 24%

profile of v4, /device:TPU:0, one launch (start us, length us, event | category | flops | bytes accessed | tf_op | source)
XLA Modules:
  0.0 58.5 jit_solution(9933998388823469221)
XLA Ops:
  0.0 1.6 %collective-permute-start = (bf16[384,1024]{1,0:T(8,128)(2,1)}, bf16[384,1024]{1,0:T(8,128)(2,1)S(1)}, u32[]{:S(2)}, u32[]{:S(2)}) collective-permute-start(bf16[384,1024]{1,0:T(8,128)(2,1)} %embeddings.1), channel_id=1, source_target_pairs={{3,0},{0,1},{1,2},{2,3},{7,4},{4,5},{5,6},{6,7},{11,8},{8,9},{9,10... | collective-permute-start | bytes 2359304 | tf_op jit(solution)/shard_map/ppermute | solution.py:78
  1.6 2.2 %prepare.1 = (bf16[400,1024]{1,0:T(8,128)(2,1)}, bf16[16,128]{1,0:T(8,128)(2,1)}) custom-call(bf16[384,1024]{1,0:T(8,128)(2,1)} %embeddings.1, s32[384]{0:T(512)} %cluster.1, s32[384]{0:T(512)} %source.1), custom_call_target="tpu_custom_call" | custom-call | tf_op jit(solution)/shard_map/prepare/pallas_call | solution.py:123
  3.8 3.2 %collective-permute-start.3 = (bf16[400,1024]{1,0:T(8,128)(2,1)}, bf16[400,1024]{1,0:T(8,128)(2,1)S(1)}, u32[]{:S(2)}, u32[]{:S(2)}) collective-permute-start(bf16[400,1024]{1,0:T(8,128)(2,1)} %get-tuple-element.24.refs_1_), channel_id=1, source_target_pairs={{13,0},{14,1},{15,2},{12,3},{1,4},{2,5},{3,6},{0,7},{5,8},{6,9},{7... | collective-permute-start | bytes 2457608 | tf_op jit(solution)/shard_map/ppermute | solution.py:78
  7.0 1.6 %collective-permute-start.4 = (bf16[400,1024]{1,0:T(8,128)(2,1)}, bf16[400,1024]{1,0:T(8,128)(2,1)S(1)}, u32[]{:S(2)}, u32[]{:S(2)}) collective-permute-start(bf16[400,1024]{1,0:T(8,128)(2,1)} %get-tuple-element.24.refs_1_), channel_id=1, source_target_pairs={{16,0},{17,1},{18,2},{19,3},{20,4},{21,5},{22,6},{23,7},{24,8},{25... | collective-permute-start | bytes 2457608 | tf_op jit(solution)/shard_map/ppermute | solution.py:78
  8.5 1.3 %collective-permute-start.6 = (bf16[400,1024]{1,0:T(8,128)(2,1)}, bf16[400,1024]{1,0:T(8,128)(2,1)S(1)}, u32[]{:S(2)}, u32[]{:S(2)}) collective-permute-start(bf16[400,1024]{1,0:T(8,128)(2,1)} %get-tuple-element.24.refs_1_), channel_id=1, source_target_pairs={{4,0},{5,1},{6,2},{7,3},{8,4},{9,5},{10,6},{11,7},{12,8},{13,9},{1... | collective-permute-start | bytes 2457608 | tf_op jit(solution)/shard_map/ppermute | solution.py:78
  9.9 1.2 %collective-permute-start.1 = (bf16[16,128]{1,0:T(8,128)(2,1)}, bf16[16,128]{1,0:T(8,128)(2,1)S(1)}, u32[]{:S(2)}, u32[]{:S(2)}) collective-permute-start(bf16[16,128]{1,0:T(8,128)(2,1)} %get-tuple-element.23), channel_id=1, source_target_pairs={{3,0},{0,1},{1,2},{2,3},{7,4},{4,5},{5,6},{6,7},{11,8},{8,9},{9,10... | collective-permute-start | bytes 12296 | tf_op jit(solution)/shard_map/ppermute | solution.py:78
  11.1 9.6 %collective-permute-done.1.tail = bf16[16,128]{1,0:T(8,128)(2,1)S(1)} collective-permute-done((bf16[16,128]{1,0:T(8,128)(2,1)}, bf16[16,128]{1,0:T(8,128)(2,1)S(1)}, u32[]{:S(2)}, u32[]{:S(2)}) %collective-permute-start.1) | collective-permute-done | bytes 4128 | tf_op jit(solution)/shard_map/ppermute | solution.py:78
  20.7 0.3 join.1.refs_0_
  20.9 0.5 collective-permute-start.2
  21.5 1.6 %collective-permute-start.8 = (bf16[400,1024]{1,0:T(8,128)(2,1)S(1)}, bf16[400,1024]{1,0:T(8,128)(2,1)S(1)}, u32[]{:S(2)}, u32[]{:S(2)}) collective-permute-start(bf16[400,1024]{1,0:T(8,128)(2,1)S(1)} %join.1.refs_0_), channel_id=1, source_target_pairs={{16,0},{17,1},{18,2},{19,3},{20,4},{21,5},{22,6},{23,7},{24,8},{25... | collective-permute-start | bytes 2457608 | tf_op jit(solution)/shard_map/ppermute | solution.py:78
  23.1 3.9 %collective-permute-done.3.refs_3_ = bf16[400,1024]{1,0:T(8,128)(2,1)S(1)} collective-permute-done((bf16[400,1024]{1,0:T(8,128)(2,1)}, bf16[400,1024]{1,0:T(8,128)(2,1)S(1)}, u32[]{:S(2)}, u32[]{:S(2)}) %collective-permute-start.3) | collective-permute-done | bytes 819232 | tf_op jit(solution)/shard_map/ppermute | solution.py:78
  27.0 1.4 %collective-permute-done.4.refs_4_ = bf16[400,1024]{1,0:T(8,128)(2,1)S(1)} collective-permute-done((bf16[400,1024]{1,0:T(8,128)(2,1)}, bf16[400,1024]{1,0:T(8,128)(2,1)S(1)}, u32[]{:S(2)}, u32[]{:S(2)}) %collective-permute-start.4) | collective-permute-done | bytes 819232 | tf_op jit(solution)/shard_map/ppermute | solution.py:78
  28.4 2.9 %collective-permute-start.5 = (bf16[400,1024]{1,0:T(8,128)(2,1)S(1)}, bf16[400,1024]{1,0:T(8,128)(2,1)S(1)}, u32[]{:S(2)}, u32[]{:S(2)}) collective-permute-start(bf16[400,1024]{1,0:T(8,128)(2,1)S(1)} %collective-permute-done.3.refs_3_), channel_id=1, source_target_pairs={{13,0},{14,1},{15,2},{12,3},{1,4},{2,5},{3,6},{0,7},{5,8},{6,9},{7... | collective-permute-start | bytes 2457608 | tf_op jit(solution)/shard_map/ppermute | solution.py:78
  31.3 0.0 collective-permute-done.6.refs_2_
  31.3 1.3 %collective-permute-start.7 = (bf16[400,1024]{1,0:T(8,128)(2,1)S(1)}, bf16[400,1024]{1,0:T(8,128)(2,1)S(1)}, u32[]{:S(2)}, u32[]{:S(2)}) collective-permute-start(bf16[400,1024]{1,0:T(8,128)(2,1)S(1)} %collective-permute-done.6.refs_2_), channel_id=1, source_target_pairs={{4,0},{5,1},{6,2},{7,3},{8,4},{9,5},{10,6},{11,7},{12,8},{13,9},{1... | collective-permute-start | bytes 2457608 | tf_op jit(solution)/shard_map/ppermute | solution.py:78
  32.6 1.1 %copy-done = bf16[400,1024]{1,0:T(8,128)(2,1)S(1)} copy-done((bf16[400,1024]{1,0:T(8,128)(2,1)S(1)}, bf16[400,1024]{1,0:T(8,128)(2,1)}, u32[]{:S(2)}) %copy-start) | copy-done | bytes 819224
  33.7 4.9 %score_early.1 = (f32[1,384]{1,0:T(1,128)S(1)}, f32[1,384]{1,0:T(1,128)S(1)}, f32[1,384]{1,0:T(1,128)S(1)}, f32[1,384]{1,0:T(1,128)S(1)}, bf16[1920,1024]{1,0:T(...) custom-call(bf16[400,1024]{1,0:T(8,128)(2,1)S(1)} %join.1.refs_0_, bf16[400,1024]{1,0:T(8,128)(2,1)S(1)} %copy-done, ...), custom_call_target="tpu_custom_call" | custom-call | flops 3321888768 | bytes 8650752 | tf_op jit(solution)/shard_map/score_early/pallas_call | solution.py:255
  38.6 2.6 %collective-permute-done.2.refs_0_ = bf16[400,1024]{1,0:T(8,128)(2,1)S(1)} collective-permute-done((bf16[400,1024]{1,0:T(8,128)(2,1)S(1)}, bf16[400,1024]{1,0:T(8,128)(2,1)S(1)}, u32[]{:S(2)}, u32[]{:S(2)}) %collective-permute-start.2) | collective-permute-done | bytes 819232 | tf_op jit(solution)/shard_map/ppermute | solution.py:78
  41.2 1.3 %score_middle.1 = (f32[1,384]{1,0:T(1,128)S(1)}, f32[1,384]{1,0:T(1,128)S(1)}, f32[1,384]{1,0:T(1,128)S(1)}) custom-call(bf16[400,1024]{1,0:T(8,128)(2,1)S(1)} %collective-permute-done.2.refs_0_, bf16[1920,1024]{1,0:T(8,128)(2,1)S(1)} %get-tuple-element.27.refs_3_.refs_1_, bf16[5,16,1024]{2,1,0:T(8,128)(2,1)S(1)} %get-tuple-element.28.refs_4_.refs_2_, ...), custom_call_target="tpu_custom_call" | custom-call | flops 905969664 | bytes 2359296 | tf_op jit(solution)/shard_map/score_middle/pallas_call | solution.py:255
  42.5 1.6 %collective-permute-done.8.refs_0_ = bf16[400,1024]{1,0:T(8,128)(2,1)S(1)} collective-permute-done((bf16[400,1024]{1,0:T(8,128)(2,1)S(1)}, bf16[400,1024]{1,0:T(8,128)(2,1)S(1)}, u32[]{:S(2)}, u32[]{:S(2)}) %collective-permute-start.8) | collective-permute-done | bytes 819232 | tf_op jit(solution)/shard_map/ppermute | solution.py:78
  44.1 1.7 %score_second.1 = (f32[1,384]{1,0:T(1,128)S(1)}, f32[1,384]{1,0:T(1,128)S(1)}, f32[1,384]{1,0:T(1,128)S(1)}) custom-call(bf16[400,1024]{1,0:T(8,128)(2,1)S(1)} %collective-permute-done.8.refs_0_, bf16[1920,1024]{1,0:T(8,128)(2,1)S(1)} %get-tuple-element.27.refs_3_.refs_1_, bf16[5,16,1024]{2,1,0:T(8,128)(2,1)S(1)} %get-tuple-element.28.refs_4_.refs_2_, ...), custom_call_target="tpu_custom_call" | custom-call | flops 1207959552 | bytes 3145728 | tf_op jit(solution)/shard_map/score_second/pallas_call | solution.py:255
  45.8 2.3 %collective-permute-start.10 = (f32[1,384]{1,0:T(1,128)S(1)}, f32[1,384]{1,0:T(1,128)S(1)}, u32[]{:S(2)}, u32[]{:S(2)}) collective-permute-start(f32[1,384]{1,0:T(1,128)S(1)} %get-tuple-element.36), channel_id=1, source_target_pairs={{0,13},{1,14},{2,15},{3,12},{4,1},{5,2},{6,3},{7,0},{8,5},{9,6},{1... | collective-permute-start | bytes 4616 | tf_op jit(solution)/shard_map/ppermute | solution.py:78
  48.1 0.0 collective-permute-start.9
  48.1 0.1 collective-permute-done.5.refs_1_
  48.2 0.0 collective-permute-done.7.refs_2_
  48.2 1.9 %score_late.1 = (f32[1,384]{1,0:T(1,128)S(1)}, f32[1,384]{1,0:T(1,128)S(1)}) custom-call(bf16[400,1024]{1,0:T(8,128)(2,1)S(1)} %collective-permute-done.8.refs_0_, bf16[400,1024]{1,0:T(8,128)(2,1)S(1)} %collective-permute-done.5.refs_1_, bf16[400,1024]{1,0:T(8,128)(2,1)S(1)} %collective-permute-done.7.refs_2_, ...), custom_call_target="tpu_custom_call" | custom-call | flops 1207959552 | bytes 3145728 | tf_op jit(solution)/shard_map/score_late/pallas_call | solution.py:255
  50.2 4.2 %collective-permute-start.11 = (f32[1,384]{1,0:T(1,128)S(1)}, f32[1,384]{1,0:T(1,128)S(1)}, u32[]{:S(2)}, u32[]{:S(2)}) collective-permute-start(f32[1,384]{1,0:T(1,128)S(1)} %get-tuple-element.39), channel_id=1, source_target_pairs={{0,19},{1,16},{2,17},{3,18},{4,23},{5,20},{6,21},{7,22},{8,27},{9,... | collective-permute-start | bytes 4616 | tf_op jit(solution)/shard_map/ppermute | solution.py:78
  54.4 0.4 collective-permute-start.12
  54.8 1.7 %score_last.1 = f32[1,384]{1,0:T(1,128)S(1)} custom-call(bf16[400,1024]{1,0:T(8,128)(2,1)S(1)} %collective-permute-done.2.refs_0_, bf16[400,1024]{1,0:T(8,128)(2,1)S(1)} %collective-permute-done.5.refs_1_, bf16[400,1024]{1,0:T(8,128)(2,1)S(1)} %collective-permute-done.7.refs_2_, bf16[1920,1024]{1,0:T(8,128)(2,1)S(1)} %get-tuple-element.27.refs_3_.refs_1_, ...), custom_call_target="tpu_custom_call" | custom-call | flops 905969664 | bytes 2359296 | tf_op jit(solution)/shard_map/score_last/pallas_call | solution.py:255
  56.5 0.0 collective-permute-done.10
  56.5 1.4 %collective-permute-done.12 = f32[1,384]{1,0:T(1,128)S(1)} collective-permute-done((f32[1,384]{1,0:T(1,128)S(1)}, f32[1,384]{1,0:T(1,128)S(1)}, u32[]{:S(2)}, u32[]{:S(2)}) %collective-permute-start.12) | collective-permute-done | bytes 1568 | tf_op jit(solution)/shard_map/ppermute | solution.py:78
  57.9 0.6 %maximum_reduce_fusion = f32[384]{0:T(512)} fusion(f32[1,384]{1,0:T(1,128)S(1)} %collective-permute-done.12, f32[1,384]{1,0:T(1,128)S(1)} %collective-permute-done.11, f32[1,384]{1,0:T(1,128)S(1)} %collective-permute-done.10, f32[1,384]{1,0:T(1,128)S(1)} %score_last.1, f32[1,384]{1,0:T(1,128)S(1)} %collective-permute-done.9), kind=kLoop, calls=%fused_computation | loop fusion | flops 1536 | bytes 9216 | tf_op jit(solution)/shard_map/max | solution.py:294
  (4 shorter events, 0.0 us)
Async XLA Ops:
  0.0 20.7 %collective-permute-start = (bf16[384,1024]{1,0:T(8,128)(2,1)}, bf16[384,1024]{1,0:T(8,128)(2,1)S(1)}, u32[]{:S(2)}, u32[]{:S(2)}) collective-permute-start(bf16[384,1024]{1,0:T(8,128)(2,1)} %embeddings.1), channel_id=1, source_target_pairs={{3,0},{0,1},{1,2},{2,3},{7,4},{4,5},{5,6},{6,7},{11,8},{8,9},{9,10... | collective-permute-start | bytes 2359304 | tf_op jit(solution)/shard_map/ppermute | solution.py:78
  3.8 23.2 %collective-permute-start.3 = (bf16[400,1024]{1,0:T(8,128)(2,1)}, bf16[400,1024]{1,0:T(8,128)(2,1)S(1)}, u32[]{:S(2)}, u32[]{:S(2)}) collective-permute-start(bf16[400,1024]{1,0:T(8,128)(2,1)} %get-tuple-element.24.refs_1_), channel_id=1, source_target_pairs={{13,0},{14,1},{15,2},{12,3},{1,4},{2,5},{3,6},{0,7},{5,8},{6,9},{7... | collective-permute-start | bytes 2457608 | tf_op jit(solution)/shard_map/ppermute | solution.py:78
  7.0 21.4 %collective-permute-start.4 = (bf16[400,1024]{1,0:T(8,128)(2,1)}, bf16[400,1024]{1,0:T(8,128)(2,1)S(1)}, u32[]{:S(2)}, u32[]{:S(2)}) collective-permute-start(bf16[400,1024]{1,0:T(8,128)(2,1)} %get-tuple-element.24.refs_1_), channel_id=1, source_target_pairs={{16,0},{17,1},{18,2},{19,3},{20,4},{21,5},{22,6},{23,7},{24,8},{25... | collective-permute-start | bytes 2457608 | tf_op jit(solution)/shard_map/ppermute | solution.py:78
  8.5 22.7 %collective-permute-start.6 = (bf16[400,1024]{1,0:T(8,128)(2,1)}, bf16[400,1024]{1,0:T(8,128)(2,1)S(1)}, u32[]{:S(2)}, u32[]{:S(2)}) collective-permute-start(bf16[400,1024]{1,0:T(8,128)(2,1)} %get-tuple-element.24.refs_1_), channel_id=1, source_target_pairs={{4,0},{5,1},{6,2},{7,3},{8,4},{9,5},{10,6},{11,7},{12,8},{13,9},{1... | collective-permute-start | bytes 2457608 | tf_op jit(solution)/shard_map/ppermute | solution.py:78
  9.9 10.8 %collective-permute-start.1 = (bf16[16,128]{1,0:T(8,128)(2,1)}, bf16[16,128]{1,0:T(8,128)(2,1)S(1)}, u32[]{:S(2)}, u32[]{:S(2)}) collective-permute-start(bf16[16,128]{1,0:T(8,128)(2,1)} %get-tuple-element.23), channel_id=1, source_target_pairs={{3,0},{0,1},{1,2},{2,3},{7,4},{4,5},{5,6},{6,7},{11,8},{8,9},{9,10... | collective-permute-start | bytes 12296 | tf_op jit(solution)/shard_map/ppermute | solution.py:78
  20.9 20.3 %collective-permute-start.2 = (bf16[400,1024]{1,0:T(8,128)(2,1)S(1)}, bf16[400,1024]{1,0:T(8,128)(2,1)S(1)}, u32[]{:S(2)}, u32[]{:S(2)}) collective-permute-start(bf16[400,1024]{1,0:T(8,128)(2,1)S(1)} %join.1.refs_0_), channel_id=1, source_target_pairs={{3,0},{0,1},{1,2},{2,3},{7,4},{4,5},{5,6},{6,7},{11,8},{8,9},{9,10... | collective-permute-start | bytes 2457608 | tf_op jit(solution)/shard_map/ppermute | solution.py:78
  21.5 22.7 %collective-permute-start.8 = (bf16[400,1024]{1,0:T(8,128)(2,1)S(1)}, bf16[400,1024]{1,0:T(8,128)(2,1)S(1)}, u32[]{:S(2)}, u32[]{:S(2)}) collective-permute-start(bf16[400,1024]{1,0:T(8,128)(2,1)S(1)} %join.1.refs_0_), channel_id=1, source_target_pairs={{16,0},{17,1},{18,2},{19,3},{20,4},{21,5},{22,6},{23,7},{24,8},{25... | collective-permute-start | bytes 2457608 | tf_op jit(solution)/shard_map/ppermute | solution.py:78
  28.4 19.9 %collective-permute-start.5 = (bf16[400,1024]{1,0:T(8,128)(2,1)S(1)}, bf16[400,1024]{1,0:T(8,128)(2,1)S(1)}, u32[]{:S(2)}, u32[]{:S(2)}) collective-permute-start(bf16[400,1024]{1,0:T(8,128)(2,1)S(1)} %collective-permute-done.3.refs_3_), channel_id=1, source_target_pairs={{13,0},{14,1},{15,2},{12,3},{1,4},{2,5},{3,6},{0,7},{5,8},{6,9},{7... | collective-permute-start | bytes 2457608 | tf_op jit(solution)/shard_map/ppermute | solution.py:78
  31.3 17.0 %collective-permute-start.7 = (bf16[400,1024]{1,0:T(8,128)(2,1)S(1)}, bf16[400,1024]{1,0:T(8,128)(2,1)S(1)}, u32[]{:S(2)}, u32[]{:S(2)}) collective-permute-start(bf16[400,1024]{1,0:T(8,128)(2,1)S(1)} %collective-permute-done.6.refs_2_), channel_id=1, source_target_pairs={{4,0},{5,1},{6,2},{7,3},{8,4},{9,5},{10,6},{11,7},{12,8},{13,9},{1... | collective-permute-start | bytes 2457608 | tf_op jit(solution)/shard_map/ppermute | solution.py:78
  32.6 1.1 %copy-start = (bf16[400,1024]{1,0:T(8,128)(2,1)S(1)}, bf16[400,1024]{1,0:T(8,128)(2,1)}, u32[]{:S(2)}) copy-start(bf16[400,1024]{1,0:T(8,128)(2,1)} %get-tuple-element.24.refs_1_) | copy-start | bytes 2457604
  45.8 10.7 %collective-permute-start.10 = (f32[1,384]{1,0:T(1,128)S(1)}, f32[1,384]{1,0:T(1,128)S(1)}, u32[]{:S(2)}, u32[]{:S(2)}) collective-permute-start(f32[1,384]{1,0:T(1,128)S(1)} %get-tuple-element.36), channel_id=1, source_target_pairs={{0,13},{1,14},{2,15},{3,12},{4,1},{5,2},{6,3},{7,0},{8,5},{9,6},{1... | collective-permute-start | bytes 4616 | tf_op jit(solution)/shard_map/ppermute | solution.py:78
  48.1 8.4 %collective-permute-start.9 = (f32[1,384]{1,0:T(1,128)S(1)}, f32[1,384]{1,0:T(1,128)S(1)}, u32[]{:S(2)}, u32[]{:S(2)}) collective-permute-start(f32[1,384]{1,0:T(1,128)S(1)} %get-tuple-element.35), channel_id=1, source_target_pairs={{0,4},{1,5},{2,6},{3,7},{4,8},{5,9},{6,10},{7,11},{8,12},{9,13},{1... | collective-permute-start | bytes 4616 | tf_op jit(solution)/shard_map/ppermute | solution.py:78
  50.2 6.4 %collective-permute-start.11 = (f32[1,384]{1,0:T(1,128)S(1)}, f32[1,384]{1,0:T(1,128)S(1)}, u32[]{:S(2)}, u32[]{:S(2)}) collective-permute-start(f32[1,384]{1,0:T(1,128)S(1)} %get-tuple-element.39), channel_id=1, source_target_pairs={{0,19},{1,16},{2,17},{3,18},{4,23},{5,20},{6,21},{7,22},{8,27},{9,... | collective-permute-start | bytes 4616 | tf_op jit(solution)/shard_map/ppermute | solution.py:78
  54.4 3.6 %collective-permute-start.12 = (f32[1,384]{1,0:T(1,128)S(1)}, f32[1,384]{1,0:T(1,128)S(1)}, u32[]{:S(2)}, u32[]{:S(2)}) collective-permute-start(f32[1,384]{1,0:T(1,128)S(1)} %get-tuple-element.40), channel_id=1, source_target_pairs={{0,16},{1,17},{2,18},{3,19},{4,20},{5,21},{6,22},{7,23},{8,24},{9,... | collective-permute-start | bytes 4616 | tf_op jit(solution)/shard_map/ppermute | solution.py:78

commit v5 on v4

--- a/solution.py
+++ b/solution.py
@@ -25,9 +25,10 @@
 TAIL = 16
 BLOCK = ROWS + TAIL
 WIDTH = 1024
-STRIPE = 128
+STRIPE = 192
 STRIPES = ROWS // STRIPE
 PACKED = (1, 0, 2, 3, 4)
+PAIR = (8, 4)
 STEPS = {
     "early": (
         (),
@@ -36,7 +37,7 @@
     ),
     "middle": ((5,), (), ((5, (2, 3, 4), (2, 3, 4)),)),
     "second": ((8,), (), ((8, (0, 2, 3, 4), (2, 3, 8)),)),
-    "late": ((8,), (7, 6), ((8, (7, 6), (8,)), (4, (7, 6), (4,)))),
+    "late": ((6, 7), (), ((7, PAIR, PAIR), (6, PAIR, PAIR))),
     "last": ((), (5, 7, 6), ((0, (5, 7, 6), (0,)),)),
 }
 
@@ -166,6 +167,7 @@
     direct, joined, strips = STEPS[step]
     results = targets(step)
     first = step == "early"
+    laid = PAIR if step == "late" else PACKED
     refs = list(refs)
 
     def take(count):
@@ -189,11 +191,24 @@
         for copy in copies:
             copy.wait()
 
+    moves = []
+    if step == "second":
+        pair, pair_ids = take(2)
+        (sems,) = take(1)
+        for i, b in enumerate(PAIR):
+            at = PACKED.index(b) if b in PACKED else None
+            rows = in_place[b].at[:ROWS] if at is None else packed.at[at * ROWS : (at + 1) * ROWS]
+            tail = in_place[b].at[ROWS:] if at is None else packed_ids.at[at]
+            moves.append(pltpu.make_async_copy(rows, pair.at[i * ROWS : (i + 1) * ROWS], sems.at[0, i]))
+            moves.append(pltpu.make_async_copy(tail, pair_ids.at[i], sems.at[1, i]))
+        for move in moves:
+            move.start()
+
     def rows_of(blocks):
         b, n = blocks[0], len(blocks)
         if b in in_place:
             return in_place[b][:ROWS, :]
-        order, ref = (joined, held) if b in joined else (PACKED, packed)
+        order, ref = (joined, held) if b in joined else (laid, packed)
         at = order.index(b)
         assert order[at : at + n] == tuple(blocks)
         return ref[at * ROWS : (at + n) * ROWS, :]
@@ -204,7 +219,7 @@
         elif b in joined:
             parts = ids[joined.index(b), :, :ROWS]
         else:
-            parts = packed_ids[PACKED.index(b), :, :ROWS]
+            parts = packed_ids[laid.index(b), :, :ROWS]
         parts = parts.astype(jnp.float32)
         return parts[0:1] * 65536.0 + parts[1:2] * 256.0 + parts[2:3]
 
@@ -241,24 +256,26 @@
         if b in earlier:
             value = jnp.maximum(value, earlier[b][...])
         outs[b][...] = value
+    for move in moves:
+        move.wait()
 
 
 def score(step, blocks, earlier, packed=()):
     direct, joined, strips = STEPS[step]
     results = targets(step)
     given = tuple(b for b in results if b in earlier)
-    n = len(joined)
-    first = step == "early"
+    n = len(PAIR) if step == "second" else len(joined)
+    hands_on = step in ("early", "second")
     pairs = sum(len(others) for _, others, _ in strips)
     vmem, free = pl.BlockSpec(memory_space=pltpu.VMEM), pl.BlockSpec(memory_space=pl.ANY)
     shapes = [((n * ROWS, WIDTH), jnp.bfloat16), ((n, TAIL, WIDTH), jnp.bfloat16)] if n else []
     values = pl.pallas_call(
         functools.partial(score_kernel, step, given),
         out_shape=[jax.ShapeDtypeStruct((1, ROWS), jnp.float32)] * len(results)
-        + [jax.ShapeDtypeStruct(*shape) for shape in shapes if first],
-        in_specs=[vmem] * len(direct) + [free] * n + [vmem] * (len(packed) + len(given)),
-        out_specs=[vmem] * (len(results) + (len(shapes) if first else 0)),
-        scratch_shapes=[pltpu.VMEM(*shape) for shape in shapes if not first]
+        + [jax.ShapeDtypeStruct(*shape) for shape in shapes if hands_on],
+        in_specs=[vmem] * len(direct) + [free] * len(joined) + [vmem] * (len(packed) + len(given)),
+        out_specs=[vmem] * (len(results) + (len(shapes) if hands_on else 0)),
+        scratch_shapes=[pltpu.VMEM(*shape) for shape in shapes if not hands_on]
         + ([pltpu.SemaphoreType.DMA((2, n))] if n else []),
         compiler_params=pltpu.CompilerParams(vmem_limit_bytes=28 << 20),
         cost_estimate=pl.CostEstimate(
@@ -279,14 +296,14 @@
             blocks[block] = receive(whole, by)
     for block, parent, by in SECOND:
         whole = blocks[parent]
-        if block == 7:
-            whole, blocks[4] = lax.optimization_barrier((whole, blocks[4]))
+        if block in (6, 7):
+            whole, _ = lax.optimization_barrier((whole, blocks[4]))
         blocks[block] = receive(whole, by)
     best, packed = score("early", blocks, {})
     best, _ = score("middle", blocks, best, packed)
-    best, _ = score("second", blocks, best, packed)
+    best, pair = score("second", blocks, best, packed)
     got = [receive(best[b], OFFSETS[b], back=True) for b in (2, 3)]
-    best, _ = score("late", blocks, best, packed)
+    best, _ = score("late", blocks, best, pair)
     got += [receive(best[b], OFFSETS[b], back=True) for b in (8, 4)]
     best, _ = score("last", blocks, best, packed)
     own = best[0]

time: 58.7 us -> 58.6 us (level)
  waiting for transfers between devices: 20.6 us -> 19.3 us
  starting transfers between devices: 22.1 us -> 23.4 us
    ppermute x13, waiting for transfers between devices: 20.6 us -> 19.3 us  [receive(): return lax.ppermute(array, 'blk', links)]
    ppermute x13, starting transfers between devices: 22.1 us -> 23.4 us  [receive(): return lax.ppermute(array, 'blk', links)]
  transfers between devices with their start and end apart: 13 -> 13, of which waited for: 7 -> 6; matrix products, arithmetic and copies ran while one was open for 0% -> 0% of each run, Pallas kernels for 24% -> 24%
where the time goes in v5:
time: 58.6 us; the launch traced here: 58.4 us
  starting transfers between devices  23.4 us (40%)
  waiting for transfers between devices  19.3 us (33%)
  Pallas kernels  13.9 us (24%)
  local copies, waits for them, and re-layouts  1.14 us (2%)
  other arithmetic  0.6 us (1%)
    ppermute x13, starting transfers between devices, receive(): return lax.ppermute(array, 'blk', links)  23.4 us
    ppermute x13, waiting for transfers between devices, receive(): return lax.ppermute(array, 'blk', links)  19.3 us
    pallas_call x5, Pallas kernels, score(): pl.pallas_call(functools.partial(score_kernel, step, given), out_shape=[j...  11.4 us
    pallas_call x1, Pallas kernels, prepare(): pl.pallas_call(prepare_kernel, out_shape=[jax.ShapeDtypeStruct(shape, jnp...  2.19 us
  transfers between devices with their start and end apart: 13, of which 6 were waited for; matrix products, arithmetic and copies ran while one was open for 0% of the time, Pallas kernels for 24%

profile of v5, /device:TPU:0, one launch (start us, length us, event | category | flops | bytes accessed | tf_op | source)
XLA Modules:
  0.0 58.4 jit_solution(5166343720364093471)
XLA Ops:
  0.0 1.6 %collective-permute-start = (bf16[384,1024]{1,0:T(8,128)(2,1)}, bf16[384,1024]{1,0:T(8,128)(2,1)S(1)}, u32[]{:S(2)}, u32[]{:S(2)}) collective-permute-start(bf16[384,1024]{1,0:T(8,128)(2,1)} %embeddings.1), channel_id=1, source_target_pairs={{3,0},{0,1},{1,2},{2,3},{7,4},{4,5},{5,6},{6,7},{11,8},{8,9},{9,10... | collective-permute-start | bytes 2359304 | tf_op jit(solution)/shard_map/ppermute | solution.py:79
  1.6 2.2 %prepare.1 = (bf16[400,1024]{1,0:T(8,128)(2,1)}, bf16[16,128]{1,0:T(8,128)(2,1)}) custom-call(bf16[384,1024]{1,0:T(8,128)(2,1)} %embeddings.1, s32[384]{0:T(512)} %cluster.1, s32[384]{0:T(512)} %source.1), custom_call_target="tpu_custom_call" | custom-call | tf_op jit(solution)/shard_map/prepare/pallas_call | solution.py:124
  3.8 1.7 %collective-permute-start.4 = (bf16[400,1024]{1,0:T(8,128)(2,1)}, bf16[400,1024]{1,0:T(8,128)(2,1)S(1)}, u32[]{:S(2)}, u32[]{:S(2)}) collective-permute-start(bf16[400,1024]{1,0:T(8,128)(2,1)} %get-tuple-element.26.refs_1_), channel_id=1, source_target_pairs={{16,0},{17,1},{18,2},{19,3},{20,4},{21,5},{22,6},{23,7},{24,8},{25... | collective-permute-start | bytes 2457608 | tf_op jit(solution)/shard_map/ppermute | solution.py:79
  5.4 3.1 %collective-permute-start.3 = (bf16[400,1024]{1,0:T(8,128)(2,1)}, bf16[400,1024]{1,0:T(8,128)(2,1)S(1)}, u32[]{:S(2)}, u32[]{:S(2)}) collective-permute-start(bf16[400,1024]{1,0:T(8,128)(2,1)} %get-tuple-element.26.refs_1_), channel_id=1, source_target_pairs={{13,0},{14,1},{15,2},{12,3},{1,4},{2,5},{3,6},{0,7},{5,8},{6,9},{7... | collective-permute-start | bytes 2457608 | tf_op jit(solution)/shard_map/ppermute | solution.py:79
  8.5 1.3 %collective-permute-start.6 = (bf16[400,1024]{1,0:T(8,128)(2,1)}, bf16[400,1024]{1,0:T(8,128)(2,1)S(1)}, u32[]{:S(2)}, u32[]{:S(2)}) collective-permute-start(bf16[400,1024]{1,0:T(8,128)(2,1)} %get-tuple-element.26.refs_1_), channel_id=1, source_target_pairs={{4,0},{5,1},{6,2},{7,3},{8,4},{9,5},{10,6},{11,7},{12,8},{13,9},{1... | collective-permute-start | bytes 2457608 | tf_op jit(solution)/shard_map/ppermute | solution.py:79
  9.8 1.1 %collective-permute-start.1 = (bf16[16,128]{1,0:T(8,128)(2,1)}, bf16[16,128]{1,0:T(8,128)(2,1)S(1)}, u32[]{:S(2)}, u32[]{:S(2)}) collective-permute-start(bf16[16,128]{1,0:T(8,128)(2,1)} %get-tuple-element.25), channel_id=1, source_target_pairs={{3,0},{0,1},{1,2},{2,3},{7,4},{4,5},{5,6},{6,7},{11,8},{8,9},{9,10... | collective-permute-start | bytes 12296 | tf_op jit(solution)/shard_map/ppermute | solution.py:79
  11.0 9.7 %collective-permute-done.1.tail = bf16[16,128]{1,0:T(8,128)(2,1)S(1)} collective-permute-done((bf16[16,128]{1,0:T(8,128)(2,1)}, bf16[16,128]{1,0:T(8,128)(2,1)S(1)}, u32[]{:S(2)}, u32[]{:S(2)}) %collective-permute-start.1) | collective-permute-done | bytes 4128 | tf_op jit(solution)/shard_map/ppermute | solution.py:79
  20.7 0.0 collective-permute-done.raw
  20.7 0.3 join.1.refs_0_
  20.9 0.5 collective-permute-start.2
  21.5 1.6 %collective-permute-start.8 = (bf16[400,1024]{1,0:T(8,128)(2,1)S(1)}, bf16[400,1024]{1,0:T(8,128)(2,1)S(1)}, u32[]{:S(2)}, u32[]{:S(2)}) collective-permute-start(bf16[400,1024]{1,0:T(8,128)(2,1)S(1)} %join.1.refs_0_), channel_id=1, source_target_pairs={{16,0},{17,1},{18,2},{19,3},{20,4},{21,5},{22,6},{23,7},{24,8},{25... | collective-permute-start | bytes 2457608 | tf_op jit(solution)/shard_map/ppermute | solution.py:79
  23.1 1.6 %collective-permute-done.4.refs_4_ = bf16[400,1024]{1,0:T(8,128)(2,1)S(1)} collective-permute-done((bf16[400,1024]{1,0:T(8,128)(2,1)}, bf16[400,1024]{1,0:T(8,128)(2,1)S(1)}, u32[]{:S(2)}, u32[]{:S(2)}) %collective-permute-start.4) | collective-permute-done | bytes 819232 | tf_op jit(solution)/shard_map/ppermute | solution.py:79
  24.7 3.6 %collective-permute-done.3.refs_3_ = bf16[400,1024]{1,0:T(8,128)(2,1)S(1)} collective-permute-done((bf16[400,1024]{1,0:T(8,128)(2,1)}, bf16[400,1024]{1,0:T(8,128)(2,1)S(1)}, u32[]{:S(2)}, u32[]{:S(2)}) %collective-permute-start.3) | collective-permute-done | bytes 819232 | tf_op jit(solution)/shard_map/ppermute | solution.py:79
  28.3 2.0 %collective-permute-start.5 = (bf16[400,1024]{1,0:T(8,128)(2,1)S(1)}, bf16[400,1024]{1,0:T(8,128)(2,1)S(1)}, u32[]{:S(2)}, u32[]{:S(2)}) collective-permute-start(bf16[400,1024]{1,0:T(8,128)(2,1)S(1)} %collective-permute-done.3.refs_3_), channel_id=1, source_target_pairs={{13,0},{14,1},{15,2},{12,3},{1,4},{2,5},{3,6},{0,7},{5,8},{6,9},{7... | collective-permute-start | bytes 2457608 | tf_op jit(solution)/shard_map/ppermute | solution.py:79
  30.3 0.0 collective-permute-done.6.refs_2_
  30.3 2.5 %collective-permute-start.7 = (bf16[400,1024]{1,0:T(8,128)(2,1)S(1)}, bf16[400,1024]{1,0:T(8,128)(2,1)S(1)}, u32[]{:S(2)}, u32[]{:S(2)}) collective-permute-start(bf16[400,1024]{1,0:T(8,128)(2,1)S(1)} %collective-permute-done.6.refs_2_), channel_id=1, source_target_pairs={{4,0},{5,1},{6,2},{7,3},{8,4},{9,5},{10,6},{11,7},{12,8},{13,9},{1... | collective-permute-start | bytes 2457608 | tf_op jit(solution)/shard_map/ppermute | solution.py:79
  32.8 1.1 %copy-done = bf16[400,1024]{1,0:T(8,128)(2,1)S(1)} copy-done((bf16[400,1024]{1,0:T(8,128)(2,1)S(1)}, bf16[400,1024]{1,0:T(8,128)(2,1)}, u32[]{:S(2)}) %copy-start) | copy-done | bytes 819224
  33.9 4.9 %score_early.1 = (f32[1,384]{1,0:T(1,128)S(1)}, f32[1,384]{1,0:T(1,128)S(1)}, f32[1,384]{1,0:T(1,128)S(1)}, f32[1,384]{1,0:T(1,128)S(1)}, bf16[1920,1024]{1,0:T(...) custom-call(bf16[400,1024]{1,0:T(8,128)(2,1)S(1)} %join.1.refs_0_, bf16[400,1024]{1,0:T(8,128)(2,1)S(1)} %copy-done, ...), custom_call_target="tpu_custom_call" | custom-call | flops 3321888768 | bytes 8650752 | tf_op jit(solution)/shard_map/score_early/pallas_call | solution.py:272
  38.8 2.4 %collective-permute-done.2.refs_0_ = bf16[400,1024]{1,0:T(8,128)(2,1)S(1)} collective-permute-done((bf16[400,1024]{1,0:T(8,128)(2,1)S(1)}, bf16[400,1024]{1,0:T(8,128)(2,1)S(1)}, u32[]{:S(2)}, u32[]{:S(2)}) %collective-permute-start.2) | collective-permute-done | bytes 819232 | tf_op jit(solution)/shard_map/ppermute | solution.py:79
  41.2 1.3 %score_middle.1 = (f32[1,384]{1,0:T(1,128)S(1)}, f32[1,384]{1,0:T(1,128)S(1)}, f32[1,384]{1,0:T(1,128)S(1)}) custom-call(bf16[400,1024]{1,0:T(8,128)(2,1)S(1)} %collective-permute-done.2.refs_0_, bf16[1920,1024]{1,0:T(8,128)(2,1)S(1)} %get-tuple-element.29.refs_3_.refs_1_, bf16[5,16,1024]{2,1,0:T(8,128)(2,1)S(1)} %get-tuple-element.30.refs_4_.refs_2_, ...), custom_call_target="tpu_custom_call" | custom-call | flops 905969664 | bytes 2359296 | tf_op jit(solution)/shard_map/score_middle/pallas_call | solution.py:272
  42.5 0.0 collective-permute-done.8.refs_0_
  42.5 1.9 %score_second.1 = (f32[1,384]{1,0:T(1,128)S(1)}, f32[1,384]{1,0:T(1,128)S(1)}, f32[1,384]{1,0:T(1,128)S(1)}, bf16[768,1024]{1,0:T(8,128)(2,1)S(1)}, bf16[2,16,1024]{2,1,0:T(8,128)(2,1)S(1)}) custom-call(bf16[400,1024]{1,0:T(8,128)(2,1)S(1)} %collective-permute-done.8.refs_0_, bf16[1920,1024]{1,0:T(8,128)(2,1)S(1)} %get-tuple-element.29.refs_3_.refs_1_, ...), custom_call_target="tpu_custom_call" | custom-call | flops 1207959552 | bytes 3145728 | tf_op jit(solution)/shard_map/score_second/pallas_call | solution.py:272
  44.5 3.8 %collective-permute-start.10 = (f32[1,384]{1,0:T(1,128)S(1)}, f32[1,384]{1,0:T(1,128)S(1)}, u32[]{:S(2)}, u32[]{:S(2)}) collective-permute-start(f32[1,384]{1,0:T(1,128)S(1)} %get-tuple-element.38), channel_id=1, source_target_pairs={{0,13},{1,14},{2,15},{3,12},{4,1},{5,2},{6,3},{7,0},{8,5},{9,6},{1... | collective-permute-start | bytes 4616 | tf_op jit(solution)/shard_map/ppermute | solution.py:79
  48.3 0.0 collective-permute-start.9
  48.3 0.9 %collective-permute-done.5.refs_1_ = bf16[400,1024]{1,0:T(8,128)(2,1)S(1)} collective-permute-done((bf16[400,1024]{1,0:T(8,128)(2,1)S(1)}, bf16[400,1024]{1,0:T(8,128)(2,1)S(1)}, u32[]{:S(2)}, u32[]{:S(2)}) %collective-permute-start.5) | collective-permute-done | bytes 819232 | tf_op jit(solution)/shard_map/ppermute | solution.py:79
  49.2 0.0 collective-permute-done.7.refs_2_.refs_0_
  49.2 1.6 %score_late.1 = (f32[1,384]{1,0:T(1,128)S(1)}, f32[1,384]{1,0:T(1,128)S(1)}) custom-call(bf16[400,1024]{1,0:T(8,128)(2,1)S(1)} %collective-permute-done.7.refs_2_.refs_0_, bf16[400,1024]{1,0:T(8,128)(2,1)S(1)} %collective-permute-done.5.refs_1_, bf16[768,1024]{1,0:T(8,128)(2,1)S(1)} %get-tuple-element.39.refs_2_, ...), custom_call_target="tpu_custom_call" | custom-call | flops 1207959552 | bytes 3145728 | tf_op jit(solution)/shard_map/score_late/pallas_call | solution.py:272
  50.8 3.4 %collective-permute-start.11 = (f32[1,384]{1,0:T(1,128)S(1)}, f32[1,384]{1,0:T(1,128)S(1)}, u32[]{:S(2)}, u32[]{:S(2)}) collective-permute-start(f32[1,384]{1,0:T(1,128)S(1)} %get-tuple-element.43), channel_id=1, source_target_pairs={{0,19},{1,16},{2,17},{3,18},{4,23},{5,20},{6,21},{7,22},{8,27},{9,... | collective-permute-start | bytes 4616 | tf_op jit(solution)/shard_map/ppermute | solution.py:79
  54.3 0.8 %collective-permute-start.12 = (f32[1,384]{1,0:T(1,128)S(1)}, f32[1,384]{1,0:T(1,128)S(1)}, u32[]{:S(2)}, u32[]{:S(2)}) collective-permute-start(f32[1,384]{1,0:T(1,128)S(1)} %get-tuple-element.44), channel_id=1, source_target_pairs={{0,16},{1,17},{2,18},{3,19},{4,20},{5,21},{6,22},{7,23},{8,24},{9,... | collective-permute-start | bytes 4616 | tf_op jit(solution)/shard_map/ppermute | solution.py:79
  55.1 1.7 %score_last.1 = f32[1,384]{1,0:T(1,128)S(1)} custom-call(bf16[400,1024]{1,0:T(8,128)(2,1)S(1)} %collective-permute-done.2.refs_0_, bf16[400,1024]{1,0:T(8,128)(2,1)S(1)} %collective-permute-done.5.refs_1_, bf16[400,1024]{1,0:T(8,128)(2,1)S(1)} %collective-permute-done.7.refs_2_.refs_0_, bf16[1920,1024]{1,0:T(8,128)(2,1)S(1)} %get-tuple-element.29.refs_3_.refs_1_, ...), custom_call_target="tpu_custom_call" | custom-call | flops 905969664 | bytes 2359296 | tf_op jit(solution)/shard_map/score_last/pallas_call | solution.py:272
  56.8 1.0 %collective-permute-done.12 = f32[1,384]{1,0:T(1,128)S(1)} collective-permute-done((f32[1,384]{1,0:T(1,128)S(1)}, f32[1,384]{1,0:T(1,128)S(1)}, u32[]{:S(2)}, u32[]{:S(2)}) %collective-permute-start.12) | collective-permute-done | bytes 1568 | tf_op jit(solution)/shard_map/ppermute | solution.py:79
  57.8 0.6 %maximum_reduce_fusion = f32[384]{0:T(512)} fusion(f32[1,384]{1,0:T(1,128)S(1)} %collective-permute-done.12, f32[1,384]{1,0:T(1,128)S(1)} %collective-permute-done.11, f32[1,384]{1,0:T(1,128)S(1)} %collective-permute-done.10, f32[1,384]{1,0:T(1,128)S(1)} %score_last.1, f32[1,384]{1,0:T(1,128)S(1)} %collective-permute-done.9), kind=kLoop, calls=%fused_computation | loop fusion | flops 1536 | bytes 9216 | tf_op jit(solution)/shard_map/max | solution.py:311
  (4 shorter events, 0.0 us)
Async XLA Ops:
  0.0 20.7 %collective-permute-start = (bf16[384,1024]{1,0:T(8,128)(2,1)}, bf16[384,1024]{1,0:T(8,128)(2,1)S(1)}, u32[]{:S(2)}, u32[]{:S(2)}) collective-permute-start(bf16[384,1024]{1,0:T(8,128)(2,1)} %embeddings.1), channel_id=1, source_target_pairs={{3,0},{0,1},{1,2},{2,3},{7,4},{4,5},{5,6},{6,7},{11,8},{8,9},{9,10... | collective-permute-start | bytes 2359304 | tf_op jit(solution)/shard_map/ppermute | solution.py:79
  3.8 20.9 %collective-permute-start.4 = (bf16[400,1024]{1,0:T(8,128)(2,1)}, bf16[400,1024]{1,0:T(8,128)(2,1)S(1)}, u32[]{:S(2)}, u32[]{:S(2)}) collective-permute-start(bf16[400,1024]{1,0:T(8,128)(2,1)} %get-tuple-element.26.refs_1_), channel_id=1, source_target_pairs={{16,0},{17,1},{18,2},{19,3},{20,4},{21,5},{22,6},{23,7},{24,8},{25... | collective-permute-start | bytes 2457608 | tf_op jit(solution)/shard_map/ppermute | solution.py:79
  5.4 22.9 %collective-permute-start.3 = (bf16[400,1024]{1,0:T(8,128)(2,1)}, bf16[400,1024]{1,0:T(8,128)(2,1)S(1)}, u32[]{:S(2)}, u32[]{:S(2)}) collective-permute-start(bf16[400,1024]{1,0:T(8,128)(2,1)} %get-tuple-element.26.refs_1_), channel_id=1, source_target_pairs={{13,0},{14,1},{15,2},{12,3},{1,4},{2,5},{3,6},{0,7},{5,8},{6,9},{7... | collective-permute-start | bytes 2457608 | tf_op jit(solution)/shard_map/ppermute | solution.py:79
  8.5 21.7 %collective-permute-start.6 = (bf16[400,1024]{1,0:T(8,128)(2,1)}, bf16[400,1024]{1,0:T(8,128)(2,1)S(1)}, u32[]{:S(2)}, u32[]{:S(2)}) collective-permute-start(bf16[400,1024]{1,0:T(8,128)(2,1)} %get-tuple-element.26.refs_1_), channel_id=1, source_target_pairs={{4,0},{5,1},{6,2},{7,3},{8,4},{9,5},{10,6},{11,7},{12,8},{13,9},{1... | collective-permute-start | bytes 2457608 | tf_op jit(solution)/shard_map/ppermute | solution.py:79
  9.8 10.8 %collective-permute-start.1 = (bf16[16,128]{1,0:T(8,128)(2,1)}, bf16[16,128]{1,0:T(8,128)(2,1)S(1)}, u32[]{:S(2)}, u32[]{:S(2)}) collective-permute-start(bf16[16,128]{1,0:T(8,128)(2,1)} %get-tuple-element.25), channel_id=1, source_target_pairs={{3,0},{0,1},{1,2},{2,3},{7,4},{4,5},{5,6},{6,7},{11,8},{8,9},{9,10... | collective-permute-start | bytes 12296 | tf_op jit(solution)/shard_map/ppermute | solution.py:79
  20.9 20.3 %collective-permute-start.2 = (bf16[400,1024]{1,0:T(8,128)(2,1)S(1)}, bf16[400,1024]{1,0:T(8,128)(2,1)S(1)}, u32[]{:S(2)}, u32[]{:S(2)}) collective-permute-start(bf16[400,1024]{1,0:T(8,128)(2,1)S(1)} %join.1.refs_0_), channel_id=1, source_target_pairs={{3,0},{0,1},{1,2},{2,3},{7,4},{4,5},{5,6},{6,7},{11,8},{8,9},{9,10... | collective-permute-start | bytes 2457608 | tf_op jit(solution)/shard_map/ppermute | solution.py:79
  21.5 21.0 %collective-permute-start.8 = (bf16[400,1024]{1,0:T(8,128)(2,1)S(1)}, bf16[400,1024]{1,0:T(8,128)(2,1)S(1)}, u32[]{:S(2)}, u32[]{:S(2)}) collective-permute-start(bf16[400,1024]{1,0:T(8,128)(2,1)S(1)} %join.1.refs_0_), channel_id=1, source_target_pairs={{16,0},{17,1},{18,2},{19,3},{20,4},{21,5},{22,6},{23,7},{24,8},{25... | collective-permute-start | bytes 2457608 | tf_op jit(solution)/shard_map/ppermute | solution.py:79
  28.3 20.9 %collective-permute-start.5 = (bf16[400,1024]{1,0:T(8,128)(2,1)S(1)}, bf16[400,1024]{1,0:T(8,128)(2,1)S(1)}, u32[]{:S(2)}, u32[]{:S(2)}) collective-permute-start(bf16[400,1024]{1,0:T(8,128)(2,1)S(1)} %collective-permute-done.3.refs_3_), channel_id=1, source_target_pairs={{13,0},{14,1},{15,2},{12,3},{1,4},{2,5},{3,6},{0,7},{5,8},{6,9},{7... | collective-permute-start | bytes 2457608 | tf_op jit(solution)/shard_map/ppermute | solution.py:79
  30.3 18.9 %collective-permute-start.7 = (bf16[400,1024]{1,0:T(8,128)(2,1)S(1)}, bf16[400,1024]{1,0:T(8,128)(2,1)S(1)}, u32[]{:S(2)}, u32[]{:S(2)}) collective-permute-start(bf16[400,1024]{1,0:T(8,128)(2,1)S(1)} %collective-permute-done.6.refs_2_), channel_id=1, source_target_pairs={{4,0},{5,1},{6,2},{7,3},{8,4},{9,5},{10,6},{11,7},{12,8},{13,9},{1... | collective-permute-start | bytes 2457608 | tf_op jit(solution)/shard_map/ppermute | solution.py:79
  32.8 1.1 %copy-start = (bf16[400,1024]{1,0:T(8,128)(2,1)S(1)}, bf16[400,1024]{1,0:T(8,128)(2,1)}, u32[]{:S(2)}) copy-start(bf16[400,1024]{1,0:T(8,128)(2,1)} %get-tuple-element.26.refs_1_) | copy-start | bytes 2457604
  44.5 12.3 %collective-permute-start.10 = (f32[1,384]{1,0:T(1,128)S(1)}, f32[1,384]{1,0:T(1,128)S(1)}, u32[]{:S(2)}, u32[]{:S(2)}) collective-permute-start(f32[1,384]{1,0:T(1,128)S(1)} %get-tuple-element.38), channel_id=1, source_target_pairs={{0,13},{1,14},{2,15},{3,12},{4,1},{5,2},{6,3},{7,0},{8,5},{9,6},{1... | collective-permute-start | bytes 4616 | tf_op jit(solution)/shard_map/ppermute | solution.py:79
  48.3 8.5 %collective-permute-start.9 = (f32[1,384]{1,0:T(1,128)S(1)}, f32[1,384]{1,0:T(1,128)S(1)}, u32[]{:S(2)}, u32[]{:S(2)}) collective-permute-start(f32[1,384]{1,0:T(1,128)S(1)} %get-tuple-element.37), channel_id=1, source_target_pairs={{0,4},{1,5},{2,6},{3,7},{4,8},{5,9},{6,10},{7,11},{8,12},{9,13},{1... | collective-permute-start | bytes 4616 | tf_op jit(solution)/shard_map/ppermute | solution.py:79
  50.8 6.0 %collective-permute-start.11 = (f32[1,384]{1,0:T(1,128)S(1)}, f32[1,384]{1,0:T(1,128)S(1)}, u32[]{:S(2)}, u32[]{:S(2)}) collective-permute-start(f32[1,384]{1,0:T(1,128)S(1)} %get-tuple-element.43), channel_id=1, source_target_pairs={{0,19},{1,16},{2,17},{3,18},{4,23},{5,20},{6,21},{7,22},{8,27},{9,... | collective-permute-start | bytes 4616 | tf_op jit(solution)/shard_map/ppermute | solution.py:79
  54.3 3.6 %collective-permute-start.12 = (f32[1,384]{1,0:T(1,128)S(1)}, f32[1,384]{1,0:T(1,128)S(1)}, u32[]{:S(2)}, u32[]{:S(2)}) collective-permute-start(f32[1,384]{1,0:T(1,128)S(1)} %get-tuple-element.44), channel_id=1, source_target_pairs={{0,16},{1,17},{2,18},{3,19},{4,20},{5,21},{6,22},{7,23},{8,24},{9,... | collective-permute-start | bytes 4616 | tf_op jit(solution)/shard_map/ppermute | solution.py:79

commit v6 on v5

--- a/solution.py
+++ b/solution.py
@@ -304,7 +304,7 @@
     best, pair = score("second", blocks, best, packed)
     got = [receive(best[b], OFFSETS[b], back=True) for b in (2, 3)]
     best, _ = score("late", blocks, best, pair)
-    got += [receive(best[b], OFFSETS[b], back=True) for b in (8, 4)]
+    got += [receive(best[b], OFFSETS[b], back=True) for b in (4, 8)]
     best, _ = score("last", blocks, best, packed)
     own = best[0]
     for value in got:

time: 58.6 us -> 58.4 us (level); the launches traced: 58.4 us -> 57.4 us
  waiting for transfers between devices: 19.3 us -> 18.3 us
    ppermute x13, waiting for transfers between devices: 19.3 us -> 18.3 us  [receive(): return lax.ppermute(array, 'blk', links)]
  transfers between devices with their start and end apart: 13 -> 13, of which waited for: 6 -> 5; matrix products, arithmetic and copies ran while one was open for 0% -> 0% of each run, Pallas kernels for 24% -> 24%
where the time goes in v6:
time: 58.4 us; the launch traced here: 57.4 us
  starting transfers between devices  23.5 us (40%)
  waiting for transfers between devices  18.3 us (31%)
  Pallas kernels  13.9 us (24%)
  local copies, waits for them, and re-layouts  1.14 us (2%)
  other arithmetic  0.6 us (1%)
    ppermute x13, starting transfers between devices, receive(): return lax.ppermute(array, 'blk', links)  23.5 us
    ppermute x13, waiting for transfers between devices, receive(): return lax.ppermute(array, 'blk', links)  18.3 us
    pallas_call x5, Pallas kernels, score(): pl.pallas_call(functools.partial(score_kernel, step, given), out_shape=[j...  11.4 us
    pallas_call x1, Pallas kernels, prepare(): pl.pallas_call(prepare_kernel, out_shape=[jax.ShapeDtypeStruct(shape, jnp...  2.19 us
  transfers between devices with their start and end apart: 13, of which 5 were waited for; matrix products, arithmetic and copies ran while one was open for 0% of the time, Pallas kernels for 24%

profile of v6, /device:TPU:0, one launch (start us, length us, event | category | flops | bytes accessed | tf_op | source)
XLA Modules:
  0.0 57.4 jit_solution(2123686220710517779)
XLA Ops:
  0.0 1.6 %collective-permute-start = (bf16[384,1024]{1,0:T(8,128)(2,1)}, bf16[384,1024]{1,0:T(8,128)(2,1)S(1)}, u32[]{:S(2)}, u32[]{:S(2)}) collective-permute-start(bf16[384,1024]{1,0:T(8,128)(2,1)} %embeddings.1), channel_id=1, source_target_pairs={{3,0},{0,1},{1,2},{2,3},{7,4},{4,5},{5,6},{6,7},{11,8},{8,9},{9,10... | collective-permute-start | bytes 2359304 | tf_op jit(solution)/shard_map/ppermute | solution.py:79
  1.6 2.2 %prepare.1 = (bf16[400,1024]{1,0:T(8,128)(2,1)}, bf16[16,128]{1,0:T(8,128)(2,1)}) custom-call(bf16[384,1024]{1,0:T(8,128)(2,1)} %embeddings.1, s32[384]{0:T(512)} %cluster.1, s32[384]{0:T(512)} %source.1), custom_call_target="tpu_custom_call" | custom-call | tf_op jit(solution)/shard_map/prepare/pallas_call | solution.py:124
  3.8 1.7 %collective-permute-start.4 = (bf16[400,1024]{1,0:T(8,128)(2,1)}, bf16[400,1024]{1,0:T(8,128)(2,1)S(1)}, u32[]{:S(2)}, u32[]{:S(2)}) collective-permute-start(bf16[400,1024]{1,0:T(8,128)(2,1)} %get-tuple-element.26.refs_1_), channel_id=1, source_target_pairs={{16,0},{17,1},{18,2},{19,3},{20,4},{21,5},{22,6},{23,7},{24,8},{25... | collective-permute-start | bytes 2457608 | tf_op jit(solution)/shard_map/ppermute | solution.py:79
  5.4 3.1 %collective-permute-start.3 = (bf16[400,1024]{1,0:T(8,128)(2,1)}, bf16[400,1024]{1,0:T(8,128)(2,1)S(1)}, u32[]{:S(2)}, u32[]{:S(2)}) collective-permute-start(bf16[400,1024]{1,0:T(8,128)(2,1)} %get-tuple-element.26.refs_1_), channel_id=1, source_target_pairs={{13,0},{14,1},{15,2},{12,3},{1,4},{2,5},{3,6},{0,7},{5,8},{6,9},{7... | collective-permute-start | bytes 2457608 | tf_op jit(solution)/shard_map/ppermute | solution.py:79
  8.5 1.3 %collective-permute-start.6 = (bf16[400,1024]{1,0:T(8,128)(2,1)}, bf16[400,1024]{1,0:T(8,128)(2,1)S(1)}, u32[]{:S(2)}, u32[]{:S(2)}) collective-permute-start(bf16[400,1024]{1,0:T(8,128)(2,1)} %get-tuple-element.26.refs_1_), channel_id=1, source_target_pairs={{4,0},{5,1},{6,2},{7,3},{8,4},{9,5},{10,6},{11,7},{12,8},{13,9},{1... | collective-permute-start | bytes 2457608 | tf_op jit(solution)/shard_map/ppermute | solution.py:79
  9.8 1.1 %collective-permute-start.1 = (bf16[16,128]{1,0:T(8,128)(2,1)}, bf16[16,128]{1,0:T(8,128)(2,1)S(1)}, u32[]{:S(2)}, u32[]{:S(2)}) collective-permute-start(bf16[16,128]{1,0:T(8,128)(2,1)} %get-tuple-element.25), channel_id=1, source_target_pairs={{3,0},{0,1},{1,2},{2,3},{7,4},{4,5},{5,6},{6,7},{11,8},{8,9},{9,10... | collective-permute-start | bytes 12296 | tf_op jit(solution)/shard_map/ppermute | solution.py:79
  11.0 9.7 %collective-permute-done.1.tail = bf16[16,128]{1,0:T(8,128)(2,1)S(1)} collective-permute-done((bf16[16,128]{1,0:T(8,128)(2,1)}, bf16[16,128]{1,0:T(8,128)(2,1)S(1)}, u32[]{:S(2)}, u32[]{:S(2)}) %collective-permute-start.1) | collective-permute-done | bytes 4128 | tf_op jit(solution)/shard_map/ppermute | solution.py:79
  20.7 0.0 collective-permute-done.raw
  20.7 0.3 join.1.refs_0_
  20.9 0.5 collective-permute-start.2
  21.5 1.6 %collective-permute-start.8 = (bf16[400,1024]{1,0:T(8,128)(2,1)S(1)}, bf16[400,1024]{1,0:T(8,128)(2,1)S(1)}, u32[]{:S(2)}, u32[]{:S(2)}) collective-permute-start(bf16[400,1024]{1,0:T(8,128)(2,1)S(1)} %join.1.refs_0_), channel_id=1, source_target_pairs={{16,0},{17,1},{18,2},{19,3},{20,4},{21,5},{22,6},{23,7},{24,8},{25... | collective-permute-start | bytes 2457608 | tf_op jit(solution)/shard_map/ppermute | solution.py:79
  23.1 1.6 %collective-permute-done.4.refs_4_ = bf16[400,1024]{1,0:T(8,128)(2,1)S(1)} collective-permute-done((bf16[400,1024]{1,0:T(8,128)(2,1)}, bf16[400,1024]{1,0:T(8,128)(2,1)S(1)}, u32[]{:S(2)}, u32[]{:S(2)}) %collective-permute-start.4) | collective-permute-done | bytes 819232 | tf_op jit(solution)/shard_map/ppermute | solution.py:79
  24.7 3.6 %collective-permute-done.3.refs_3_ = bf16[400,1024]{1,0:T(8,128)(2,1)S(1)} collective-permute-done((bf16[400,1024]{1,0:T(8,128)(2,1)}, bf16[400,1024]{1,0:T(8,128)(2,1)S(1)}, u32[]{:S(2)}, u32[]{:S(2)}) %collective-permute-start.3) | collective-permute-done | bytes 819232 | tf_op jit(solution)/shard_map/ppermute | solution.py:79
  28.3 2.0 %collective-permute-start.5 = (bf16[400,1024]{1,0:T(8,128)(2,1)S(1)}, bf16[400,1024]{1,0:T(8,128)(2,1)S(1)}, u32[]{:S(2)}, u32[]{:S(2)}) collective-permute-start(bf16[400,1024]{1,0:T(8,128)(2,1)S(1)} %collective-permute-done.3.refs_3_), channel_id=1, source_target_pairs={{13,0},{14,1},{15,2},{12,3},{1,4},{2,5},{3,6},{0,7},{5,8},{6,9},{7... | collective-permute-start | bytes 2457608 | tf_op jit(solution)/shard_map/ppermute | solution.py:79
  30.3 0.0 collective-permute-done.6.refs_2_
  30.3 2.5 %collective-permute-start.7 = (bf16[400,1024]{1,0:T(8,128)(2,1)S(1)}, bf16[400,1024]{1,0:T(8,128)(2,1)S(1)}, u32[]{:S(2)}, u32[]{:S(2)}) collective-permute-start(bf16[400,1024]{1,0:T(8,128)(2,1)S(1)} %collective-permute-done.6.refs_2_), channel_id=1, source_target_pairs={{4,0},{5,1},{6,2},{7,3},{8,4},{9,5},{10,6},{11,7},{12,8},{13,9},{1... | collective-permute-start | bytes 2457608 | tf_op jit(solution)/shard_map/ppermute | solution.py:79
  32.8 1.1 %copy-done = bf16[400,1024]{1,0:T(8,128)(2,1)S(1)} copy-done((bf16[400,1024]{1,0:T(8,128)(2,1)S(1)}, bf16[400,1024]{1,0:T(8,128)(2,1)}, u32[]{:S(2)}) %copy-start) | copy-done | bytes 819224
  33.9 4.9 %score_early.1 = (f32[1,384]{1,0:T(1,128)S(1)}, f32[1,384]{1,0:T(1,128)S(1)}, f32[1,384]{1,0:T(1,128)S(1)}, f32[1,384]{1,0:T(1,128)S(1)}, bf16[1920,1024]{1,0:T(...) custom-call(bf16[400,1024]{1,0:T(8,128)(2,1)S(1)} %join.1.refs_0_, bf16[400,1024]{1,0:T(8,128)(2,1)S(1)} %copy-done, ...), custom_call_target="tpu_custom_call" | custom-call | flops 3321888768 | bytes 8650752 | tf_op jit(solution)/shard_map/score_early/pallas_call | solution.py:272
  38.8 2.4 %collective-permute-done.2.refs_0_ = bf16[400,1024]{1,0:T(8,128)(2,1)S(1)} collective-permute-done((bf16[400,1024]{1,0:T(8,128)(2,1)S(1)}, bf16[400,1024]{1,0:T(8,128)(2,1)S(1)}, u32[]{:S(2)}, u32[]{:S(2)}) %collective-permute-start.2) | collective-permute-done | bytes 819232 | tf_op jit(solution)/shard_map/ppermute | solution.py:79
  41.2 1.3 %score_middle.1 = (f32[1,384]{1,0:T(1,128)S(1)}, f32[1,384]{1,0:T(1,128)S(1)}, f32[1,384]{1,0:T(1,128)S(1)}) custom-call(bf16[400,1024]{1,0:T(8,128)(2,1)S(1)} %collective-permute-done.2.refs_0_, bf16[1920,1024]{1,0:T(8,128)(2,1)S(1)} %get-tuple-element.29.refs_3_.refs_1_, bf16[5,16,1024]{2,1,0:T(8,128)(2,1)S(1)} %get-tuple-element.30.refs_4_.refs_2_, ...), custom_call_target="tpu_custom_call" | custom-call | flops 905969664 | bytes 2359296 | tf_op jit(solution)/shard_map/score_middle/pallas_call | solution.py:272
  42.5 1.9 %score_second.1 = (f32[1,384]{1,0:T(1,128)S(1)}, f32[1,384]{1,0:T(1,128)S(1)}, f32[1,384]{1,0:T(1,128)S(1)}, bf16[768,1024]{1,0:T(8,128)(2,1)S(1)}, bf16[2,16,1024]{2,1,0:T(8,128)(2,1)S(1)}) custom-call(bf16[400,1024]{1,0:T(8,128)(2,1)S(1)} %collective-permute-done.8.refs_0_, bf16[1920,1024]{1,0:T(8,128)(2,1)S(1)} %get-tuple-element.29.refs_3_.refs_1_, ...), custom_call_target="tpu_custom_call" | custom-call | flops 1207959552 | bytes 3145728 | tf_op jit(solution)/shard_map/score_second/pallas_call | solution.py:272
  44.5 3.8 %collective-permute-start.10 = (f32[1,384]{1,0:T(1,128)S(1)}, f32[1,384]{1,0:T(1,128)S(1)}, u32[]{:S(2)}, u32[]{:S(2)}) collective-permute-start(f32[1,384]{1,0:T(1,128)S(1)} %get-tuple-element.38), channel_id=1, source_target_pairs={{0,13},{1,14},{2,15},{3,12},{4,1},{5,2},{6,3},{7,0},{8,5},{9,6},{1... | collective-permute-start | bytes 4616 | tf_op jit(solution)/shard_map/ppermute | solution.py:79
  48.3 0.0 collective-permute-start.9
  48.3 0.9 %collective-permute-done.5.refs_1_ = bf16[400,1024]{1,0:T(8,128)(2,1)S(1)} collective-permute-done((bf16[400,1024]{1,0:T(8,128)(2,1)S(1)}, bf16[400,1024]{1,0:T(8,128)(2,1)S(1)}, u32[]{:S(2)}, u32[]{:S(2)}) %collective-permute-start.5) | collective-permute-done | bytes 819232 | tf_op jit(solution)/shard_map/ppermute | solution.py:79
  49.2 0.0 collective-permute-done.7.refs_2_.refs_0_
  49.2 1.6 %score_late.1 = (f32[1,384]{1,0:T(1,128)S(1)}, f32[1,384]{1,0:T(1,128)S(1)}) custom-call(bf16[400,1024]{1,0:T(8,128)(2,1)S(1)} %collective-permute-done.7.refs_2_.refs_0_, bf16[400,1024]{1,0:T(8,128)(2,1)S(1)} %collective-permute-done.5.refs_1_, bf16[768,1024]{1,0:T(8,128)(2,1)S(1)} %get-tuple-element.39.refs_2_, ...), custom_call_target="tpu_custom_call" | custom-call | flops 1207959552 | bytes 3145728 | tf_op jit(solution)/shard_map/score_late/pallas_call | solution.py:272
  50.8 0.7 %collective-permute-start.11 = (f32[1,384]{1,0:T(1,128)S(1)}, f32[1,384]{1,0:T(1,128)S(1)}, u32[]{:S(2)}, u32[]{:S(2)}) collective-permute-start(f32[1,384]{1,0:T(1,128)S(1)} %get-tuple-element.43), channel_id=1, source_target_pairs={{0,16},{1,17},{2,18},{3,19},{4,20},{5,21},{6,22},{7,23},{8,24},{9,... | collective-permute-start | bytes 4616 | tf_op jit(solution)/shard_map/ppermute | solution.py:79
  51.6 3.5 %collective-permute-start.12 = (f32[1,384]{1,0:T(1,128)S(1)}, f32[1,384]{1,0:T(1,128)S(1)}, u32[]{:S(2)}, u32[]{:S(2)}) collective-permute-start(f32[1,384]{1,0:T(1,128)S(1)} %get-tuple-element.44), channel_id=1, source_target_pairs={{0,19},{1,16},{2,17},{3,18},{4,23},{5,20},{6,21},{7,22},{8,27},{9,... | collective-permute-start | bytes 4616 | tf_op jit(solution)/shard_map/ppermute | solution.py:79
  55.1 1.7 %score_last.1 = f32[1,384]{1,0:T(1,128)S(1)} custom-call(bf16[400,1024]{1,0:T(8,128)(2,1)S(1)} %collective-permute-done.2.refs_0_, bf16[400,1024]{1,0:T(8,128)(2,1)S(1)} %collective-permute-done.5.refs_1_, bf16[400,1024]{1,0:T(8,128)(2,1)S(1)} %collective-permute-done.7.refs_2_.refs_0_, bf16[1920,1024]{1,0:T(8,128)(2,1)S(1)} %get-tuple-element.29.refs_3_.refs_1_, ...), custom_call_target="tpu_custom_call" | custom-call | flops 905969664 | bytes 2359296 | tf_op jit(solution)/shard_map/score_last/pallas_call | solution.py:272
  56.8 0.0 collective-permute-done.11
  56.8 0.0 collective-permute-done.12
  56.8 0.6 %maximum_reduce_fusion = f32[384]{0:T(512)} fusion(f32[1,384]{1,0:T(1,128)S(1)} %collective-permute-done.12, f32[1,384]{1,0:T(1,128)S(1)} %collective-permute-done.11, f32[1,384]{1,0:T(1,128)S(1)} %collective-permute-done.10, f32[1,384]{1,0:T(1,128)S(1)} %score_last.1, f32[1,384]{1,0:T(1,128)S(1)} %collective-permute-done.9), kind=kLoop, calls=%fused_computation | loop fusion | flops 1536 | bytes 9216 | tf_op jit(solution)/shard_map/max | solution.py:311
  (4 shorter events, 0.0 us)
Async XLA Ops:
  0.0 20.7 %collective-permute-start = (bf16[384,1024]{1,0:T(8,128)(2,1)}, bf16[384,1024]{1,0:T(8,128)(2,1)S(1)}, u32[]{:S(2)}, u32[]{:S(2)}) collective-permute-start(bf16[384,1024]{1,0:T(8,128)(2,1)} %embeddings.1), channel_id=1, source_target_pairs={{3,0},{0,1},{1,2},{2,3},{7,4},{4,5},{5,6},{6,7},{11,8},{8,9},{9,10... | collective-permute-start | bytes 2359304 | tf_op jit(solution)/shard_map/ppermute | solution.py:79
  3.8 20.9 %collective-permute-start.4 = (bf16[400,1024]{1,0:T(8,128)(2,1)}, bf16[400,1024]{1,0:T(8,128)(2,1)S(1)}, u32[]{:S(2)}, u32[]{:S(2)}) collective-permute-start(bf16[400,1024]{1,0:T(8,128)(2,1)} %get-tuple-element.26.refs_1_), channel_id=1, source_target_pairs={{16,0},{17,1},{18,2},{19,3},{20,4},{21,5},{22,6},{23,7},{24,8},{25... | collective-permute-start | bytes 2457608 | tf_op jit(solution)/shard_map/ppermute | solution.py:79
  5.4 22.9 %collective-permute-start.3 = (bf16[400,1024]{1,0:T(8,128)(2,1)}, bf16[400,1024]{1,0:T(8,128)(2,1)S(1)}, u32[]{:S(2)}, u32[]{:S(2)}) collective-permute-start(bf16[400,1024]{1,0:T(8,128)(2,1)} %get-tuple-element.26.refs_1_), channel_id=1, source_target_pairs={{13,0},{14,1},{15,2},{12,3},{1,4},{2,5},{3,6},{0,7},{5,8},{6,9},{7... | collective-permute-start | bytes 2457608 | tf_op jit(solution)/shard_map/ppermute | solution.py:79
  8.5 21.7 %collective-permute-start.6 = (bf16[400,1024]{1,0:T(8,128)(2,1)}, bf16[400,1024]{1,0:T(8,128)(2,1)S(1)}, u32[]{:S(2)}, u32[]{:S(2)}) collective-permute-start(bf16[400,1024]{1,0:T(8,128)(2,1)} %get-tuple-element.26.refs_1_), channel_id=1, source_target_pairs={{4,0},{5,1},{6,2},{7,3},{8,4},{9,5},{10,6},{11,7},{12,8},{13,9},{1... | collective-permute-start | bytes 2457608 | tf_op jit(solution)/shard_map/ppermute | solution.py:79
  9.8 10.8 %collective-permute-start.1 = (bf16[16,128]{1,0:T(8,128)(2,1)}, bf16[16,128]{1,0:T(8,128)(2,1)S(1)}, u32[]{:S(2)}, u32[]{:S(2)}) collective-permute-start(bf16[16,128]{1,0:T(8,128)(2,1)} %get-tuple-element.25), channel_id=1, source_target_pairs={{3,0},{0,1},{1,2},{2,3},{7,4},{4,5},{5,6},{6,7},{11,8},{8,9},{9,10... | collective-permute-start | bytes 12296 | tf_op jit(solution)/shard_map/ppermute | solution.py:79
  20.9 20.3 %collective-permute-start.2 = (bf16[400,1024]{1,0:T(8,128)(2,1)S(1)}, bf16[400,1024]{1,0:T(8,128)(2,1)S(1)}, u32[]{:S(2)}, u32[]{:S(2)}) collective-permute-start(bf16[400,1024]{1,0:T(8,128)(2,1)S(1)} %join.1.refs_0_), channel_id=1, source_target_pairs={{3,0},{0,1},{1,2},{2,3},{7,4},{4,5},{5,6},{6,7},{11,8},{8,9},{9,10... | collective-permute-start | bytes 2457608 | tf_op jit(solution)/shard_map/ppermute | solution.py:79
  21.5 21.0 %collective-permute-start.8 = (bf16[400,1024]{1,0:T(8,128)(2,1)S(1)}, bf16[400,1024]{1,0:T(8,128)(2,1)S(1)}, u32[]{:S(2)}, u32[]{:S(2)}) collective-permute-start(bf16[400,1024]{1,0:T(8,128)(2,1)S(1)} %join.1.refs_0_), channel_id=1, source_target_pairs={{16,0},{17,1},{18,2},{19,3},{20,4},{21,5},{22,6},{23,7},{24,8},{25... | collective-permute-start | bytes 2457608 | tf_op jit(solution)/shard_map/ppermute | solution.py:79
  28.3 20.9 %collective-permute-start.5 = (bf16[400,1024]{1,0:T(8,128)(2,1)S(1)}, bf16[400,1024]{1,0:T(8,128)(2,1)S(1)}, u32[]{:S(2)}, u32[]{:S(2)}) collective-permute-start(bf16[400,1024]{1,0:T(8,128)(2,1)S(1)} %collective-permute-done.3.refs_3_), channel_id=1, source_target_pairs={{13,0},{14,1},{15,2},{12,3},{1,4},{2,5},{3,6},{0,7},{5,8},{6,9},{7... | collective-permute-start | bytes 2457608 | tf_op jit(solution)/shard_map/ppermute | solution.py:79
  30.3 18.9 %collective-permute-start.7 = (bf16[400,1024]{1,0:T(8,128)(2,1)S(1)}, bf16[400,1024]{1,0:T(8,128)(2,1)S(1)}, u32[]{:S(2)}, u32[]{:S(2)}) collective-permute-start(bf16[400,1024]{1,0:T(8,128)(2,1)S(1)} %collective-permute-done.6.refs_2_), channel_id=1, source_target_pairs={{4,0},{5,1},{6,2},{7,3},{8,4},{9,5},{10,6},{11,7},{12,8},{13,9},{1... | collective-permute-start | bytes 2457608 | tf_op jit(solution)/shard_map/ppermute | solution.py:79
  32.8 1.1 %copy-start = (bf16[400,1024]{1,0:T(8,128)(2,1)S(1)}, bf16[400,1024]{1,0:T(8,128)(2,1)}, u32[]{:S(2)}) copy-start(bf16[400,1024]{1,0:T(8,128)(2,1)} %get-tuple-element.26.refs_1_) | copy-start | bytes 2457604
  44.5 12.3 %collective-permute-start.10 = (f32[1,384]{1,0:T(1,128)S(1)}, f32[1,384]{1,0:T(1,128)S(1)}, u32[]{:S(2)}, u32[]{:S(2)}) collective-permute-start(f32[1,384]{1,0:T(1,128)S(1)} %get-tuple-element.38), channel_id=1, source_target_pairs={{0,13},{1,14},{2,15},{3,12},{4,1},{5,2},{6,3},{7,0},{8,5},{9,6},{1... | collective-permute-start | bytes 4616 | tf_op jit(solution)/shard_map/ppermute | solution.py:79
  48.3 8.5 %collective-permute-start.9 = (f32[1,384]{1,0:T(1,128)S(1)}, f32[1,384]{1,0:T(1,128)S(1)}, u32[]{:S(2)}, u32[]{:S(2)}) collective-permute-start(f32[1,384]{1,0:T(1,128)S(1)} %get-tuple-element.37), channel_id=1, source_target_pairs={{0,4},{1,5},{2,6},{3,7},{4,8},{5,9},{6,10},{7,11},{8,12},{9,13},{1... | collective-permute-start | bytes 4616 | tf_op jit(solution)/shard_map/ppermute | solution.py:79
  50.8 6.0 %collective-permute-start.11 = (f32[1,384]{1,0:T(1,128)S(1)}, f32[1,384]{1,0:T(1,128)S(1)}, u32[]{:S(2)}, u32[]{:S(2)}) collective-permute-start(f32[1,384]{1,0:T(1,128)S(1)} %get-tuple-element.43), channel_id=1, source_target_pairs={{0,16},{1,17},{2,18},{3,19},{4,20},{5,21},{6,22},{7,23},{8,24},{9,... | collective-permute-start | bytes 4616 | tf_op jit(solution)/shard_map/ppermute | solution.py:79
  51.6 5.3 %collective-permute-start.12 = (f32[1,384]{1,0:T(1,128)S(1)}, f32[1,384]{1,0:T(1,128)S(1)}, u32[]{:S(2)}, u32[]{:S(2)}) collective-permute-start(f32[1,384]{1,0:T(1,128)S(1)} %get-tuple-element.44), channel_id=1, source_target_pairs={{0,19},{1,16},{2,17},{3,18},{4,23},{5,20},{6,21},{7,22},{8,27},{9,... | collective-permute-start | bytes 4616 | tf_op jit(solution)/shard_map/ppermute | solution.py:79
